TPU v7x, 32 devices: a whole 2x2x4 slice. The times are simulated.
32 devices in a mesh: segment: 4 (over x, core), tx: 2 (over y), ty: 4 (over z).
Axes of the slice: x: 2, y: 2, z: 4, core: 2. Of those that a mesh axis runs over, the one named last changes fastest.
Arguments:
- act_in: bfloat16 [4, 32, 256, 128], P('segment', 'tx', 'ty'), may hold values from -6 to 6
- partner_in: bfloat16 [4, 32, 256, 128], P('segment', 'tx', 'ty'), may hold values from -6 to 6
- stashed: bfloat16 [4, 32, 256, 128], P('segment', 'tx', 'ty'), may hold values from -6 to 6
- grad_in: bfloat16 [4, 32, 256, 128], P('segment', 'tx', 'ty'), may hold values from -6 to 6
- down_weights: bfloat16 [4, 3, 3, 128, 192], P('segment'), may hold values from -0.1875 to 0.1875
- up_weights: bfloat16 [4, 3, 3, 192, 128], P('segment'), may hold values from -0.15625 to 0.15625
- coarse: bfloat16 [512, 128], P(('tx', 'ty')), may hold values from -6 to 6
- nest_owner: int32 [512, 1], P(('tx', 'ty')), may hold values from 0 to 3; in each aligned block of 64 rows (0 to 63, 64 to 127, ...) at most 32 rows name the same one
- nest_cell: int32 [512], P(('tx', 'ty')), may hold values from 0 to 63
- land_weight: int32 [8, 64], P('tx', 'ty'), may hold values from 1 to 4
Outputs:
- act_out: bfloat16 [4, 32, 256, 128], P('segment', 'tx', 'ty')
- grad_out: bfloat16 [4, 32, 256, 128], P('segment', 'tx', 'ty')
- partner_out: bfloat16 [4, 32, 256, 128], P('segment', 'tx', 'ty')
- down_grads: float32 [4, 221184], P('segment', ('tx', 'ty'))
- up_grads: float32 [4, 221184], P('segment', ('tx', 'ty'))
Inputs may be any that keep to these rules, and one draw needn't show every extreme that they name: `nest_owner`: within the rows of one device (aligned blocks of 64 rows) no owner is named more than 32 times, a bound that some block reaches; every owner is named by some row.
All inputs are finite; a program needn't handle non-finite values.
Results may differ from a plain program's by a relative error of at most 0.0085.
Values may be sent and summed in bfloat16 or wider, within the bound.
No kernel may reach another device: no remote copies, remote signals or barrier semaphores. Data moves between devices by JAX's collectives and lax.ppermute only.
A program may use at most 64 MiB of HBM per device.

v0:
```python
import math

import jax
import jax.numpy as jnp
from jax import lax
from jax.sharding import PartitionSpec as P


def padded_2(shard, sides, width):
    for axis, dim in sides:
        peers, length = (lax.axis_size(axis), shard.shape[dim])
        up = [(i, (i + 1) % peers) for i in range(peers - 1)]
        down = [(j, i) for i, j in up]
        last = lax.slice_in_dim(shard, length - width, length, axis=dim)
        leading = lax.slice_in_dim(shard, 0, width, axis=dim)
        before = lax.ppermute(last, axis, up)
        after = lax.ppermute(leading, axis, down)
        shard = jnp.concatenate([before, shard, after], axis=dim)
    return shard


def from_behind(block, axis, distance):
    devices = range(lax.axis_size(axis))
    route = [(i - distance, i) for i in devices if i - distance in devices]
    return lax.ppermute(block, axis, route)


def convolve(inputs, kernel, stride, padding, dilation):
    result = lax.conv_general_dilated(
        inputs[None],
        kernel,
        (stride, stride),
        padding,
        lhs_dilation=(dilation, dilation),
        dimension_numbers=("NHWC", "HWIO", "NHWC"),
        preferred_element_type=jnp.float32,
    )
    return result[0]


def flipped(kernel):
    return jnp.transpose(kernel[::-1, ::-1], (0, 1, 3, 2))


def enlarge(values, factor):
    return jnp.repeat(jnp.repeat(values, factor, axis=0), factor, axis=1)


def pooled(values):
    height, breadth, channels = values.shape
    return values.reshape(height // 2, 2, breadth // 2, 2, channels).sum(axis=(1, 3))


def silu_slope(preact):
    logistic = jax.nn.sigmoid(preact)
    return logistic * (1.0 + preact * (1.0 - logistic))


def kernel_grad(padded, cotangent, stride):
    height, breadth, channels = cotangent.shape
    flat_grad = cotangent.reshape(height * breadth, channels)
    pieces = []
    for row_tap in range(3):
        for col_tap in range(3):
            window = padded[
                row_tap : row_tap + stride * (height - 1) + 1 : stride,
                col_tap : col_tap + stride * (breadth - 1) + 1 : stride,
            ]
            window = window.reshape(height * breadth, window.shape[-1])
            pieces.append(
                lax.dot_general(
                    window, flat_grad, (((0,), (0,)), ((), ())), preferred_element_type=jnp.float32
                )
            )
    return jnp.stack(pieces).reshape(-1)


def with_rims(block_cells):
    return padded_2(block_cells, (("tx", 0), ("ty", 1)), 1)


def lower_parts(block_cells, down_kernel):
    input_rim = with_rims(block_cells)
    pre_down = convolve(input_rim, down_kernel, 2, "VALID", 1)
    reduced = jax.nn.silu(pre_down).astype(jnp.bfloat16)
    raised_rim = enlarge(with_rims(reduced), 2)[1:-1, 1:-1]
    return (input_rim, pre_down, raised_rim)


def fetch_condition(coarse, nest_owner, nest_cell):
    owners = lax.axis_size("ty")
    needed = nest_cell.shape[0]
    capacity = max(2, 2 * needed // owners)
    owner_ids = nest_owner[:, 0]
    one_hot = (owner_ids[:, None] == jnp.arange(owners, dtype=jnp.int32)[None, :]).astype(jnp.int32)
    earlier = jnp.cumsum(one_hot, axis=0) - one_hot
    slot_ids = jnp.sum(earlier * one_hot, axis=1)
    request = jnp.zeros((owners, capacity), jnp.int32).at[owner_ids, slot_ids].set(nest_cell)
    answered = coarse[lax.all_to_all(request, "ty", split_axis=0, concat_axis=0, tiled=True)]
    replies = lax.all_to_all(answered, "ty", split_axis=0, concat_axis=0, tiled=True)
    return replies[owner_ids, slot_ids]


def local(
    act_in,
    partner_in,
    stashed,
    grad_in,
    down_weights,
    up_weights,
    coarse,
    nest_owner,
    nest_cell,
    land_weight,
):
    segments = lax.axis_size("segment")
    position = lax.axis_index("segment")
    decoder = (position >= segments // 2).astype(jnp.float32)
    encoder = 1.0 - decoder
    last_segment = position == segments - 1
    height, breadth, channels = (act_in.shape[1], act_in.shape[2], act_in.shape[3])
    fetched = fetch_condition(coarse, nest_owner, nest_cell)
    condition = enlarge(fetched.reshape(height // 4, breadth // 4, channels), 4).astype(jnp.float32)
    down_kernel = down_weights[0]
    up_kernel = up_weights[0]
    scaling = 1.0 / math.sqrt(height * breadth * lax.axis_size("tx") * lax.axis_size("ty"))
    block_in = (
        act_in[0].astype(jnp.float32) + decoder * partner_in[0].astype(jnp.float32) + condition
    ).astype(jnp.bfloat16)
    input_rim, pre_down, raised_rim = lower_parts(block_in, down_kernel)
    output = (block_in.astype(jnp.float32) + convolve(raised_rim, up_kernel, 1, "VALID", 1)).astype(
        jnp.bfloat16
    )
    weighting = jnp.where(last_segment, enlarge(land_weight.astype(jnp.float32), 4), 1.0)
    out_grad = (
        (grad_in[0].astype(jnp.float32) + encoder * partner_in[0].astype(jnp.float32))
        * weighting[:, :, None]
    ).astype(jnp.bfloat16)
    back_rim, pre_back, raised_back = lower_parts(stashed[0], down_kernel)
    up_term = kernel_grad(raised_back, out_grad, 1) * scaling
    raised_grad = convolve(with_rims(out_grad), flipped(up_kernel), 1, "VALID", 1)
    pre_grad = (pooled(raised_grad) * silu_slope(pre_back)).astype(jnp.bfloat16)
    grad_rim = with_rims(pre_grad)[1:, 1:]
    in_grad = (
        out_grad.astype(jnp.float32)
        + convolve(grad_rim, flipped(down_kernel), 1, ((1, 0), (1, 0)), 2)
    ).astype(jnp.bfloat16)
    down_term = kernel_grad(back_rim, pre_grad, 2) * scaling
    up_sum, down_sum = (
        lax.psum_scatter(up_term, ("tx", "ty"), scatter_dimension=0, tiled=True),
        lax.psum_scatter(down_term, ("tx", "ty"), scatter_dimension=0, tiled=True),
    )
    from_before = from_behind(output, "segment", 1)
    from_after = from_behind(in_grad, "segment", -1)
    far_act = from_behind(output, "segment", segments - 1)
    far_grad = from_behind(in_grad, "segment", 1 - segments)
    from_partner = jnp.select(
        [position == 0, position == 1, position == 2], [far_grad, from_after, from_before], far_act
    )
    return (from_before[None], from_after[None], from_partner[None], down_sum[None], up_sum[None])


def solution(mesh):
    placed = (
        P("segment", "tx", "ty", None),
        P("segment", "tx", "ty", None),
        P("segment", "tx", "ty", None),
        P("segment", "tx", "ty", None),
        P("segment", None, None, None, None),
        P("segment", None, None, None, None),
        P(("tx", "ty"), None),
        P(("tx", "ty"), None),
        P(("tx", "ty")),
        P("tx", "ty"),
    )
    return jax.shard_map(
        local,
        mesh=mesh,
        in_specs=placed,
        out_specs=(
            P("segment", "tx", "ty", None),
            P("segment", "tx", "ty", None),
            P("segment", "tx", "ty", None),
            P("segment", ("tx", "ty")),
            P("segment", ("tx", "ty")),
        ),
        check_vma=False,
    )
```

profile of v0, /device:TPU:0, one launch (start us, length us, event | category | flops | bytes accessed | tf_op | source)
XLA Modules:
  0.0 240.5 jit_solution(6688288033901331387)
XLA Ops:
  8.1 0.8 select_reduce_fusion
  10.2 10.1 %scatter_fusion = s32[4,32]{1,0:T(4,128)} fusion(s32[4,32]{1,0:T(4,128)} %broadcast.96, s32[64]{0:T(128)S(1)} %get-tuple-element.24, s32[64]{0:T(128)} %param.18), kind=kCustom, calls=%fused_computation.2 | custom fusion | bytes 1280 | tf_op jit(solution)/shard_map/scatter | solution.py:98
  20.3 6.3 %all-to-all-start = ((s32[4,1,32]{2,1,0:T(1,128)}), s32[4,1,32]{2,1,0:T(1,128)S(1)}, u32[]{:S(2)}, u32[]{:S(2)}) async-start(s32[4,1,32]{2,1,0:T(1,128)} %bitcast.5), calls=%async_computation | async-start | bytes 4096 | tf_op jit(solution)/shard_map/all_to_all | solution.py:99
  26.6 3.4 %collective-permute-start.13 = (bf16[1,64,128]{2,1,0:T(8,128)(2,1)S(1)}, bf16[1,64,128]{2,1,0:T(8,128)(2,1)S(1)}, u32[]{:S(2)}, u32[]{:S(2)}) collective-permute-start(bf16[1,64,128]{2,1,0:T(8,128)(2,1)S(1)} %get-tuple-element.34), channel_id=1, source_target_pairs={{0,4},{1,5},{2,6},{3,7},{8,12},{9,13},{10,14},{11,15},{16,20},{17,... | collective-permute-start | bytes 49160 | tf_op jit(solution)/shard_map/ppermute | solution.py:16
  30.1 1.3 collective-permute-start.14
  31.4 2.5 %slice.173 = bf16[8,32,128]{2,1,0:T(8,128)(2,1)} slice(bf16[16,64,128]{2,1,0:T(8,128)(2,1)S(1)} %bitcast.241), slice={[0:15:2], [0:63:2], [0:128:1]} | slice | bytes 131072 | tf_op jit(solution)/shard_map/slice | solution.py:65
  33.9 2.5 %slice.174 = bf16[8,32,128]{2,1,0:T(8,128)(2,1)} slice(bf16[16,64,128]{2,1,0:T(8,128)(2,1)S(1)} %bitcast.242), slice={[0:15:2], [1:64:2], [0:128:1]} | slice | bytes 131072 | tf_op jit(solution)/shard_map/slice | solution.py:65
  36.3 2.5 %slice.176 = bf16[8,32,128]{2,1,0:T(8,128)(2,1)} slice(bf16[16,64,128]{2,1,0:T(8,128)(2,1)S(1)} %bitcast.243), slice={[1:16:2], [0:63:2], [0:128:1]} | slice | bytes 131072 | tf_op jit(solution)/shard_map/slice | solution.py:65
  38.9 2.5 %slice.177 = bf16[8,32,128]{2,1,0:T(8,128)(2,1)} slice(bf16[16,64,128]{2,1,0:T(8,128)(2,1)S(1)} %bitcast.244), slice={[1:16:2], [1:64:2], [0:128:1]} | slice | bytes 131072 | tf_op jit(solution)/shard_map/slice | solution.py:65
  41.7 3.9 %collective-permute-start.15 = (bf16[18,1,128]{2,1,0:T(2,128)(2,1)S(1)}, bf16[18,1,128]{2,1,0:T(2,128)(2,1)S(1)}, u32[]{:S(2)}, u32[]{:S(2)}) collective-permute-start(bf16[18,1,128]{2,1,0:T(2,128)(2,1)S(1)} %get-tuple-element.32), channel_id=1, source_target_pairs={{0,1},{1,2},{2,3},{4,5},{5,6},{6,7},{8,9},{9,10},{10,11},{12,13},{... | collective-permute-start | bytes 13832 | tf_op jit(solution)/shard_map/ppermute | solution.py:16
  45.6 1.3 collective-permute-start.16
  46.9 1.3 gather_fusion
  48.2 5.7 %all-to-all-start.1 = ((bf16[4,32,128]{2,1,0:T(8,128)(2,1)}), bf16[4,32,128]{2,1,0:T(8,128)(2,1)S(1)}, u32[]{:S(2)}, u32[]{:S(2)}) async-start(bf16[4,32,128]{2,1,0:T(8,128)(2,1)} %bitcast.7), calls=%async_computation.1 | async-start | bytes 65536 | tf_op jit(solution)/shard_map/all_to_all | solution.py:100
  56.1 2.5 %slice.169 = bf16[8,32,128]{2,1,0:T(8,128)(2,1)} slice(bf16[18,66,128]{2,1,0:T(8,128)(2,1)S(1)} %pad_maximum_fusion), slice={[0:15:2], [0:63:2], [0:128:1]} | slice | bytes 131072 | tf_op jit(solution)/shard_map/slice | solution.py:65
  61.4 1.3 collective-permute-start.10
  62.7 4.5 %collective-permute-start.9 = (bf16[1,64,128]{2,0,1:T(2,128)(2,1)S(1)}, bf16[1,64,128]{2,0,1:T(2,128)(2,1)S(1)}, u32[]{:S(2)}, u32[]{:S(2)}) collective-permute-start(bf16[1,64,128]{2,0,1:T(2,128)(2,1)S(1)} %get-tuple-element.36), channel_id=1, source_target_pairs={{0,4},{1,5},{2,6},{3,7},{8,12},{9,13},{10,14},{11,15},{16,20},{17,... | collective-permute-start | bytes 49160 | tf_op jit(solution)/shard_map/ppermute | solution.py:16
  67.3 1.3 collective-permute-start
  68.6 1.3 collective-permute-start.1
  70.0 3.9 %collective-permute-start.11 = (bf16[18,1,128]{2,0,1:T(8,128)(2,1)S(1)}, bf16[18,1,128]{2,0,1:T(8,128)(2,1)S(1)}, u32[]{:S(2)}, u32[]{:S(2)}) collective-permute-start(bf16[18,1,128]{2,0,1:T(8,128)(2,1)S(1)} %get-tuple-element.28), channel_id=1, source_target_pairs={{0,1},{1,2},{2,3},{4,5},{5,6},{6,7},{8,9},{9,10},{10,11},{12,13},{... | collective-permute-start | bytes 13832 | tf_op jit(solution)/shard_map/ppermute | solution.py:16
  73.9 1.3 collective-permute-start.12
  75.8 5.1 %collective-permute-start.2 = (bf16[18,1,128]{2,0,1:T(8,128)(2,1)}, bf16[18,1,128]{2,0,1:T(8,128)(2,1)}, u32[]{:S(2)}, u32[]{:S(2)}) collective-permute-start(bf16[18,1,128]{2,0,1:T(8,128)(2,1)} %get-tuple-element.30), channel_id=1, source_target_pairs={{0,1},{1,2},{2,3},{4,5},{5,6},{6,7},{8,9},{9,10},{10,11},{12,13},{... | collective-permute-start | bytes 13832 | tf_op jit(solution)/shard_map/ppermute | solution.py:16
  81.0 1.4 collective-permute-start.3
  82.8 0.9 convolution_select_fusion
  84.9 0.8 reduce_sum.22
  86.6 5.3 %collective-permute-start.23 = (bf16[1,32,192]{2,0,1:T(2,128)(2,1)}, bf16[1,32,192]{2,0,1:T(2,128)(2,1)}, u32[]{:S(2)}, u32[]{:S(2)}) collective-permute-start(bf16[1,32,192]{2,0,1:T(2,128)(2,1)} %get-tuple-element.46), channel_id=1, source_target_pairs={{0,4},{1,5},{2,6},{3,7},{8,12},{9,13},{10,14},{11,15},{16,20},{17,... | collective-permute-start | bytes 36872 | tf_op jit(solution)/shard_map/ppermute | solution.py:16
  91.9 1.3 collective-permute-start.24
  96.5 1.5 mul.65
  98.0 5.1 %collective-permute-start.17 = (bf16[1,32,192]{2,0,1:T(2,128)(2,1)S(1)}, bf16[1,32,192]{2,0,1:T(2,128)(2,1)S(1)}, u32[]{:S(2)}, u32[]{:S(2)}) collective-permute-start(bf16[1,32,192]{2,0,1:T(2,128)(2,1)S(1)} %copy-done.17), channel_id=1, source_target_pairs={{0,4},{1,5},{2,6},{3,7},{8,12},{9,13},{10,14},{11,15},{16,20},{17,... | collective-permute-start | bytes 36872 | tf_op jit(solution)/shard_map/ppermute | solution.py:16
  103.2 1.4 collective-permute-start.18
  104.7 0.9 maximum_bitcast_fusion
  106.5 4.5 %collective-permute-start.4 = (bf16[1,32,192]{2,0,1:T(2,128)(2,1)S(1)}, bf16[1,32,192]{2,0,1:T(2,128)(2,1)S(1)}, u32[]{:S(2)}, u32[]{:S(2)}) collective-permute-start(bf16[1,32,192]{2,0,1:T(2,128)(2,1)S(1)} %get-tuple-element.50), channel_id=1, source_target_pairs={{0,4},{1,5},{2,6},{3,7},{8,12},{9,13},{10,14},{11,15},{16,20},{17,... | collective-permute-start | bytes 36872 | tf_op jit(solution)/shard_map/ppermute | solution.py:16
  111.0 1.3 collective-permute-start.5
  113.0 4.5 %collective-permute-start.25 = (bf16[10,1,192]{2,0,1:T(8,128)(2,1)S(1)}, bf16[10,1,192]{2,0,1:T(8,128)(2,1)S(1)}, u32[]{:S(2)}, u32[]{:S(2)}) collective-permute-start(bf16[10,1,192]{2,0,1:T(8,128)(2,1)S(1)} %get-tuple-element.42), channel_id=1, source_target_pairs={{0,1},{1,2},{2,3},{4,5},{5,6},{6,7},{8,9},{9,10},{10,11},{12,13},{... | collective-permute-start | bytes 11528 | tf_op jit(solution)/shard_map/ppermute | solution.py:16
  117.6 1.3 collective-permute-start.26
  118.9 1.3 collective-permute-start.19
  120.3 5.2 %collective-permute-start.6 = (bf16[10,1,192]{2,0,1:T(8,128)(2,1)S(1)}, bf16[10,1,192]{2,0,1:T(8,128)(2,1)S(1)}, u32[]{:S(2)}, u32[]{:S(2)}) collective-permute-start(bf16[10,1,192]{2,0,1:T(8,128)(2,1)S(1)} %get-tuple-element.44), channel_id=1, source_target_pairs={{0,1},{1,2},{2,3},{4,5},{5,6},{6,7},{8,9},{9,10},{10,11},{12,13},{... | collective-permute-start | bytes 11528 | tf_op jit(solution)/shard_map/ppermute | solution.py:16
  125.5 1.3 collective-permute-start.7
  126.8 0.9 pad_maximum_fusion.3
  132.1 1.0 broadcast_multiply_fusion
  133.4 0.9 copy-done.21
  135.1 1.3 collective-permute-start.20
  136.4 1.3 collective-permute-start.22
  139.8 1.3 convolution_select_fusion.2
  141.2 4.3 %collective-permute-start.21 = (bf16[16,64,128]{2,0,1:T(8,128)(2,1)S(1)}, bf16[16,64,128]{2,0,1:T(8,128)(2,1)S(1)}, u32[]{:S(2)}, u32[]{:S(2)}) collective-permute-start(bf16[16,64,128]{2,0,1:T(8,128)(2,1)S(1)} %fusion.48), channel_id=1, source_target_pairs={{0,24},{1,25},{2,26},{3,27},{4,28},{5,29},{6,30},{7,31}} | collective-permute-start | bytes 786440 | tf_op jit(solution)/shard_map/ppermute | solution.py:25
  145.6 1.3 collective-permute-start.8
  153.8 76.7 %all-reduce.5.cloned.1.call-done = (f32[221184]{0:T(1024)}, f32[221184]{0:T(1024)}) async-done(((f32[221184]{0:T(1024)}, f32[221184]{0:T(1024)}), (f32[221184]{0:T(1024)}, f32[221184]{0:T(1024)})) %all-reduce.5.cloned.1.call-update) | async-done | bytes 1769488
  230.6 1.5 dynamic-slice.1
  232.1 1.5 dynamic-slice.3
  (187 shorter events, 26.8 us)
Async XLA Ops:
  7.2 75.6 %copy-start = (bf16[1,3,3,192,128]{4,3,2,1,0:T(8,128)(2,1)S(1)}, bf16[1,3,3,192,128]{4,3,2,1,0:T(8,128)(2,1)}, u32[]{:S(2)}) copy-start(bf16[1,3,3,192,128]{4,3,2,1,0:T(8,128)(2,1)} %param.15) | copy-start | bytes 1327108
  7.2 19.4 %copy-start.1 = (bf16[1,16,64,128]{3,2,1,0:T(8,128)(2,1)S(1)}, bf16[1,16,64,128]{3,2,1,0:T(8,128)(2,1)}, u32[]{:S(2)}) copy-start(bf16[1,16,64,128]{3,2,1,0:T(8,128)(2,1)} %param.12) | copy-start | bytes 786436
  7.2 24.2 %copy-start.18 = (s32[4,16]{1,0:T(4,128)S(1)}, s32[4,16]{1,0:T(4,128)}, u32[]{:S(2)}) copy-start(s32[4,16]{1,0:T(4,128)} %param.19) | copy-start | bytes 772
  10.2 36.7 %copy-start.2 = (bf16[64,128]{1,0:T(8,128)(2,1)S(1)}, bf16[64,128]{1,0:T(8,128)(2,1)}, u32[]{:S(2)}) copy-start(bf16[64,128]{1,0:T(8,128)(2,1)} %param.16) | copy-start | bytes 49156
  20.3 21.2 %all-to-all-start = ((s32[4,1,32]{2,1,0:T(1,128)}), s32[4,1,32]{2,1,0:T(1,128)S(1)}, u32[]{:S(2)}, u32[]{:S(2)}) async-start(s32[4,1,32]{2,1,0:T(1,128)} %bitcast.5), calls=%async_computation | async-start | bytes 4096 | tf_op jit(solution)/shard_map/all_to_all | solution.py:99
  26.6 14.9 %collective-permute-start.13 = (bf16[1,64,128]{2,1,0:T(8,128)(2,1)S(1)}, bf16[1,64,128]{2,1,0:T(8,128)(2,1)S(1)}, u32[]{:S(2)}, u32[]{:S(2)}) collective-permute-start(bf16[1,64,128]{2,1,0:T(8,128)(2,1)S(1)} %get-tuple-element.34), channel_id=1, source_target_pairs={{0,4},{1,5},{2,6},{3,7},{8,12},{9,13},{10,14},{11,15},{16,20},{17,... | collective-permute-start | bytes 49160 | tf_op jit(solution)/shard_map/ppermute | solution.py:16
  30.1 11.5 %collective-permute-start.14 = (bf16[1,64,128]{2,1,0:T(8,128)(2,1)S(1)}, bf16[1,64,128]{2,1,0:T(8,128)(2,1)S(1)}, u32[]{:S(2)}, u32[]{:S(2)}) collective-permute-start(bf16[1,64,128]{2,1,0:T(8,128)(2,1)S(1)} %get-tuple-element.35), channel_id=1, source_target_pairs={{4,0},{5,1},{6,2},{7,3},{12,8},{13,9},{14,10},{15,11},{20,16},{21,... | collective-permute-start | bytes 49160 | tf_op jit(solution)/shard_map/ppermute | solution.py:17
  41.7 12.7 %collective-permute-start.15 = (bf16[18,1,128]{2,1,0:T(2,128)(2,1)S(1)}, bf16[18,1,128]{2,1,0:T(2,128)(2,1)S(1)}, u32[]{:S(2)}, u32[]{:S(2)}) collective-permute-start(bf16[18,1,128]{2,1,0:T(2,128)(2,1)S(1)} %get-tuple-element.32), channel_id=1, source_target_pairs={{0,1},{1,2},{2,3},{4,5},{5,6},{6,7},{8,9},{9,10},{10,11},{12,13},{... | collective-permute-start | bytes 13832 | tf_op jit(solution)/shard_map/ppermute | solution.py:16
  45.6 8.8 %collective-permute-start.16 = (bf16[18,1,128]{2,1,0:T(2,128)(2,1)S(1)}, bf16[18,1,128]{2,1,0:T(2,128)(2,1)S(1)}, u32[]{:S(2)}, u32[]{:S(2)}) collective-permute-start(bf16[18,1,128]{2,1,0:T(2,128)(2,1)S(1)} %get-tuple-element.33), channel_id=1, source_target_pairs={{1,0},{2,1},{3,2},{5,4},{6,5},{7,6},{9,8},{10,9},{11,10},{13,12},{... | collective-permute-start | bytes 13832 | tf_op jit(solution)/shard_map/ppermute | solution.py:17
  48.2 11.7 %all-to-all-start.1 = ((bf16[4,32,128]{2,1,0:T(8,128)(2,1)}), bf16[4,32,128]{2,1,0:T(8,128)(2,1)S(1)}, u32[]{:S(2)}, u32[]{:S(2)}) async-start(bf16[4,32,128]{2,1,0:T(8,128)(2,1)} %bitcast.7), calls=%async_computation.1 | async-start | bytes 65536 | tf_op jit(solution)/shard_map/all_to_all | solution.py:100
  53.9 176.7 %all-reduce.5.cloned.1.call-start = ((), (), s32[]{:S(2)}) async-start(), calls=%async_computation.2 | async-start | bytes 3538944
  56.0 4.8 %copy-start.4 = (bf16[1,16,64,128]{3,2,1,0:T(8,128)(2,1)S(1)}, bf16[1,16,64,128]{3,2,1,0:T(8,128)(2,1)}, u32[]{:S(2)}) copy-start(bf16[1,16,64,128]{3,2,1,0:T(8,128)(2,1)} %param.13) | copy-start | bytes 786436
  56.0 4.8 %copy-start.5 = (bf16[1,16,64,128]{3,2,1,0:T(8,128)(2,1)S(1)}, bf16[1,16,64,128]{3,2,1,0:T(8,128)(2,1)}, u32[]{:S(2)}) copy-start(bf16[1,16,64,128]{3,2,1,0:T(8,128)(2,1)} %param.11) | copy-start | bytes 786436
  56.0 4.8 %copy-start.6 = (bf16[1,16,64,128]{3,2,1,0:T(8,128)(2,1)S(1)}, bf16[1,16,64,128]{3,2,1,0:T(8,128)(2,1)}, u32[]{:S(2)}) copy-start(bf16[1,16,64,128]{3,2,1,0:T(8,128)(2,1)} %param.10) | copy-start | bytes 786436
  61.4 8.5 %collective-permute-start.10 = (bf16[1,64,128]{2,0,1:T(2,128)(2,1)S(1)}, bf16[1,64,128]{2,0,1:T(2,128)(2,1)S(1)}, u32[]{:S(2)}, u32[]{:S(2)}) collective-permute-start(bf16[1,64,128]{2,0,1:T(2,128)(2,1)S(1)} %get-tuple-element.37), channel_id=1, source_target_pairs={{4,0},{5,1},{6,2},{7,3},{12,8},{13,9},{14,10},{15,11},{20,16},{21,... | collective-permute-start | bytes 49160 | tf_op jit(solution)/shard_map/ppermute | solution.py:17
  62.7 7.2 %collective-permute-start.9 = (bf16[1,64,128]{2,0,1:T(2,128)(2,1)S(1)}, bf16[1,64,128]{2,0,1:T(2,128)(2,1)S(1)}, u32[]{:S(2)}, u32[]{:S(2)}) collective-permute-start(bf16[1,64,128]{2,0,1:T(2,128)(2,1)S(1)} %get-tuple-element.36), channel_id=1, source_target_pairs={{0,4},{1,5},{2,6},{3,7},{8,12},{9,13},{10,14},{11,15},{16,20},{17,... | collective-permute-start | bytes 49160 | tf_op jit(solution)/shard_map/ppermute | solution.py:16
  67.3 7.9 %collective-permute-start = (bf16[1,64,128]{2,0,1:T(2,128)(2,1)S(1)}, bf16[1,64,128]{2,0,1:T(2,128)(2,1)S(1)}, u32[]{:S(2)}, u32[]{:S(2)}) collective-permute-start(bf16[1,64,128]{2,0,1:T(2,128)(2,1)S(1)} %get-tuple-element.40), channel_id=1, source_target_pairs={{0,4},{1,5},{2,6},{3,7},{8,12},{9,13},{10,14},{11,15},{16,20},{17,... | collective-permute-start | bytes 49160 | tf_op jit(solution)/shard_map/ppermute | solution.py:16
  68.6 6.6 %collective-permute-start.1 = (bf16[1,64,128]{2,0,1:T(2,128)(2,1)S(1)}, bf16[1,64,128]{2,0,1:T(2,128)(2,1)S(1)}, u32[]{:S(2)}, u32[]{:S(2)}) collective-permute-start(bf16[1,64,128]{2,0,1:T(2,128)(2,1)S(1)} %get-tuple-element.41), channel_id=1, source_target_pairs={{4,0},{5,1},{6,2},{7,3},{12,8},{13,9},{14,10},{15,11},{20,16},{21,... | collective-permute-start | bytes 49160 | tf_op jit(solution)/shard_map/ppermute | solution.py:17
  70.0 12.4 %collective-permute-start.11 = (bf16[18,1,128]{2,0,1:T(8,128)(2,1)S(1)}, bf16[18,1,128]{2,0,1:T(8,128)(2,1)S(1)}, u32[]{:S(2)}, u32[]{:S(2)}) collective-permute-start(bf16[18,1,128]{2,0,1:T(8,128)(2,1)S(1)} %get-tuple-element.28), channel_id=1, source_target_pairs={{0,1},{1,2},{2,3},{4,5},{5,6},{6,7},{8,9},{9,10},{10,11},{12,13},{... | collective-permute-start | bytes 13832 | tf_op jit(solution)/shard_map/ppermute | solution.py:16
  73.9 8.5 %collective-permute-start.12 = (bf16[18,1,128]{2,0,1:T(8,128)(2,1)S(1)}, bf16[18,1,128]{2,0,1:T(8,128)(2,1)S(1)}, u32[]{:S(2)}, u32[]{:S(2)}) collective-permute-start(bf16[18,1,128]{2,0,1:T(8,128)(2,1)S(1)} %get-tuple-element.29), channel_id=1, source_target_pairs={{1,0},{2,1},{3,2},{5,4},{6,5},{7,6},{9,8},{10,9},{11,10},{13,12},{... | collective-permute-start | bytes 13832 | tf_op jit(solution)/shard_map/ppermute | solution.py:17
  75.2 7.6 %copy-start.8 = (bf16[1,64,128]{2,0,1:T(2,128)(2,1)}, bf16[1,64,128]{2,0,1:T(2,128)(2,1)S(1)}, u32[]{:S(2)}) copy-start(bf16[1,64,128]{2,0,1:T(2,128)(2,1)S(1)} %collective-permute-done) | copy-start | bytes 49156
  75.2 7.5 %copy-start.10 = (bf16[1,64,128]{2,0,1:T(2,128)(2,1)}, bf16[1,64,128]{2,0,1:T(2,128)(2,1)S(1)}, u32[]{:S(2)}) copy-start(bf16[1,64,128]{2,0,1:T(2,128)(2,1)S(1)} %collective-permute-done.1) | copy-start | bytes 49156
  75.8 27.3 %collective-permute-start.2 = (bf16[18,1,128]{2,0,1:T(8,128)(2,1)}, bf16[18,1,128]{2,0,1:T(8,128)(2,1)}, u32[]{:S(2)}, u32[]{:S(2)}) collective-permute-start(bf16[18,1,128]{2,0,1:T(8,128)(2,1)} %get-tuple-element.30), channel_id=1, source_target_pairs={{0,1},{1,2},{2,3},{4,5},{5,6},{6,7},{8,9},{9,10},{10,11},{12,13},{... | collective-permute-start | bytes 13832 | tf_op jit(solution)/shard_map/ppermute | solution.py:16
  81.0 23.7 %collective-permute-start.3 = (bf16[18,1,128]{2,0,1:T(8,128)(2,1)}, bf16[18,1,128]{2,0,1:T(8,128)(2,1)}, u32[]{:S(2)}, u32[]{:S(2)}) collective-permute-start(bf16[18,1,128]{2,0,1:T(8,128)(2,1)} %get-tuple-element.31), channel_id=1, source_target_pairs={{1,0},{2,1},{3,2},{5,4},{6,5},{7,6},{9,8},{10,9},{11,10},{13,12},{... | collective-permute-start | bytes 13832 | tf_op jit(solution)/shard_map/ppermute | solution.py:17
  84.9 9.0 %copy-start.7 = (bf16[8,32,128]{2,1,0:T(8,128)(2,1)S(1)}, bf16[8,32,128]{2,1,0:T(8,128)(2,1)}, u32[]{:S(2)}) copy-start(bf16[8,32,128]{2,1,0:T(8,128)(2,1)} %slice.169) | copy-start | bytes 196612
  85.7 9.1 %copy-start.15 = (bf16[8,32,128]{2,1,0:T(8,128)(2,1)S(1)}, bf16[8,32,128]{2,1,0:T(8,128)(2,1)}, u32[]{:S(2)}) copy-start(bf16[8,32,128]{2,1,0:T(8,128)(2,1)} %slice.173) | copy-start | bytes 196612
  85.8 9.2 %copy-start.14 = (bf16[8,32,128]{2,1,0:T(8,128)(2,1)S(1)}, bf16[8,32,128]{2,1,0:T(8,128)(2,1)}, u32[]{:S(2)}) copy-start(bf16[8,32,128]{2,1,0:T(8,128)(2,1)} %slice.174) | copy-start | bytes 196612
  86.6 8.9 %copy-start.13 = (bf16[8,32,128]{2,1,0:T(8,128)(2,1)S(1)}, bf16[8,32,128]{2,1,0:T(8,128)(2,1)}, u32[]{:S(2)}) copy-start(bf16[8,32,128]{2,1,0:T(8,128)(2,1)} %slice.176) | copy-start | bytes 196612
  86.6 24.4 %collective-permute-start.23 = (bf16[1,32,192]{2,0,1:T(2,128)(2,1)}, bf16[1,32,192]{2,0,1:T(2,128)(2,1)}, u32[]{:S(2)}, u32[]{:S(2)}) collective-permute-start(bf16[1,32,192]{2,0,1:T(2,128)(2,1)} %get-tuple-element.46), channel_id=1, source_target_pairs={{0,4},{1,5},{2,6},{3,7},{8,12},{9,13},{10,14},{11,15},{16,20},{17,... | collective-permute-start | bytes 36872 | tf_op jit(solution)/shard_map/ppermute | solution.py:16
  91.9 20.4 %collective-permute-start.24 = (bf16[1,32,192]{2,0,1:T(2,128)(2,1)}, bf16[1,32,192]{2,0,1:T(2,128)(2,1)}, u32[]{:S(2)}, u32[]{:S(2)}) collective-permute-start(bf16[1,32,192]{2,0,1:T(2,128)(2,1)} %get-tuple-element.47), channel_id=1, source_target_pairs={{4,0},{5,1},{6,2},{7,3},{12,8},{13,9},{14,10},{15,11},{20,16},{21,... | collective-permute-start | bytes 36872 | tf_op jit(solution)/shard_map/ppermute | solution.py:17
  96.4 6.7 %copy-start.16 = (bf16[1,32,192]{2,0,1:T(2,128)(2,1)S(1)}, bf16[1,32,192]{2,0,1:T(2,128)(2,1)}, u32[]{:S(2)}) copy-start(bf16[1,32,192]{2,0,1:T(2,128)(2,1)} %get-tuple-element.49) | copy-start | bytes 36868
  96.5 8.2 %copy-start.9 = (bf16[1,64,128]{2,0,1:T(2,128)(2,1)S(1)}, bf16[1,64,128]{2,0,1:T(2,128)(2,1)}, u32[]{:S(2)}) copy-start(bf16[1,64,128]{2,0,1:T(2,128)(2,1)} %copy-done.8) | copy-start | bytes 49156
  96.5 8.2 %copy-start.11 = (bf16[1,64,128]{2,0,1:T(2,128)(2,1)S(1)}, bf16[1,64,128]{2,0,1:T(2,128)(2,1)}, u32[]{:S(2)}) copy-start(bf16[1,64,128]{2,0,1:T(2,128)(2,1)} %copy-done.10) | copy-start | bytes 49156
  98.0 19.6 %collective-permute-start.17 = (bf16[1,32,192]{2,0,1:T(2,128)(2,1)S(1)}, bf16[1,32,192]{2,0,1:T(2,128)(2,1)S(1)}, u32[]{:S(2)}, u32[]{:S(2)}) collective-permute-start(bf16[1,32,192]{2,0,1:T(2,128)(2,1)S(1)} %copy-done.17), channel_id=1, source_target_pairs={{0,4},{1,5},{2,6},{3,7},{8,12},{9,13},{10,14},{11,15},{16,20},{17,... | collective-permute-start | bytes 36872 | tf_op jit(solution)/shard_map/ppermute | solution.py:16
  103.2 2.6 %copy-start.20 = (bf16[1,3,3,128,192]{3,4,2,1,0:T(8,128)(2,1)S(1)}, bf16[1,3,3,128,192]{3,4,2,1,0:T(8,128)(2,1)}, u32[]{:S(2)}) copy-start(bf16[1,3,3,128,192]{3,4,2,1,0:T(8,128)(2,1)} %param.14) | copy-start | bytes 1327108
  103.2 15.7 %collective-permute-start.18 = (bf16[1,32,192]{2,0,1:T(2,128)(2,1)S(1)}, bf16[1,32,192]{2,0,1:T(2,128)(2,1)S(1)}, u32[]{:S(2)}, u32[]{:S(2)}) collective-permute-start(bf16[1,32,192]{2,0,1:T(2,128)(2,1)S(1)} %copy-done.16), channel_id=1, source_target_pairs={{4,0},{5,1},{6,2},{7,3},{12,8},{13,9},{14,10},{15,11},{20,16},{21,... | collective-permute-start | bytes 36872 | tf_op jit(solution)/shard_map/ppermute | solution.py:17
  106.5 13.8 %collective-permute-start.4 = (bf16[1,32,192]{2,0,1:T(2,128)(2,1)S(1)}, bf16[1,32,192]{2,0,1:T(2,128)(2,1)S(1)}, u32[]{:S(2)}, u32[]{:S(2)}) collective-permute-start(bf16[1,32,192]{2,0,1:T(2,128)(2,1)S(1)} %get-tuple-element.50), channel_id=1, source_target_pairs={{0,4},{1,5},{2,6},{3,7},{8,12},{9,13},{10,14},{11,15},{16,20},{17,... | collective-permute-start | bytes 36872 | tf_op jit(solution)/shard_map/ppermute | solution.py:16
  111.0 9.2 %collective-permute-start.5 = (bf16[1,32,192]{2,0,1:T(2,128)(2,1)S(1)}, bf16[1,32,192]{2,0,1:T(2,128)(2,1)S(1)}, u32[]{:S(2)}, u32[]{:S(2)}) collective-permute-start(bf16[1,32,192]{2,0,1:T(2,128)(2,1)S(1)} %get-tuple-element.51), channel_id=1, source_target_pairs={{4,0},{5,1},{6,2},{7,3},{12,8},{13,9},{14,10},{15,11},{20,16},{21,... | collective-permute-start | bytes 36872 | tf_op jit(solution)/shard_map/ppermute | solution.py:17
  113.0 13.7 %collective-permute-start.25 = (bf16[10,1,192]{2,0,1:T(8,128)(2,1)S(1)}, bf16[10,1,192]{2,0,1:T(8,128)(2,1)S(1)}, u32[]{:S(2)}, u32[]{:S(2)}) collective-permute-start(bf16[10,1,192]{2,0,1:T(8,128)(2,1)S(1)} %get-tuple-element.42), channel_id=1, source_target_pairs={{0,1},{1,2},{2,3},{4,5},{5,6},{6,7},{8,9},{9,10},{10,11},{12,13},{... | collective-permute-start | bytes 11528 | tf_op jit(solution)/shard_map/ppermute | solution.py:16
  117.6 9.2 %collective-permute-start.26 = (bf16[10,1,192]{2,0,1:T(8,128)(2,1)S(1)}, bf16[10,1,192]{2,0,1:T(8,128)(2,1)S(1)}, u32[]{:S(2)}, u32[]{:S(2)}) collective-permute-start(bf16[10,1,192]{2,0,1:T(8,128)(2,1)S(1)} %get-tuple-element.43), channel_id=1, source_target_pairs={{1,0},{2,1},{3,2},{5,4},{6,5},{7,6},{9,8},{10,9},{11,10},{13,12},{... | collective-permute-start | bytes 11528 | tf_op jit(solution)/shard_map/ppermute | solution.py:17
  118.9 14.1 %collective-permute-start.19 = (bf16[10,1,192]{2,0,1:T(8,128)(2,1)S(1)}, bf16[10,1,192]{2,0,1:T(8,128)(2,1)S(1)}, u32[]{:S(2)}, u32[]{:S(2)}) collective-permute-start(bf16[10,1,192]{2,0,1:T(8,128)(2,1)S(1)} %pad_maximum_fusion.10), channel_id=1, source_target_pairs={{1,0},{2,1},{3,2},{5,4},{6,5},{7,6},{9,8},{10,9},{11,10},{13,12},{... | collective-permute-start | bytes 11528 | tf_op jit(solution)/shard_map/ppermute | solution.py:17
  120.3 17.4 %collective-permute-start.6 = (bf16[10,1,192]{2,0,1:T(8,128)(2,1)S(1)}, bf16[10,1,192]{2,0,1:T(8,128)(2,1)S(1)}, u32[]{:S(2)}, u32[]{:S(2)}) collective-permute-start(bf16[10,1,192]{2,0,1:T(8,128)(2,1)S(1)} %get-tuple-element.44), channel_id=1, source_target_pairs={{0,1},{1,2},{2,3},{4,5},{5,6},{6,7},{8,9},{9,10},{10,11},{12,13},{... | collective-permute-start | bytes 11528 | tf_op jit(solution)/shard_map/ppermute | solution.py:16
  125.5 12.3 %collective-permute-start.7 = (bf16[10,1,192]{2,0,1:T(8,128)(2,1)S(1)}, bf16[10,1,192]{2,0,1:T(8,128)(2,1)S(1)}, u32[]{:S(2)}, u32[]{:S(2)}) collective-permute-start(bf16[10,1,192]{2,0,1:T(8,128)(2,1)S(1)} %get-tuple-element.45), channel_id=1, source_target_pairs={{1,0},{2,1},{3,2},{5,4},{6,5},{7,6},{9,8},{10,9},{11,10},{13,12},{... | collective-permute-start | bytes 11528 | tf_op jit(solution)/shard_map/ppermute | solution.py:17
  135.1 15.7 %collective-permute-start.20 = (bf16[16,64,128]{2,0,1:T(8,128)(2,1)S(1)}, bf16[16,64,128]{2,0,1:T(8,128)(2,1)S(1)}, u32[]{:S(2)}, u32[]{:S(2)}) collective-permute-start(bf16[16,64,128]{2,0,1:T(8,128)(2,1)S(1)} %fusion.46), channel_id=1, source_target_pairs={{8,0},{16,8},{24,16},{9,1},{17,9},{25,17},{10,2},{18,10},{26,18},{... | collective-permute-start | bytes 786440 | tf_op jit(solution)/shard_map/ppermute | solution.py:25
  136.4 14.4 %collective-permute-start.22 = (bf16[16,64,128]{2,0,1:T(8,128)(2,1)S(1)}, bf16[16,64,128]{2,0,1:T(8,128)(2,1)S(1)}, u32[]{:S(2)}, u32[]{:S(2)}) collective-permute-start(bf16[16,64,128]{2,0,1:T(8,128)(2,1)S(1)} %fusion.46), channel_id=1, source_target_pairs={{24,0},{25,1},{26,2},{27,3},{28,4},{29,5},{30,6},{31,7}} | collective-permute-start | bytes 786440 | tf_op jit(solution)/shard_map/ppermute | solution.py:25
  141.0 8.5 %copy-start.22 = (u32[32]{0:T(128)S(1)}, u32[32]{0:T(128)}, u32[]{:S(2)}) copy-start(u32[32]{0:T(128)} %constant.107) | copy-start | bytes 388
  141.2 10.2 %collective-permute-start.21 = (bf16[16,64,128]{2,0,1:T(8,128)(2,1)S(1)}, bf16[16,64,128]{2,0,1:T(8,128)(2,1)S(1)}, u32[]{:S(2)}, u32[]{:S(2)}) collective-permute-start(bf16[16,64,128]{2,0,1:T(8,128)(2,1)S(1)} %fusion.48), channel_id=1, source_target_pairs={{0,24},{1,25},{2,26},{3,27},{4,28},{5,29},{6,30},{7,31}} | collective-permute-start | bytes 786440 | tf_op jit(solution)/shard_map/ppermute | solution.py:25
  145.6 5.9 %collective-permute-start.8 = (bf16[16,64,128]{2,0,1:T(8,128)(2,1)S(1)}, bf16[16,64,128]{2,0,1:T(8,128)(2,1)S(1)}, u32[]{:S(2)}, u32[]{:S(2)}) collective-permute-start(bf16[16,64,128]{2,0,1:T(8,128)(2,1)S(1)} %fusion.48), channel_id=1, source_target_pairs={{0,8},{8,16},{16,24},{1,9},{9,17},{17,25},{2,10},{10,18},{18,26},{... | collective-permute-start | bytes 786440 | tf_op jit(solution)/shard_map/ppermute | solution.py:25
  (10 other events, 13.4 us)
Sparse Core Ops, SparseCore 0:
  133.5 97.0 all-reduce.4
where the time goes:
time: 242 us; the launch traced here: 241 us
  starting transfers between devices  82.8 us (34%)
  waiting for transfers between devices  77.5 us (32%)
  local copies, waits for them, and re-layouts  43.6 us (18%)
  between operations  18 us (7%)
  other arithmetic  9.96 us (4%)
  matrix products  8.72 us (4%)
    unnamed x2, waiting for transfers between devices  76.8 us
    ppermute x11, starting transfers between devices, padded_2(): before = lax.ppermute(last, axis, up)  46.9 us
    ppermute x12, starting transfers between devices, padded_2(): after = lax.ppermute(leading, axis, down)  15.7 us
    slice x9, local copies, waits for them, and re-layouts, kernel_grad(): padded[row_tap:row_tap + stride * (height - 1) + 1:stride, col_tap:col_ta...  13.4 us
    scatter x1, local copies, waits for them, and re-layouts, fetch_condition(): jnp.zeros((owners, capacity), jnp.int32).at[owner_ids, slot_ids]  10.1 us
    unnamed x63, local copies, waits for them, and re-layouts  8.39 us
    ppermute x4, starting transfers between devices, from_behind(): return lax.ppermute(block, axis, route)  8.19 us
    all_to_all x1, starting transfers between devices, fetch_condition(): lax.all_to_all(request, 'ty', split_axis=0, concat_axis=0, tiled=True)  6.32 us
  transfers between devices with their start and end apart: 30, of which 2 were waited for; matrix products, arithmetic and copies ran while one was open for 18% of the time, Pallas kernels for 0%

commit v1 on v0

v1 whole, which is shorter than its diff:
```python
import functools
import math

import jax
import jax.numpy as jnp
from jax import lax
from jax.experimental import pallas as pl
from jax.experimental.pallas import tpu as pltpu
from jax.sharding import PartitionSpec as P

F32 = jnp.float32
BF16 = jnp.bfloat16
VMEM = pl.BlockSpec(memory_space=pltpu.VMEM)
SMEM = pl.BlockSpec(memory_space=pltpu.SMEM)
LEFT = 8
PAD = 48
STRIP_ROWS = 7


def whole_block(leaf):
    return pl.BlockSpec(leaf.shape, lambda i: (0,) * len(leaf.shape))


def call(body, out_shape, in_specs, scratch=(), flops=0, moved=0, limit=48, grid=()):
    out_specs = jax.tree.map(whole_block if grid else lambda _: VMEM, out_shape)
    return pl.pallas_call(
        body,
        out_shape=out_shape,
        grid=grid,
        in_specs=in_specs,
        out_specs=out_specs,
        scratch_shapes=list(scratch),
        compiler_params=pltpu.CompilerParams(vmem_limit_bytes=limit * 1024 * 1024),
        cost_estimate=pl.CostEstimate(flops=flops, bytes_accessed=moved, transcendentals=0),
    )


def sublane(shape):
    return lax.broadcasted_iota(jnp.int32, shape, len(shape) - 2)


def flag(condition):
    return jnp.where(condition, 1.0, 0.0).astype(F32)


def traits():
    segments = lax.axis_size("segment")
    position = lax.axis_index("segment")
    decoder = flag(position >= segments // 2)
    return decoder, 1.0 - decoder, position == segments - 1


def edge_kernel(owner, cell, land, act_l, act_r, par_l, par_r, st_l, st_r, gr_l, gr_r, coarse, pay0, pay1):
    decoder, encoder, last = traits()
    rows = act_l.shape[1]
    groups = rows // 4
    per_row = cell.shape[0] // groups
    low = sublane((8, 128)) < 4

    def weights(first):
        parts = []
        for row in range(groups):
            pair = [jnp.where(last, land[row, first + k], 1).astype(F32) for k in range(2)]
            parts.append(jnp.where(low, pair[0], pair[1])[None])
        plane = jnp.concatenate(parts, axis=0)
        return jnp.broadcast_to(plane[:, None], (groups, 4, 8, 128)).reshape(rows, 8, 128)

    def ids(column):
        tile = jnp.zeros((8, 128), F32)
        where = sublane((8, 128))
        for row in range(groups):
            spot = row * per_row + column
            tile = jnp.where(where == row, owner[spot, 0].astype(F32), tile)
            tile = jnp.where(where == 4 + row, cell[spot].astype(F32), tile)
        return tile

    def parts(side, act, par, st, gr, first):
        pick = slice(0, 8) if side == 0 else slice(8, 16)
        f = lambda ref: ref[0].astype(F32)[:, pick]
        grad = ((f(gr) + encoder * f(par)) * weights(first)).astype(BF16).astype(F32)
        block = f(act) + decoder * f(par)
        return grad, f(st), block

    where = sublane((rows, 8, 128))
    grad, st, block = parts(0, act_l, par_l, st_l, gr_l, 0)
    after = jnp.where(
        where < 3, grad, jnp.where(where < 5, pltpu.roll(st, 3, 1), pltpu.roll(block, 5, 1))
    )
    grad, st, block = parts(1, act_r, par_r, st_r, gr_r, per_row - 2)
    before = jnp.where(
        where == 7, grad, jnp.where(where == 6, pltpu.roll(st, 7, 1), pltpu.roll(block, 6, 1))
    )
    even = lax.axis_index("ty") % 2 == 0
    pay0[0:rows] = jnp.where(even, before, after).astype(BF16)
    pay1[0:rows] = jnp.where(even, after, before).astype(BF16)
    left_ids, right_ids = ids(0), ids(per_row - 1)
    pay0[rows] = jnp.where(even, right_ids, left_ids).astype(BF16)
    pay1[rows] = jnp.where(even, left_ids, right_ids).astype(BF16)
    held = coarse[...].reshape(coarse.shape[0] // 8, 8, 128)
    pay0[rows + 1 :] = held
    pay1[rows + 1 :] = held


def extend_kernel(
    merged, owner, cell, land, act, par, st, gr, z0, z1, coarse, *rest
):
    if merged:
        z2, ypay0, ypay1, ext, table, plane = rest
    else:
        ypay0, ypay1, ext, table, plane = rest
    decoder, encoder, last = traits()
    rows, breadth = act.shape[1], act.shape[2]
    groups = rows // 4
    per_row = cell.shape[0] // groups
    cells = coarse.shape[0] if merged else cell.shape[0]
    ty, owners = lax.axis_index("ty"), lax.axis_size("ty")
    even = ty % 2 == 0
    has_before, has_after = ty > 0, ty < owners - 1
    low = sublane((8, 128)) < 4
    if merged:
        table[pl.ds(pl.multiple_of(ty * cells, 8), cells)] = coarse[...].astype(F32)
        others = (
            (ty ^ 1, z0[rows + 1 :].astype(F32).reshape(cells, 128)),
            (ty ^ 3, z1[rows + 1 :].astype(F32).reshape(cells, 128)),
            (ty ^ 2, z2[...].astype(F32)),
        )
        for other, value in others:
            table[pl.ds(pl.multiple_of(other * cells, 8), cells)] = value
    else:
        table[...] = coarse[...].astype(F32)

    first, second = z0[0 : rows + 1].astype(F32), z1[0 : rows + 1].astype(F32)
    before = jnp.where(has_before, jnp.where(even, second, first), 0.0)
    after = jnp.where(has_after, jnp.where(even, first, second), 0.0)

    def rim_condition(tile, valid):
        wanted = tile[rows]
        spot = wanted * cells + pltpu.roll(wanted, 4, 0)
        lanes = lax.broadcasted_iota(jnp.int32, (8, table.shape[0]), 1).astype(F32)
        spread = jnp.broadcast_to(spot[:, 0:1], lanes.shape)
        hot = jnp.where(spread == lanes, 1.0, 0.0).astype(BF16)
        named = lax.dot(hot, table[...].astype(BF16), preferred_element_type=F32)
        picked = [jnp.broadcast_to(named[row : row + 1], (8, 128))[None] for row in range(groups)]
        spread_rows = jnp.concatenate([p for p in picked for _ in range(4)], axis=0)
        return jnp.where(valid, spread_rows, 0.0)

    wide = LEFT + breadth
    ext[0, :, 0:8] = before[0:rows].astype(BF16)
    ext[1, :, 0:8] = pltpu.roll(before[0:rows], 1, 1).astype(BF16)
    rim = pltpu.roll(before[0:rows], 2, 1) + rim_condition(before, has_before)
    ext[2, :, 0:8] = rim.astype(BF16)
    ext[0, :, wide : wide + 8] = after[0:rows].astype(BF16)
    ext[1, :, wide : wide + 8] = pltpu.roll(after[0:rows], 5, 1).astype(BF16)
    rim = pltpu.roll(after[0:rows], 3, 1) + rim_condition(after, has_after)
    ext[2, :, wide : wide + 8] = rim.astype(BF16)
    ext[1, :, LEFT:wide] = st[0]

    for group in range(groups):
        for part in range(breadth // 8):
            spots = [group * per_row + 2 * part + k for k in range(2)]
            named = [
                jnp.broadcast_to(table[pl.ds(owner[s, 0] * cells + cell[s], 1)], (8, 128)) for s in spots
            ]
            plane[0, group, 8 * part : 8 * part + 8] = jnp.where(low, named[0], named[1])
            weigh = [jnp.where(last, land[group, 2 * part + k], 1).astype(F32) for k in range(2)]
            plane[1, group, 8 * part : 8 * part + 8] = jnp.where(low, weigh[0], weigh[1])
    for row in range(rows):
        partner = par[0, row].astype(F32)
        block = act[0, row].astype(F32) + decoder * partner + plane[0, row // 4]
        ext[2, row, LEFT:wide] = block.astype(BF16)
        grad = (gr[0, row].astype(F32) + encoder * partner) * plane[1, row // 4]
        ext[0, row, LEFT:wide] = grad.astype(BF16)

    upper = lax.axis_index("tx") % 2 == 0
    leading = [(0, 0), (0, 1), (0, 2), (1, 0), (1, 1), (2, 0), (2, 1)]
    closing = [(0, rows - 1), (1, rows - 1), (2, rows - 3), (2, rows - 2), (2, rows - 1)]
    closing = closing + closing[-1:] * 2
    for k in range(STRIP_ROWS):
        top, bottom = ext[leading[k]], ext[closing[k]]
        ypay0[k] = jnp.where(upper, bottom, top)
        ypay1[k] = jnp.where(upper, top, bottom)


def rims(y0, y1):
    tx = lax.axis_index("tx")
    upper = tx % 2 == 0
    before_ok, after_ok = tx > 0, tx < lax.axis_size("tx") - 1

    def row(valid, from_first, k):
        value = jnp.where(from_first, y0[k].astype(F32), y1[k].astype(F32))
        return jnp.where(valid, value, 0.0)

    before = lambda k: row(before_ok, jnp.logical_not(upper), k)
    after = lambda k: row(after_ok, upper, k)
    return before, after


def spread_taps(field, taps, odd_taps, count, first):
    for row in range(count):
        target = taps if row % 2 == 0 else odd_taps
        for tap in range(3):
            value = field[row, pl.ds(first + tap, PAD, stride=2), :]
            target[row // 2, :, tap * 128 : tap * 128 + 128] = value.astype(BF16)


def three_rows(even_taps, odd_taps, count):
    wide = 3 * 128
    whole = lambda ref, a: ref[a : a + count].reshape(count * PAD, wide)
    return whole(even_taps, 0), whole(odd_taps, 0), whole(even_taps, 1)


def lower(even_taps, odd_taps, count, down):
    views = three_rows(even_taps, odd_taps, count)
    wide = 3 * 128
    total = None
    for a in range(3):
        term = lax.dot(views[a], down[a * wide : a * wide + wide], preferred_element_type=F32)
        total = term if total is None else total + term
    return total


def lane_taps(up, flat_up):
    for tap in range(9):
        flat_up[:, tap * 128 : tap * 128 + 128] = up[tap]


def grads_kernel(
    ext, y0, y1, down, up, coupled, up_flat, down_flat, field, even_taps, odd_taps, sums, flat_up, d0, d1
):
    rows = ext.shape[1]
    breadth = ext.shape[2] - 16
    half_rows, half_cols = rows // 2, breadth // 2
    count = half_rows + 1
    before, after = rims(y0, y1)
    wide = ext.shape[2]
    tx, ty = lax.axis_index("tx"), lax.axis_index("ty")
    has_below, has_right = tx < lax.axis_size("tx") - 1, ty < lax.axis_size("ty") - 1
    lane_taps(up, flat_up)
    field[:, wide:] = jnp.zeros((field.shape[0], field.shape[1] - wide, 128), F32)
    field[0, 0:wide] = before(1)
    for row in range(rows):
        field[row + 1, 0:wide] = ext[1, row].astype(F32)
    for k in range(2):
        field[rows + 1 + k, 0:wide] = after(3 + k)
    spread_taps(field, even_taps, odd_taps, 2 * count + 1, LEFT - 1)
    pre_back = lower(even_taps, odd_taps, count, down)
    logistic = 1.0 / (1.0 + jnp.exp(-pre_back))
    reduced = pre_back * logistic
    slope = logistic * (1.0 + pre_back * (1.0 - logistic))
    depth = pre_back.shape[1]
    shape = (count, PAD, depth)
    row = lax.broadcasted_iota(jnp.int32, shape, 0).reshape(count * PAD, depth)
    col = lax.broadcasted_iota(jnp.int32, shape, 1).reshape(count * PAD, depth)
    own = (row < half_rows) & (col < half_cols)
    inside = ((row < half_rows) | has_below) & ((col < half_cols) | (has_right & (col == half_cols)))
    reduced = jnp.where(own, reduced, 0.0).astype(BF16)

    field[0, 0:wide] = before(0)
    for row_id in range(rows):
        field[row_id + 1, 0:wide] = ext[0, row_id].astype(F32)
    for k in range(3):
        field[rows + 1 + k, 0:wide] = after(k)
    previous = None
    for row_id in range(2 * count + 2):
        plane = [field[row_id, pl.ds(LEFT - 1 + k, PAD, stride=2), :] for k in range(4)]
        current = [plane[2] + plane[3], plane[1] + plane[2], plane[0] + plane[1]]
        if row_id > 0:
            start = row_id - 2
            for a in range(3):
                if (start - 1 + a) % 2 == 0 and 0 <= (start - 1 + a) // 2 < count:
                    p = (start - 1 + a) // 2
                    for b in range(3):
                        tap = 3 * a + b
                        sums[p, :, tap * 128 : tap * 128 + 128] = (previous[b] + current[b]).astype(BF16)
        previous = current
    windows = sums[...].reshape(count * PAD, 9 * 128)
    raised = lax.dot_general(windows, flat_up[...], (((1,), (1,)), ((), ())), preferred_element_type=F32)
    pre_grad = jnp.where(inside, raised * slope, 0.0).astype(BF16)
    coupled[...] = pre_grad.reshape(count, PAD, depth)

    terms = lax.dot_general(reduced, windows, (((0,), (0,)), ((), ())), preferred_element_type=F32)
    for tap in range(9):
        up_flat[tap * depth : tap * depth + depth] = terms[:, tap * 128 : tap * 128 + 128]

    own_grad = jnp.where(own, pre_grad, jnp.zeros_like(pre_grad))
    views = three_rows(even_taps, odd_taps, count)
    span = 3 * 128
    for a in range(3):
        term = lax.dot_general(views[a], own_grad, (((0,), (0,)), ((), ())), preferred_element_type=F32)
        d0[a * span : a * span + span] = term[:, 0:128]
        d1[a * span : a * span + span, 0:64] = term[:, 128:192]
    pairs = d0.shape[0] // 2
    left_even, left_odd = d0[pl.ds(0, pairs, stride=2)], d0[pl.ds(1, pairs, stride=2)]
    right_even, right_odd = d1[pl.ds(0, pairs, stride=2)], d1[pl.ds(1, pairs, stride=2)]
    near = lax.broadcasted_iota(jnp.int32, left_even.shape, 1) < 64
    turned = pltpu.roll(left_odd, 64, 1)
    down_flat[pl.ds(0, pairs, stride=3)] = left_even
    down_flat[pl.ds(1, pairs, stride=3)] = jnp.where(near, right_even, turned)
    down_flat[pl.ds(2, pairs, stride=3)] = jnp.where(near, turned, pltpu.roll(right_odd, 64, 1))


def relay_kernel(
    ext, y0, y1, coupled, down, up, ahead, behind, field, even_taps, odd_taps, products, flat_up, mixed, fine
):
    rows = ext.shape[1]
    breadth = ext.shape[2] - 16
    half_rows, half_cols = rows // 2, breadth // 2
    wide = ext.shape[2]
    depth = coupled.shape[2]
    tx, ty = lax.axis_index("tx"), lax.axis_index("ty")
    has_below, has_right = tx < lax.axis_size("tx") - 1, ty < lax.axis_size("ty") - 1
    position, segments = lax.axis_index("segment"), lax.axis_size("segment")

    count = half_rows + 1
    grads = coupled[...].reshape(count * PAD, depth)
    moved = lax.dot_general(grads, down[...], (((1,), (1,)), ((), ())), preferred_element_type=F32)
    products[0:count] = moved.reshape(count, PAD, 9 * 128)

    def part(p, a, b, offset):
        tap = 3 * a + b
        return products[p, offset : offset + half_cols, tap * 128 : tap * 128 + 128]

    for p in range(half_rows):
        fine[2 * p, pl.ds(0, half_cols, stride=2), :] = part(p, 1, 1, 0)
        fine[2 * p, pl.ds(1, half_cols, stride=2), :] = part(p, 1, 2, 0) + part(p, 1, 0, 1)
        fine[2 * p + 1, pl.ds(0, half_cols, stride=2), :] = part(p, 2, 1, 0) + part(p + 1, 0, 1, 0)
        fine[2 * p + 1, pl.ds(1, half_cols, stride=2), :] = (
            part(p, 2, 2, 0) + part(p, 2, 0, 1) + part(p + 1, 0, 2, 0) + part(p + 1, 0, 0, 1)
        )
    for row in range(rows):
        value = ext[0, row, LEFT : LEFT + breadth].astype(F32) + fine[row]
        behind[row] = value.astype(BF16)

    lane_taps(up, flat_up)
    before, after = rims(y0, y1)
    count = half_rows + 2
    field[:, wide:] = jnp.zeros((field.shape[0], field.shape[1] - wide, 128), F32)
    for k in range(3):
        field[k, 0:wide] = before(2 + k)
    for row in range(rows):
        field[row + 3, 0:wide] = ext[2, row].astype(F32)
    for k in range(2):
        field[rows + 3 + k, 0:wide] = after(5 + k)
    spread_taps(field, even_taps, odd_taps, 2 * count + 1, LEFT - 3)
    pre_down = lower(even_taps, odd_taps, count, down)
    reduced = pre_down / (1.0 + jnp.exp(-pre_down))
    shape = (count, PAD, depth)
    row_id = lax.broadcasted_iota(jnp.int32, shape, 0).reshape(count * PAD, depth)
    col_id = lax.broadcasted_iota(jnp.int32, shape, 1).reshape(count * PAD, depth)
    inside = ((row_id <= half_rows) | has_below) & ((col_id <= half_cols) | has_right)
    reduced = jnp.where(inside, reduced, 0.0).astype(BF16)
    raised = lax.dot(reduced, flat_up[...], preferred_element_type=F32)
    products[0:count] = raised.reshape(count, PAD, 9 * 128)

    def tap_rows(p, dy, b):
        at = lambda q, a: products[q, :, (3 * a + b) * 128 : (3 * a + b) * 128 + 128]
        if dy == 0:
            return at(p, 0) + at(p + 1, 1) + at(p + 1, 2)
        return at(p + 1, 0) + at(p + 1, 1) + at(p + 2, 2)

    for p in range(half_rows):
        for dy in range(2):
            col = [tap_rows(p, dy, b) for b in range(3)]
            mixed[0, 0:PAD], mixed[1, 0:PAD] = col[0], col[1] + col[2]
            mixed[2, 0:PAD], mixed[3, 0:PAD] = col[0] + col[1], col[2]
            line = 2 * p + dy
            fine[line, pl.ds(0, half_cols, stride=2), :] = mixed[0, 0:half_cols] + mixed[1, 1 : half_cols + 1]
            fine[line, pl.ds(1, half_cols, stride=2), :] = (
                mixed[2, 1 : half_cols + 1] + mixed[3, 2 : half_cols + 2]
            )
    for row in range(rows):
        value = (ext[2, row, LEFT : LEFT + breadth].astype(F32) + fine[row]).astype(BF16)
        in_grad = behind[row]
        ahead[row] = jnp.where(position == segments - 1, in_grad, value)
        behind[row] = jnp.where(position == 0, value, in_grad)


def swaps(axis):
    size = lax.axis_size(axis)
    pairs = [(i, i + 1) for i in range(0, size - 1, 2)]
    other = [(i, i + 1) for i in range(1, size - 1, 2)]
    both = lambda pairs: pairs + [(j, i) for i, j in pairs]
    return both(pairs), both(other)


def crossed(axis, distance):
    return [(i, i ^ distance) for i in range(lax.axis_size(axis))]


def split_kernel(up_flat, down_flat, up_send, up_keep, down_send, down_keep):
    half = up_keep.shape[0]
    tx = lax.axis_index("tx")
    mine, theirs = pl.multiple_of(tx * half, 8), pl.multiple_of((1 - tx) * half, 8)
    for flat, send, keep in ((up_flat, up_send, up_keep), (down_flat, down_send, down_keep)):
        send[...] = flat[pl.ds(theirs, half)].astype(BF16)
        keep[...] = flat[pl.ds(mine, half)]


def pieces_kernel(got, kept, own, *sends):
    count = own.shape[0]
    ty = lax.axis_index("ty")
    for distance, target in enumerate(sends):
        start = pl.multiple_of((ty ^ (distance + 1)) * count, 8)
        total = kept[pl.ds(start, count)] + got[pl.ds(start, count)].astype(F32)
        target[...] = total.astype(BF16)
    start = pl.multiple_of(ty * count, 8)
    own[...] = kept[pl.ds(start, count)] + got[pl.ds(start, count)].astype(F32)


def total_kernel(scaling, own, first, second, third, out):
    total = own[...] + first[...].astype(F32) + second[...].astype(F32) + third[...].astype(F32)
    out[...] = total * scaling


def shape(dims, kind):
    return jax.ShapeDtypeStruct(tuple(dims), kind)


def local(
    act_in,
    partner_in,
    stashed,
    grad_in,
    down_weights,
    up_weights,
    coarse,
    nest_owner,
    nest_cell,
    land_weight,
):
    height, breadth, channels = act_in.shape[1:]
    depth = down_weights.shape[-1]
    half_rows = height // 2
    n_tx, n_ty = lax.axis_size("tx"), lax.axis_size("ty")
    position, segments = lax.axis_index("segment"), lax.axis_size("segment")
    scaling = 1.0 / math.sqrt(height * breadth * n_tx * n_ty)
    down_flat_w = down_weights.reshape(9 * channels, depth)
    up_taps = up_weights.reshape(9, depth, channels)

    left = pl.BlockSpec((1, height, 16, channels), lambda i: (0, 0, 0, 0))
    right = pl.BlockSpec((1, height, 16, channels), lambda i: (0, 0, breadth // 16 - 1, 0))
    pay = shape((height + 1 + coarse.shape[0] // 8, 8, channels), BF16)
    z_pay0, z_pay1 = call(edge_kernel, (pay, pay), [SMEM] * 3 + [left, right] * 4 + [whole_block(coarse)], grid=(1,))(
        nest_owner,
        nest_cell,
        land_weight,
        act_in,
        act_in,
        partner_in,
        partner_in,
        stashed,
        stashed,
        grad_in,
        grad_in,
        coarse,
    )
    merged = n_ty == 4
    pairs, others = swaps("ty")
    if merged:
        others = crossed("ty", 3)
    z0 = lax.ppermute(z_pay0, "ty", pairs)
    z1 = lax.ppermute(z_pay1, "ty", others)
    if merged:
        table_parts = (coarse, lax.ppermute(coarse, "ty", crossed("ty", 2)))
    else:
        table_parts = (lax.all_gather(coarse, "ty", tiled=True),)
    strips = shape((STRIP_ROWS, breadth + 16, channels), BF16)
    operands = (act_in, partner_in, stashed, grad_in, z0, z1, table_parts[0], *table_parts[1:])
    y_pay0, y_pay1, ext = call(
        functools.partial(extend_kernel, merged),
        (strips, strips, shape((3, height, breadth + 16, channels), BF16)),
        [SMEM] * 3 + [VMEM] * len(operands),
        [
            pltpu.VMEM((n_ty * coarse.shape[0], channels), F32),
            pltpu.VMEM((2, height // 4, breadth, channels), F32),
        ],
    )(nest_owner, nest_cell, land_weight, *operands)
    pairs, others = swaps("tx")
    y0 = lax.ppermute(y_pay0, "tx", pairs)
    y1 = lax.ppermute(y_pay1, "tx", others) if others else y_pay1

    wide = 2 * PAD + 16
    count = half_rows + 2
    rows_flat = 9 * depth
    taps = [
        pltpu.VMEM((2 * count + 2, wide, channels), F32),
        pltpu.VMEM((count + 1, PAD, 3 * channels), BF16),
        pltpu.VMEM((count + 1, PAD, 3 * channels), BF16),
    ]
    flat_up = pltpu.VMEM((depth, 9 * channels), BF16)
    coupled, up_flat, down_flat = call(
        grads_kernel,
        (
            shape((half_rows + 1, PAD, depth), BF16),
            shape((rows_flat, channels), F32),
            shape((rows_flat, channels), F32),
        ),
        [VMEM] * 5,
        taps
        + [
            pltpu.VMEM((half_rows + 1, PAD, 9 * channels), BF16),
            flat_up,
            pltpu.VMEM((9 * channels, 128), F32),
            pltpu.VMEM((9 * channels, 128), F32),
        ],
        flops=500_000_000,
        moved=4_000_000,
    )(ext, y0, y1, down_flat_w, up_taps)

    if n_tx == 2 and n_ty == 4:
        half, piece = rows_flat // 2, rows_flat // 8
        up_send, up_keep, down_send, down_keep = call(
            split_kernel,
            (shape((half, channels), BF16), shape((half, channels), F32)) * 2,
            [VMEM] * 2,
        )(up_flat, down_flat)
        sums = []
        for send, keep in ((down_send, down_keep), (up_send, up_keep)):
            got = lax.ppermute(send, "tx", crossed("tx", 1))
            own, *sends = call(
                pieces_kernel,
                (shape((piece, channels), F32),) + (shape((piece, channels), BF16),) * 3,
                [VMEM] * 2,
            )(got, keep)
            arrived = [lax.ppermute(s, "ty", crossed("ty", d + 1)) for d, s in enumerate(sends)]
            total = call(
                functools.partial(total_kernel, scaling), shape((piece, channels), F32), [VMEM] * 4
            )(own, *arrived)
            sums.append(total.reshape(1, -1))
        down_sum, up_sum = sums
    else:
        pooled = lambda flat: lax.psum_scatter(
            flat.reshape(-1) * scaling, ("tx", "ty"), scatter_dimension=0, tiled=True
        )[None]
        down_sum, up_sum = pooled(down_flat), pooled(up_flat)

    tile = shape((height, breadth, channels), BF16)
    ahead, behind = call(
        relay_kernel,
        (tile, tile),
        [VMEM] * 6,
        taps
        + [
            pltpu.VMEM((count, PAD, 9 * channels), F32),
            flat_up,
            pltpu.VMEM((4, PAD, channels), F32),
            pltpu.VMEM((height, breadth, channels), F32),
        ],
        flops=600_000_000,
        moved=4_000_000,
    )(ext, y0, y1, coupled, down_flat_w, up_taps)
    from_before = lax.ppermute(ahead, "segment", [(i, (i + 1) % segments) for i in range(segments)])
    from_after = lax.ppermute(behind, "segment", [((i + 1) % segments, i) for i in range(segments)])
    blank = jnp.zeros_like(from_before)
    act_out = jnp.where(position == 0, blank, from_before)
    grad_out = jnp.where(position == segments - 1, blank, from_after)
    partner_out = jnp.where(position % 2 == 0, from_before, from_after)
    return (act_out[None], grad_out[None], partner_out[None], down_sum, up_sum)


def solution(mesh):
    tile = P("segment", "tx", "ty", None)
    weights = P("segment", None, None, None, None)
    grads = P("segment", ("tx", "ty"))
    rows = P(("tx", "ty"))
    return jax.shard_map(
        local,
        mesh=mesh,
        in_specs=(tile,) * 4 + (weights,) * 2 + (P(("tx", "ty"), None),) * 2 + (rows, P("tx", "ty")),
        out_specs=(tile,) * 3 + (grads,) * 2,
        check_vma=False,
    )
```

time: 242 us -> 49.9 us (0.21)
  starting transfers between devices: 82.8 us -> 19.5 us
  waiting for transfers between devices: 77.5 us -> 15 us
  local copies, waits for them, and re-layouts: 43.6 us -> 4.83 us
  between operations: 18 us -> 0.77 us
  other arithmetic: 9.96 us -> 0.9 us
  matrix products: 8.72 us -> 0 us
  Pallas kernels: 0 us -> 8.63 us
    unnamed x2 -> x0, waiting for transfers between devices: 76.8 us -> none
    ppermute x27 -> x14, starting transfers between devices: 70.8 us -> 19.5 us  [the longest x6 8.35 us: local(): lax.ppermute(s, 'ty', crossed('ty', d + 1))]
    slice x16 -> x0, local copies, waits for them, and re-layouts: 14.9 us -> none  [the longest x9 13.4 us: kernel_grad(): padded[row_tap:row_tap + stride * (height - 1) + 1:stride, col_tap:col_ta...]
    ppermute x27 -> x14, waiting for transfers between devices: 0.69 us -> 15 us  [the longest x1 4.53 us: local(): table_parts = (coarse, lax.ppermute(coarse, 'ty', crossed('ty', 2)))]
    all_to_all x2 -> x0, starting transfers between devices: 12 us -> none  [the longest x1 6.32 us: fetch_condition(): lax.all_to_all(request, 'ty', split_axis=0, concat_axis=0, tiled=True)]
    scatter x1 -> x0, local copies, waits for them, and re-layouts: 10.1 us -> none  [fetch_condition(): jnp.zeros((owners, capacity), jnp.int32).at[owner_ids, slot_ids]]
    pallas_call x0 -> x9, Pallas kernels: none -> 8.63 us  [the longest x1 2.23 us: local(): call(relay_kernel, (tile, tile), [VMEM] * 6, taps + [pltpu.VMEM((count, P...]
    dot_general x18 -> x0, matrix products: 5.13 us -> none  [kernel_grad(): lax.dot_general(window, flat_grad, (((0,), (0,)), ((), ())), preferred_el...]
  transfers between devices with their start and end apart: 30 -> 14, of which waited for: 2 -> 5; matrix products, arithmetic and copies ran while one was open for 18% -> 2% of each run, Pallas kernels for 0% -> 6%
where the time goes in v1:
time: 49.9 us; the launch traced here: 49.6 us
  starting transfers between devices  19.5 us (39%)
  waiting for transfers between devices  15 us (30%)
  Pallas kernels  8.63 us (17%)
  local copies, waits for them, and re-layouts  4.83 us (10%)
  other arithmetic  0.9 us (2%)
  between operations  0.77 us (2%)
    ppermute x6, starting transfers between devices, local(): lax.ppermute(s, 'ty', crossed('ty', d + 1))  8.35 us
    unnamed x20, local copies, waits for them, and re-layouts  4.83 us
    ppermute x1, waiting for transfers between devices, local(): table_parts = (coarse, lax.ppermute(coarse, 'ty', crossed('ty', 2)))  4.53 us
    ppermute x2, waiting for transfers between devices, local(): got = lax.ppermute(send, 'tx', crossed('tx', 1))  4.37 us
    ppermute x1, waiting for transfers between devices, local(): y0 = lax.ppermute(y_pay0, 'tx', pairs)  3.32 us
    ppermute x1, starting transfers between devices, local(): z0 = lax.ppermute(z_pay0, 'ty', pairs)  3.09 us
    ppermute x6, waiting for transfers between devices, local(): lax.ppermute(s, 'ty', crossed('ty', d + 1))  2.74 us
    ppermute x1, starting transfers between devices, local(): z1 = lax.ppermute(z_pay1, 'ty', others)  2.47 us
  transfers between devices with their start and end apart: 14, of which 5 were waited for; matrix products, arithmetic and copies ran while one was open for 2% of the time, Pallas kernels for 6%

profile of v1, /device:TPU:0, one launch (start us, length us, event | category | flops | bytes accessed | tf_op | source)
XLA Modules:
  0.0 49.6 jit_solution(15737904997966003848)
XLA Ops:
  0.6 0.0 copy-start.7
  0.6 0.0 copy-start.6
  0.7 0.0 copy-start.5
  0.7 0.8 %copy.16.owner = s32[64,1]{1,0:T(8,128)S(1)} copy(s32[64,1]{0,1:T(1,128)} %param.17) | data formatting | bytes 512 | tf_op args[7]
  1.4 0.0 copy-start
  1.5 0.9 %copy-done = bf16[1,16,64,128]{3,2,1,0:T(8,128)(2,1)S(1)} copy-done((bf16[1,16,64,128]{3,2,1,0:T(8,128)(2,1)S(1)}, bf16[1,16,64,128]{3,2,1,0:T(8,128)(2,1)}, u32[]{:S(2)}) %copy-start) | copy-done | bytes 262168
  2.4 0.9 %copy-done.1 = bf16[1,16,64,128]{3,2,1,0:T(8,128)(2,1)S(1)} copy-done((bf16[1,16,64,128]{3,2,1,0:T(8,128)(2,1)S(1)}, bf16[1,16,64,128]{3,2,1,0:T(8,128)(2,1)}, u32[]{:S(2)}) %copy-start.1) | copy-done | bytes 262168
  3.4 0.9 %copy-done.2 = bf16[1,16,64,128]{3,2,1,0:T(8,128)(2,1)S(1)} copy-done((bf16[1,16,64,128]{3,2,1,0:T(8,128)(2,1)S(1)}, bf16[1,16,64,128]{3,2,1,0:T(8,128)(2,1)}, u32[]{:S(2)}) %copy-start.2) | copy-done | bytes 262168
  4.3 0.9 %copy-done.3 = bf16[1,16,64,128]{3,2,1,0:T(8,128)(2,1)S(1)} copy-done((bf16[1,16,64,128]{3,2,1,0:T(8,128)(2,1)S(1)}, bf16[1,16,64,128]{3,2,1,0:T(8,128)(2,1)}, u32[]{:S(2)}) %copy-start.3) | copy-done | bytes 262168
  5.2 1.2 %shard_map.137 = (bf16[25,8,128]{2,1,0:T(8,128)(2,1)S(1)}, bf16[25,8,128]{2,1,0:T(8,128)(2,1)S(1)}) custom-call(s32[64,1]{1,0:T(8,128)S(1)} %copy.16.owner, s32[64]{0:T(128)S(1)} %copy-done.7, s32[4,16]{1,0:T(4,128)S(1)} %copy-done.6, bf16[1,16,64,128]{3,2,1,0:T(8,128)(2,1)S(1)} %copy-done, bf16[1,16,64,128]{3,2,1,0:T(8,128)(2,1)S(1)} %copy-done, ...), custom_call_target="tpu_custom_call" | custom-call | tf_op jit(solution)/shard_map/pallas_call | solution.py:443
  6.4 3.1 %collective-permute-start = (bf16[25,8,128]{2,1,0:T(8,128)(2,1)S(1)}, bf16[25,8,128]{2,1,0:T(8,128)(2,1)S(1)}, u32[]{:S(2)}, u32[]{:S(2)}) collective-permute-start(bf16[25,8,128]{2,1,0:T(8,128)(2,1)S(1)} %get-tuple-element.27), channel_id=1, source_target_pairs={{0,1},{2,3},{1,0},{3,2},{4,5},{6,7},{5,4},{7,6},{8,9},{10,11},{9,8... | collective-permute-start | bytes 153608 | tf_op jit(solution)/shard_map/ppermute | solution.py:461
  9.5 2.5 %collective-permute-start.1 = (bf16[25,8,128]{2,1,0:T(8,128)(2,1)S(1)}, bf16[25,8,128]{2,1,0:T(8,128)(2,1)S(1)}, u32[]{:S(2)}, u32[]{:S(2)}) collective-permute-start(bf16[25,8,128]{2,1,0:T(8,128)(2,1)S(1)} %get-tuple-element.28), channel_id=1, source_target_pairs={{0,3},{1,2},{2,1},{3,0},{4,7},{5,6},{6,5},{7,4},{8,11},{9,10},{10,... | collective-permute-start | bytes 153608 | tf_op jit(solution)/shard_map/ppermute | solution.py:462
  12.0 0.1 collective-permute-start.2
  12.1 4.5 %collective-permute-done.2.rest_0_ = bf16[64,128]{1,0:T(8,128)(2,1)S(1)} collective-permute-done((bf16[64,128]{1,0:T(8,128)(2,1)S(1)}, bf16[64,128]{1,0:T(8,128)(2,1)S(1)}, u32[]{:S(2)}, u32[]{:S(2)}) %collective-permute-start.2) | collective-permute-done | bytes 16416 | tf_op jit(solution)/shard_map/ppermute | solution.py:464
  16.7 0.0 collective-permute-done.z0
  16.7 0.0 collective-permute-done.1.z1
  16.7 1.6 %shard_map.138 = (bf16[7,80,128]{2,1,0:T(8,128)(2,1)S(1)}, bf16[7,80,128]{2,1,0:T(8,128)(2,1)S(1)}, bf16[3,16,80,128]{3,2,1,0:T(8,128)(2,1)S(1)}) custom-call(s32[64,1]{1,0:T(8,128)S(1)} %copy.16.owner, s32[64]{0:T(128)S(1)} %copy-done.7, s32[4,16]{1,0:T(4,128)S(1)} %copy-done.6, bf16[1,16,64,128]{3,2,1,0:T(8,128)(2,1)S(1)} %copy-done, ...), custom_call_target="tpu_custom_call" | custom-call | tf_op jit(solution)/shard_map/pallas_call | solution.py:469
  18.3 0.0 copy-start.4
  18.3 1.6 %collective-permute-start.3 = (bf16[7,80,128]{2,1,0:T(8,128)(2,1)S(1)}, bf16[7,80,128]{2,1,0:T(8,128)(2,1)S(1)}, u32[]{:S(2)}, u32[]{:S(2)}) collective-permute-start(bf16[7,80,128]{2,1,0:T(8,128)(2,1)S(1)} %get-tuple-element.30), channel_id=1, source_target_pairs={{0,4},{4,0},{1,5},{5,1},{2,6},{6,2},{3,7},{7,3},{8,12},{12,8},{9,1... | collective-permute-start | bytes 430088 | tf_op jit(solution)/shard_map/ppermute | solution.py:479
  19.9 0.2 copy.17
  20.1 3.3 %collective-permute-done.3.y0 = bf16[7,80,128]{2,1,0:T(8,128)(2,1)S(1)} collective-permute-done((bf16[7,80,128]{2,1,0:T(8,128)(2,1)S(1)}, bf16[7,80,128]{2,1,0:T(8,128)(2,1)S(1)}, u32[]{:S(2)}, u32[]{:S(2)}) %collective-permute-start.3) | collective-permute-done | bytes 143392 | tf_op jit(solution)/shard_map/ppermute | solution.py:479
  23.4 2.1 %shard_map.139 = (bf16[9,48,192]{2,1,0:T(8,128)(2,1)S(1)}, f32[1728,128]{1,0:T(8,128)S(1)}, f32[1728,128]{1,0:T(8,128)S(1)}) custom-call(bf16[3,16,80,128]{3,2,1,0:T(8,128)(2,1)S(1)} %get-tuple-element.29.ext, bf16[7,80,128]{2,1,0:T(8,128)(2,1)S(1)} %collective-permute-done.3.y0, bf16[7,80,128]{2,1,0:T(8,128)(2,1)S(1)} %get-tuple-element.31.y1, ...), custom_call_target="tpu_custom_call" | custom-call | flops 500000000 | bytes 4000000 | tf_op jit(solution)/shard_map/pallas_call | solution.py:491
  25.5 0.1 shard_map.141
  25.6 1.6 %collective-permute-start.6 = (bf16[864,128]{1,0:T(8,128)(2,1)S(1)}, bf16[864,128]{1,0:T(8,128)(2,1)S(1)}, u32[]{:S(2)}, u32[]{:S(2)}) collective-permute-start(bf16[864,128]{1,0:T(8,128)(2,1)S(1)} %get-tuple-element.37), channel_id=1, source_target_pairs={{0,4},{4,0},{1,5},{5,1},{2,6},{6,2},{3,7},{7,3},{8,12},{12,8},{9,1... | collective-permute-start | bytes 663560 | tf_op jit(solution)/shard_map/ppermute | solution.py:519
  27.2 2.2 %shard_map.140 = (bf16[16,64,128]{2,1,0:T(8,128)(2,1)S(1)}, bf16[16,64,128]{2,1,0:T(8,128)(2,1)S(1)}) custom-call(bf16[3,16,80,128]{3,2,1,0:T(8,128)(2,1)S(1)} %get-tuple-element.29.ext, bf16[7,80,128]{2,1,0:T(8,128)(2,1)S(1)} %collective-permute-done.3.y0, bf16[7,80,128]{2,1,0:T(8,128)(2,1)S(1)} %get-tuple-element.31.y1, ...), custom_call_target="tpu_custom_call" | custom-call | flops 600000000 | bytes 4000000 | tf_op jit(solution)/shard_map/pallas_call | solution.py:538
  29.4 0.1 collective-permute-start.4
  29.5 1.7 %collective-permute-start.5 = (bf16[16,64,128]{2,1,0:T(8,128)(2,1)S(1)}, bf16[16,64,128]{2,1,0:T(8,128)(2,1)S(1)}, u32[]{:S(2)}, u32[]{:S(2)}) collective-permute-start(bf16[16,64,128]{2,1,0:T(8,128)(2,1)S(1)} %get-tuple-element.34), channel_id=1, source_target_pairs={{8,0},{16,8},{24,16},{0,24},{9,1},{17,9},{25,17},{1,25},{10,2},{18... | collective-permute-start | bytes 786440 | tf_op jit(solution)/shard_map/ppermute | solution.py:553
  31.2 0.5 %collective-permute-start.10 = (bf16[864,128]{1,0:T(8,128)(2,1)S(1)}, bf16[864,128]{1,0:T(8,128)(2,1)S(1)}, u32[]{:S(2)}, u32[]{:S(2)}) collective-permute-start(bf16[864,128]{1,0:T(8,128)(2,1)S(1)} %get-tuple-element.43), channel_id=1, source_target_pairs={{0,4},{4,0},{1,5},{5,1},{2,6},{6,2},{3,7},{7,3},{8,12},{12,8},{9,1... | collective-permute-start | bytes 663560 | tf_op jit(solution)/shard_map/ppermute | solution.py:519
  31.7 0.0 collective-permute-done.6.got
  31.8 0.8 %collective-permute-start.7 = (bf16[216,128]{1,0:T(8,128)(2,1)S(1)}, bf16[216,128]{1,0:T(8,128)(2,1)S(1)}, u32[]{:S(2)}, u32[]{:S(2)}) collective-permute-start(bf16[216,128]{1,0:T(8,128)(2,1)S(1)} %get-tuple-element.40), channel_id=1, source_target_pairs={{0,1},{1,0},{2,3},{3,2},{4,5},{5,4},{6,7},{7,6},{8,9},{9,8},{10,11... | collective-permute-start | bytes 165896 | tf_op jit(solution)/shard_map/ppermute | solution.py:525
  32.6 1.5 %collective-permute-start.8 = (bf16[216,128]{1,0:T(8,128)(2,1)S(1)}, bf16[216,128]{1,0:T(8,128)(2,1)S(1)}, u32[]{:S(2)}, u32[]{:S(2)}) collective-permute-start(bf16[216,128]{1,0:T(8,128)(2,1)S(1)} %get-tuple-element.41), channel_id=1, source_target_pairs={{0,2},{1,3},{2,0},{3,1},{4,6},{5,7},{6,4},{7,5},{8,10},{9,11},{10,... | collective-permute-start | bytes 165896 | tf_op jit(solution)/shard_map/ppermute | solution.py:525
  34.1 4.4 %collective-permute-done.10.got = bf16[864,128]{1,0:T(8,128)(2,1)S(1)} collective-permute-done((bf16[864,128]{1,0:T(8,128)(2,1)S(1)}, bf16[864,128]{1,0:T(8,128)(2,1)S(1)}, u32[]{:S(2)}, u32[]{:S(2)}) %collective-permute-start.10) | collective-permute-done | bytes 221216 | tf_op jit(solution)/shard_map/ppermute | solution.py:519
  38.4 1.6 %collective-permute-start.9 = (bf16[216,128]{1,0:T(8,128)(2,1)S(1)}, bf16[216,128]{1,0:T(8,128)(2,1)S(1)}, u32[]{:S(2)}, u32[]{:S(2)}) collective-permute-start(bf16[216,128]{1,0:T(8,128)(2,1)S(1)} %get-tuple-element.42), channel_id=1, source_target_pairs={{0,3},{1,2},{2,1},{3,0},{4,7},{5,6},{6,5},{7,4},{8,11},{9,10},{10,... | collective-permute-start | bytes 165896 | tf_op jit(solution)/shard_map/ppermute | solution.py:525
  40.1 0.1 shard_map.144
  40.1 0.0 collective-permute-done.4
  40.1 0.1 collective-permute-start.11
  40.2 0.0 collective-permute-done.5
  40.2 2.7 %collective-permute-start.12 = (bf16[216,128]{1,0:T(8,128)(2,1)S(1)}, bf16[216,128]{1,0:T(8,128)(2,1)S(1)}, u32[]{:S(2)}, u32[]{:S(2)}) collective-permute-start(bf16[216,128]{1,0:T(8,128)(2,1)S(1)} %get-tuple-element.47), channel_id=1, source_target_pairs={{0,2},{1,3},{2,0},{3,1},{4,6},{5,7},{6,4},{7,5},{8,10},{9,11},{10,... | collective-permute-start | bytes 165896 | tf_op jit(solution)/shard_map/ppermute | solution.py:525
  43.0 0.0 collective-permute-done.7.first
  43.0 1.6 %collective-permute-start.13 = (bf16[216,128]{1,0:T(8,128)(2,1)S(1)}, bf16[216,128]{1,0:T(8,128)(2,1)S(1)}, u32[]{:S(2)}, u32[]{:S(2)}) collective-permute-start(bf16[216,128]{1,0:T(8,128)(2,1)S(1)} %get-tuple-element.48), channel_id=1, source_target_pairs={{0,3},{1,2},{2,1},{3,0},{4,7},{5,6},{6,5},{7,4},{8,11},{9,10},{10,... | collective-permute-start | bytes 165896 | tf_op jit(solution)/shard_map/ppermute | solution.py:525
  44.6 0.9 %select_bitcast_fusion = (bf16[1,16,64,128]{3,2,1,0:T(8,128)(2,1)}, bf16[1,16,64,128]{3,2,1,0:T(8,128)(2,1)}, bf16[1,16,64,128]{3,2,1,0:T(8,128)(2,1)}) fusion(bf16[16,64,128]{2,1,0:T(8,128)(2,1)S(1)} %collective-permute-done.4, bf16[16,64,128]{2,1,0:T(8,128)(2,1)S(1)} %collective-permute-done.5, pred[]{:T(512)S(6)} %eq.13, pred[]{:T(512)S(6)} %eq.12, pred[]{:T(512)S(6)} %eq.11), kind=kLoop, calls=%fused_computation | loop fusion | flops 393216 | bytes 1310723 | tf_op jit(solution)/shard_map/broadcast_in_dim | solution.py:558
  45.5 0.0 collective-permute-done.8.second
  45.5 0.0 collective-permute-done.9.third
  45.5 0.7 %shard_map.143 = f32[216,128]{1,0:T(8,128)} custom-call(f32[216,128]{1,0:T(8,128)S(1)} %get-tuple-element.39.own, bf16[216,128]{1,0:T(8,128)(2,1)S(1)} %collective-permute-done.7.first, bf16[216,128]{1,0:T(8,128)(2,1)S(1)} %collective-permute-done.8.second, bf16[216,128]{1,0:T(8,128)(2,1)S(1)} %collective-permute-done.9.third), custom_call_target="tpu_custom_call" | custom-call | tf_op jit(solution)/shard_map/pallas_call | solution.py:526
  46.2 0.0 collective-permute-done.11.first
  46.2 1.0 %collective-permute-done.12.second = bf16[216,128]{1,0:T(8,128)(2,1)S(1)} collective-permute-done((bf16[216,128]{1,0:T(8,128)(2,1)S(1)}, bf16[216,128]{1,0:T(8,128)(2,1)S(1)}, u32[]{:S(2)}, u32[]{:S(2)}) %collective-permute-start.12) | collective-permute-done | bytes 55328 | tf_op jit(solution)/shard_map/ppermute | solution.py:525
  47.1 1.8 %collective-permute-done.13.third = bf16[216,128]{1,0:T(8,128)(2,1)S(1)} collective-permute-done((bf16[216,128]{1,0:T(8,128)(2,1)S(1)}, bf16[216,128]{1,0:T(8,128)(2,1)S(1)}, u32[]{:S(2)}, u32[]{:S(2)}) %collective-permute-start.13) | collective-permute-done | bytes 55328 | tf_op jit(solution)/shard_map/ppermute | solution.py:525
  48.9 0.7 %shard_map.145 = f32[216,128]{1,0:T(8,128)} custom-call(f32[216,128]{1,0:T(8,128)S(1)} %get-tuple-element.45.own, bf16[216,128]{1,0:T(8,128)(2,1)S(1)} %collective-permute-done.11.first, bf16[216,128]{1,0:T(8,128)(2,1)S(1)} %collective-permute-done.12.second, bf16[216,128]{1,0:T(8,128)(2,1)S(1)} %collective-permute-done.13.third), custom_call_target="tpu_custom_call" | custom-call | tf_op jit(solution)/shard_map/pallas_call | solution.py:526
  (10 shorter events, 0.1 us)
Async XLA Ops:
  0.6 0.8 %copy-start.7 = (s32[64]{0:T(128)S(1)}, s32[64]{0:T(128)}, u32[]{:S(2)}) copy-start(s32[64]{0:T(128)} %cell.3) | copy-start | bytes 772
  0.6 0.8 %copy-start.6 = (s32[4,16]{1,0:T(4,128)S(1)}, s32[4,16]{1,0:T(4,128)}, u32[]{:S(2)}) copy-start(s32[4,16]{1,0:T(4,128)} %land.3) | copy-start | bytes 772
  0.7 0.8 %copy-start.5 = (bf16[64,128]{1,0:T(8,128)(2,1)S(1)}, bf16[64,128]{1,0:T(8,128)(2,1)}, u32[]{:S(2)}) copy-start(bf16[64,128]{1,0:T(8,128)(2,1)} %coarse.3) | copy-start | bytes 49156
  1.4 1.0 %copy-start = (bf16[1,16,64,128]{3,2,1,0:T(8,128)(2,1)S(1)}, bf16[1,16,64,128]{3,2,1,0:T(8,128)(2,1)}, u32[]{:S(2)}) copy-start(bf16[1,16,64,128]{3,2,1,0:T(8,128)(2,1)} %act.1) | copy-start | bytes 786436
  2.4 0.9 %copy-start.1 = (bf16[1,16,64,128]{3,2,1,0:T(8,128)(2,1)S(1)}, bf16[1,16,64,128]{3,2,1,0:T(8,128)(2,1)}, u32[]{:S(2)}) copy-start(bf16[1,16,64,128]{3,2,1,0:T(8,128)(2,1)} %par.1) | copy-start | bytes 786436
  3.3 0.9 %copy-start.2 = (bf16[1,16,64,128]{3,2,1,0:T(8,128)(2,1)S(1)}, bf16[1,16,64,128]{3,2,1,0:T(8,128)(2,1)}, u32[]{:S(2)}) copy-start(bf16[1,16,64,128]{3,2,1,0:T(8,128)(2,1)} %st.1) | copy-start | bytes 786436
  4.3 0.9 %copy-start.3 = (bf16[1,16,64,128]{3,2,1,0:T(8,128)(2,1)S(1)}, bf16[1,16,64,128]{3,2,1,0:T(8,128)(2,1)}, u32[]{:S(2)}) copy-start(bf16[1,16,64,128]{3,2,1,0:T(8,128)(2,1)} %gr.1) | copy-start | bytes 786436
  6.4 10.2 %collective-permute-start = (bf16[25,8,128]{2,1,0:T(8,128)(2,1)S(1)}, bf16[25,8,128]{2,1,0:T(8,128)(2,1)S(1)}, u32[]{:S(2)}, u32[]{:S(2)}) collective-permute-start(bf16[25,8,128]{2,1,0:T(8,128)(2,1)S(1)} %get-tuple-element.27), channel_id=1, source_target_pairs={{0,1},{2,3},{1,0},{3,2},{4,5},{6,7},{5,4},{7,6},{8,9},{10,11},{9,8... | collective-permute-start | bytes 153608 | tf_op jit(solution)/shard_map/ppermute | solution.py:461
  9.5 10.3 %copy-start.8 = (bf16[1,3,3,128,192]{3,4,2,1,0:T(8,128)(2,1)S(1)}, bf16[1,3,3,128,192]{3,4,2,1,0:T(8,128)(2,1)}, u32[]{:S(2)}) copy-start(bf16[1,3,3,128,192]{3,4,2,1,0:T(8,128)(2,1)} %param.14) | copy-start | bytes 1327108
  9.5 7.1 %collective-permute-start.1 = (bf16[25,8,128]{2,1,0:T(8,128)(2,1)S(1)}, bf16[25,8,128]{2,1,0:T(8,128)(2,1)S(1)}, u32[]{:S(2)}, u32[]{:S(2)}) collective-permute-start(bf16[25,8,128]{2,1,0:T(8,128)(2,1)S(1)} %get-tuple-element.28), channel_id=1, source_target_pairs={{0,3},{1,2},{2,1},{3,0},{4,7},{5,6},{6,5},{7,4},{8,11},{9,10},{10,... | collective-permute-start | bytes 153608 | tf_op jit(solution)/shard_map/ppermute | solution.py:462
  12.0 4.6 %collective-permute-start.2 = (bf16[64,128]{1,0:T(8,128)(2,1)S(1)}, bf16[64,128]{1,0:T(8,128)(2,1)S(1)}, u32[]{:S(2)}, u32[]{:S(2)}) collective-permute-start(bf16[64,128]{1,0:T(8,128)(2,1)S(1)} %copy-done.5), channel_id=1, source_target_pairs={{0,2},{1,3},{2,0},{3,1},{4,6},{5,7},{6,4},{7,5},{8,10},{9,11},{10,... | collective-permute-start | bytes 49160 | tf_op jit(solution)/shard_map/ppermute | solution.py:464
  18.3 5.2 %copy-start.4 = (bf16[1,3,3,192,128]{4,3,2,1,0:T(8,128)(2,1)S(1)}, bf16[1,3,3,192,128]{4,3,2,1,0:T(8,128)(2,1)}, u32[]{:S(2)}) copy-start(bf16[1,3,3,192,128]{4,3,2,1,0:T(8,128)(2,1)} %param.15) | copy-start | bytes 1327108
  18.3 5.2 %collective-permute-start.3 = (bf16[7,80,128]{2,1,0:T(8,128)(2,1)S(1)}, bf16[7,80,128]{2,1,0:T(8,128)(2,1)S(1)}, u32[]{:S(2)}, u32[]{:S(2)}) collective-permute-start(bf16[7,80,128]{2,1,0:T(8,128)(2,1)S(1)} %get-tuple-element.30), channel_id=1, source_target_pairs={{0,4},{4,0},{1,5},{5,1},{2,6},{6,2},{3,7},{7,3},{8,12},{12,8},{9,1... | collective-permute-start | bytes 430088 | tf_op jit(solution)/shard_map/ppermute | solution.py:479
  25.6 6.1 %collective-permute-start.6 = (bf16[864,128]{1,0:T(8,128)(2,1)S(1)}, bf16[864,128]{1,0:T(8,128)(2,1)S(1)}, u32[]{:S(2)}, u32[]{:S(2)}) collective-permute-start(bf16[864,128]{1,0:T(8,128)(2,1)S(1)} %get-tuple-element.37), channel_id=1, source_target_pairs={{0,4},{4,0},{1,5},{5,1},{2,6},{6,2},{3,7},{7,3},{8,12},{12,8},{9,1... | collective-permute-start | bytes 663560 | tf_op jit(solution)/shard_map/ppermute | solution.py:519
  29.4 10.7 %collective-permute-start.4 = (bf16[16,64,128]{2,1,0:T(8,128)(2,1)S(1)}, bf16[16,64,128]{2,1,0:T(8,128)(2,1)S(1)}, u32[]{:S(2)}, u32[]{:S(2)}) collective-permute-start(bf16[16,64,128]{2,1,0:T(8,128)(2,1)S(1)} %get-tuple-element.33), channel_id=1, source_target_pairs={{0,8},{8,16},{16,24},{24,0},{1,9},{9,17},{17,25},{25,1},{2,10},{10... | collective-permute-start | bytes 786440 | tf_op jit(solution)/shard_map/ppermute | solution.py:552
  29.5 10.7 %collective-permute-start.5 = (bf16[16,64,128]{2,1,0:T(8,128)(2,1)S(1)}, bf16[16,64,128]{2,1,0:T(8,128)(2,1)S(1)}, u32[]{:S(2)}, u32[]{:S(2)}) collective-permute-start(bf16[16,64,128]{2,1,0:T(8,128)(2,1)S(1)} %get-tuple-element.34), channel_id=1, source_target_pairs={{8,0},{16,8},{24,16},{0,24},{9,1},{17,9},{25,17},{1,25},{10,2},{18... | collective-permute-start | bytes 786440 | tf_op jit(solution)/shard_map/ppermute | solution.py:553
  31.2 7.2 %collective-permute-start.10 = (bf16[864,128]{1,0:T(8,128)(2,1)S(1)}, bf16[864,128]{1,0:T(8,128)(2,1)S(1)}, u32[]{:S(2)}, u32[]{:S(2)}) collective-permute-start(bf16[864,128]{1,0:T(8,128)(2,1)S(1)} %get-tuple-element.43), channel_id=1, source_target_pairs={{0,4},{4,0},{1,5},{5,1},{2,6},{6,2},{3,7},{7,3},{8,12},{12,8},{9,1... | collective-permute-start | bytes 663560 | tf_op jit(solution)/shard_map/ppermute | solution.py:519
  31.8 11.2 %collective-permute-start.7 = (bf16[216,128]{1,0:T(8,128)(2,1)S(1)}, bf16[216,128]{1,0:T(8,128)(2,1)S(1)}, u32[]{:S(2)}, u32[]{:S(2)}) collective-permute-start(bf16[216,128]{1,0:T(8,128)(2,1)S(1)} %get-tuple-element.40), channel_id=1, source_target_pairs={{0,1},{1,0},{2,3},{3,2},{4,5},{5,4},{6,7},{7,6},{8,9},{9,8},{10,11... | collective-permute-start | bytes 165896 | tf_op jit(solution)/shard_map/ppermute | solution.py:525
  32.6 12.9 %collective-permute-start.8 = (bf16[216,128]{1,0:T(8,128)(2,1)S(1)}, bf16[216,128]{1,0:T(8,128)(2,1)S(1)}, u32[]{:S(2)}, u32[]{:S(2)}) collective-permute-start(bf16[216,128]{1,0:T(8,128)(2,1)S(1)} %get-tuple-element.41), channel_id=1, source_target_pairs={{0,2},{1,3},{2,0},{3,1},{4,6},{5,7},{6,4},{7,5},{8,10},{9,11},{10,... | collective-permute-start | bytes 165896 | tf_op jit(solution)/shard_map/ppermute | solution.py:525
  38.4 7.1 %collective-permute-start.9 = (bf16[216,128]{1,0:T(8,128)(2,1)S(1)}, bf16[216,128]{1,0:T(8,128)(2,1)S(1)}, u32[]{:S(2)}, u32[]{:S(2)}) collective-permute-start(bf16[216,128]{1,0:T(8,128)(2,1)S(1)} %get-tuple-element.42), channel_id=1, source_target_pairs={{0,3},{1,2},{2,1},{3,0},{4,7},{5,6},{6,5},{7,4},{8,11},{9,10},{10,... | collective-permute-start | bytes 165896 | tf_op jit(solution)/shard_map/ppermute | solution.py:525
  40.1 6.1 %collective-permute-start.11 = (bf16[216,128]{1,0:T(8,128)(2,1)S(1)}, bf16[216,128]{1,0:T(8,128)(2,1)S(1)}, u32[]{:S(2)}, u32[]{:S(2)}) collective-permute-start(bf16[216,128]{1,0:T(8,128)(2,1)S(1)} %get-tuple-element.46), channel_id=1, source_target_pairs={{0,1},{1,0},{2,3},{3,2},{4,5},{5,4},{6,7},{7,6},{8,9},{9,8},{10,11... | collective-permute-start | bytes 165896 | tf_op jit(solution)/shard_map/ppermute | solution.py:525
  40.2 6.9 %collective-permute-start.12 = (bf16[216,128]{1,0:T(8,128)(2,1)S(1)}, bf16[216,128]{1,0:T(8,128)(2,1)S(1)}, u32[]{:S(2)}, u32[]{:S(2)}) collective-permute-start(bf16[216,128]{1,0:T(8,128)(2,1)S(1)} %get-tuple-element.47), channel_id=1, source_target_pairs={{0,2},{1,3},{2,0},{3,1},{4,6},{5,7},{6,4},{7,5},{8,10},{9,11},{10,... | collective-permute-start | bytes 165896 | tf_op jit(solution)/shard_map/ppermute | solution.py:525
  43.0 6.0 %collective-permute-start.13 = (bf16[216,128]{1,0:T(8,128)(2,1)S(1)}, bf16[216,128]{1,0:T(8,128)(2,1)S(1)}, u32[]{:S(2)}, u32[]{:S(2)}) collective-permute-start(bf16[216,128]{1,0:T(8,128)(2,1)S(1)} %get-tuple-element.48), channel_id=1, source_target_pairs={{0,3},{1,2},{2,1},{3,0},{4,7},{5,6},{6,5},{7,4},{8,11},{9,10},{10,... | collective-permute-start | bytes 165896 | tf_op jit(solution)/shard_map/ppermute | solution.py:525

commit v2 on v1

v2 whole, which is shorter than its diff:
```python
import functools
import math

import jax
import jax.numpy as jnp
from jax import lax
from jax.experimental import pallas as pl
from jax.experimental.pallas import tpu as pltpu
from jax.sharding import PartitionSpec as P

F32 = jnp.float32
BF16 = jnp.bfloat16
VMEM = pl.BlockSpec(memory_space=pltpu.VMEM)
SMEM = pl.BlockSpec(memory_space=pltpu.SMEM)
HBM = pl.BlockSpec(memory_space=pltpu.HBM)
LEFT = 8
PAD = 48
STRIP_ROWS = 7


def call(body, out_shape, in_specs, scratch=(), flops=0, moved=0, limit=48):
    out_specs = jax.tree.map(lambda _: VMEM, out_shape)
    return pl.pallas_call(
        body,
        out_shape=out_shape,
        in_specs=in_specs,
        out_specs=out_specs,
        scratch_shapes=list(scratch),
        compiler_params=pltpu.CompilerParams(vmem_limit_bytes=limit * 1024 * 1024),
        cost_estimate=pl.CostEstimate(flops=flops, bytes_accessed=moved, transcendentals=0),
    )


def in_hbm(*operands):
    return [pltpu.with_memory_space_constraint(x, pltpu.HBM) for x in operands]


def sublane(shape):
    return lax.broadcasted_iota(jnp.int32, shape, len(shape) - 2)


def flag(condition):
    return jnp.where(condition, 1.0, 0.0).astype(F32)


def traits():
    segments = lax.axis_size("segment")
    position = lax.axis_index("segment")
    decoder = flag(position >= segments // 2)
    return decoder, 1.0 - decoder, position == segments - 1


def edge_kernel(owner_in, cell_in, land_in, act, par, st, gr, coarse, grad_out, pay0, pay1, *scratch):
    act_l, act_r, st_l, st_r, par_v, gr_v, plane, held_v, owner, cell, land, arrived = scratch
    rows, breadth = gr.shape[1], gr.shape[2]
    first, final = pl.ds(0, 16), pl.ds(breadth - 16, 16)
    copies = [
        pltpu.make_async_copy(source, target, arrived.at[k])
        for k, (source, target) in enumerate(
            (
                (gr.at[0], gr_v),
                (par.at[0], par_v),
                (act.at[0, :, first], act_l),
                (act.at[0, :, final], act_r),
                (st.at[0, :, first], st_l),
                (st.at[0, :, final], st_r),
                (coarse, held_v),
                (owner_in, owner),
                (cell_in, cell),
                (land_in, land),
            )
        )
    ]
    for copy in copies:
        copy.start()
    for copy in copies[7:]:
        copy.wait()
    decoder, encoder, last = traits()
    groups = rows // 4
    per_row = breadth // 4
    low = sublane((8, 128)) < 4
    for group in range(groups):
        for part in range(breadth // 8):
            weigh = [jnp.where(last, land[group, 2 * part + k], 1).astype(F32) for k in range(2)]
            plane[group, 8 * part : 8 * part + 8] = jnp.where(low, weigh[0], weigh[1])

    def ids(column):
        tile = jnp.zeros((8, 128), F32)
        where = sublane((8, 128))
        for row in range(groups):
            spot = row * per_row + column
            tile = jnp.where(where == row, owner[spot].astype(F32), tile)
            tile = jnp.where(where == 4 + row, cell[spot].astype(F32), tile)
        return tile

    left_ids, right_ids = ids(0), ids(per_row - 1)
    for copy in copies[:7]:
        copy.wait()
    for row in range(rows):
        grad = gr_v[row].astype(F32) + encoder * par_v[row].astype(F32)
        grad_out[row] = (grad * plane[row // 4]).astype(BF16)

    where = sublane((rows, 8, 128))
    begin, end = slice(0, 16), slice(breadth - 16, breadth)
    grad = grad_out[:, begin].astype(F32)[:, 0:8]
    stash = st_l[...].astype(F32)[:, 0:8]
    block = act_l[...].astype(F32)[:, 0:8] + decoder * par_v[:, begin].astype(F32)[:, 0:8]
    after = jnp.where(
        where < 3, grad, jnp.where(where < 5, pltpu.roll(stash, 3, 1), pltpu.roll(block, 5, 1))
    )
    grad = grad_out[:, end].astype(F32)[:, 8:16]
    stash = st_r[...].astype(F32)[:, 8:16]
    block = act_r[...].astype(F32)[:, 8:16] + decoder * par_v[:, end].astype(F32)[:, 8:16]
    before = jnp.where(
        where == 7, grad, jnp.where(where == 6, pltpu.roll(stash, 7, 1), pltpu.roll(block, 6, 1))
    )
    even = lax.axis_index("ty") % 2 == 0
    strips = jnp.where(even, before, after).astype(BF16), jnp.where(even, after, before).astype(BF16)
    named = jnp.where(even, right_ids, left_ids), jnp.where(even, left_ids, right_ids)
    held = held_v[...].reshape(coarse.shape[0] // 8, 8, 128)
    for k, pay in enumerate((pay0, pay1)):
        pay[0:rows] = strips[k]
        pay[rows] = named[k].astype(BF16)
        pay[rows + 1 :] = held


def prepare_kernel(act, par, st, up, down, base, stash, flat_up, flat_down, *scratch):
    act_v, par_v, up_v, down_v, arrived = scratch
    pairs = (act.at[0], act_v), (par.at[0], par_v), (up, up_v), (down, down_v), (st.at[0], stash)
    copies = [pltpu.make_async_copy(*pair, arrived.at[k]) for k, pair in enumerate(pairs)]
    for copy in copies:
        copy.start()
    decoder, _, _ = traits()
    for copy in copies:
        copy.wait()
    for row in range(act_v.shape[0]):
        base[row] = act_v[row].astype(F32) + decoder * par_v[row].astype(F32)
    lane_taps(up_v, flat_up)
    lane_taps(down_v, flat_down)


def side_rims(z0, z1, rows):
    ty = lax.axis_index("ty")
    even = ty % 2 == 0
    first, second = z0[0:rows].astype(F32), z1[0:rows].astype(F32)
    before = jnp.where(ty > 0, jnp.where(even, second, first), 0.0)
    after = jnp.where(ty < lax.axis_size("ty") - 1, jnp.where(even, first, second), 0.0)
    return before, after


def rim_kernel(z0, z1, _weights, _stash, rim):
    before, after = side_rims(z0, z1, rim.shape[0])
    rim[...] = jnp.where(sublane(rim.shape) < 5, after, before).astype(BF16)


def condition_kernel(merged, owner, cell, base, z0, z1, coarse, *rest):
    rows, breadth = base.shape[0], base.shape[1]
    groups = rows // 4
    per_row = breadth // 4
    cells = groups * per_row
    wide = LEFT + breadth
    ty = lax.axis_index("ty")
    low = sublane((8, 128)) < 4
    if merged:
        z2, pay, ext, table, plane = rest
        table[pl.ds(pl.multiple_of(ty * cells, 8), cells)] = coarse[...].astype(F32)
        others = (
            (ty ^ 1, z0[rows + 1 :].astype(F32).reshape(cells, 128)),
            (ty ^ 3, z1[rows + 1 :].astype(F32).reshape(cells, 128)),
            (ty ^ 2, z2[...].astype(F32)),
        )
        for other, value in others:
            table[pl.ds(pl.multiple_of(other * cells, 8), cells)] = value
    else:
        st, grad_own, pay, pay1, full, table, plane = rest
        ext = full.at[2]
        table[...] = coarse[...].astype(F32)
    before, after = side_rims(z0, z1, rows + 1)

    def rim_condition(tile, valid):
        wanted = tile[rows]
        spot = wanted * cells + pltpu.roll(wanted, 4, 0)
        lanes = lax.broadcasted_iota(jnp.int32, (8, table.shape[0]), 1).astype(F32)
        spread = jnp.broadcast_to(spot[:, 0:1], lanes.shape)
        hot = jnp.where(spread == lanes, 1.0, 0.0).astype(BF16)
        named = lax.dot(hot, table[...].astype(BF16), preferred_element_type=F32)
        picked = [jnp.broadcast_to(named[row : row + 1], (8, 128))[None] for row in range(groups)]
        spread_rows = jnp.concatenate([p for p in picked for _ in range(4)], axis=0)
        return jnp.where(valid, spread_rows, 0.0)

    rim = pltpu.roll(before[0:rows], 2, 1) + rim_condition(before, ty > 0)
    ext[:, 0:8] = rim.astype(BF16)
    rim = pltpu.roll(after[0:rows], 3, 1) + rim_condition(after, ty < lax.axis_size("ty") - 1)
    ext[:, wide : wide + 8] = rim.astype(BF16)
    for group in range(groups):
        for part in range(breadth // 8):
            spots = [group * per_row + 2 * part + k for k in range(2)]
            named = [
                jnp.broadcast_to(table[pl.ds(owner[s] * cells + cell[s], 1)], (8, 128)) for s in spots
            ]
            plane[group, 8 * part : 8 * part + 8] = jnp.where(low, named[0], named[1])
    for row in range(rows):
        ext[row, LEFT:wide] = (base[row] + plane[row // 4]).astype(BF16)

    upper = lax.axis_index("tx") % 2 == 0
    if merged:
        near = sublane((8, 128)) < 5
        for k in range(3):
            top, bottom = min(k, 1), rows - 3 + k
            for part in range(breadth // 8):
                cols = pl.ds(LEFT + 8 * part, 8)
                pay[9 * k + part] = jnp.where(upper, ext[bottom, cols], ext[top, cols])
            tiles = [
                jnp.where(near, ext[row, pl.ds(wide, 8)], ext[row, pl.ds(0, 8)]) for row in (top, bottom)
            ]
            pay[9 * k + breadth // 8] = jnp.where(upper, tiles[1], tiles[0])
        return
    full[0, :, 0:8] = before[0:rows].astype(BF16)
    full[1, :, 0:8] = pltpu.roll(before[0:rows], 1, 1).astype(BF16)
    full[0, :, wide : wide + 8] = after[0:rows].astype(BF16)
    full[1, :, wide : wide + 8] = pltpu.roll(after[0:rows], 5, 1).astype(BF16)
    full[0, :, LEFT:wide] = grad_own[...]
    full[1, :, LEFT:wide] = st[...]
    leading = [(0, 0), (0, 1), (0, 2), (1, 0), (1, 1), (2, 0), (2, 1)]
    closing = [(0, rows - 1), (1, rows - 1), (2, rows - 3), (2, rows - 2), (2, rows - 1)]
    closing = closing + closing[-1:] * 2
    for k in range(STRIP_ROWS):
        top, bottom = full[leading[k]], full[closing[k]]
        pay[k] = jnp.where(upper, bottom, top)
        pay1[k] = jnp.where(upper, top, bottom)


def rims(y0, y1):
    tx = lax.axis_index("tx")
    upper = tx % 2 == 0
    before_ok, after_ok = tx > 0, tx < lax.axis_size("tx") - 1

    def row(valid, from_first, k):
        value = jnp.where(from_first, y0[k].astype(F32), y1[k].astype(F32))
        return jnp.where(valid, value, 0.0)

    before = lambda k: row(before_ok, jnp.logical_not(upper), k)
    after = lambda k: row(after_ok, upper, k)
    return before, after


def spread_taps(field, taps, odd_taps, count, first):
    for row in range(count):
        target = taps if row % 2 == 0 else odd_taps
        for tap in range(3):
            value = field[row, pl.ds(first + tap, PAD, stride=2), :]
            target[row // 2, :, tap * 128 : tap * 128 + 128] = value.astype(BF16)


def three_rows(even_taps, odd_taps, count):
    wide = 3 * 128
    whole = lambda ref, a: ref[a : a + count].reshape(count * PAD, wide)
    return whole(even_taps, 0), whole(odd_taps, 0), whole(even_taps, 1)


def lower(even_taps, odd_taps, count, down):
    views = three_rows(even_taps, odd_taps, count)
    wide = 3 * 128
    total = None
    for a in range(3):
        term = lax.dot_general(
            views[a],
            down[:, a * wide : a * wide + wide],
            (((1,), (1,)), ((), ())),
            preferred_element_type=F32,
        )
        total = term if total is None else total + term
    return total


def lane_taps(taps, flat):
    for tap in range(9):
        flat[:, tap * 128 : tap * 128 + 128] = taps[tap]


def sweep(wide, field, even_taps, odd_taps, sums, flat_up, down, count, fill_stash, fill_grad):
    field[:, wide:] = jnp.zeros((field.shape[0], field.shape[1] - wide, 128), F32)
    fill_stash()
    spread_taps(field, even_taps, odd_taps, 2 * count + 1, LEFT - 1)
    pre_back = lower(even_taps, odd_taps, count, down)
    logistic = 1.0 / (1.0 + jnp.exp(-pre_back))
    reduced = pre_back * logistic
    slope = logistic * (1.0 + pre_back * (1.0 - logistic))
    fill_grad()
    previous = None
    for row in range(2 * count + 2):
        plane = [field[row, pl.ds(LEFT - 1 + k, PAD, stride=2), :] for k in range(4)]
        current = [plane[2] + plane[3], plane[1] + plane[2], plane[0] + plane[1]]
        if row > 0:
            for a in range(3):
                double = row - 3 + a
                if double % 2 == 0 and 0 <= double // 2 < count:
                    for b in range(3):
                        lanes = slice((3 * a + b) * 128, (3 * a + b) * 128 + 128)
                        sums[double // 2, :, lanes] = (previous[b] + current[b]).astype(BF16)
        previous = current
    windows = sums[...].reshape(count * PAD, 9 * 128)
    raised = lax.dot_general(windows, flat_up[...], (((1,), (1,)), ((), ())), preferred_element_type=F32)
    return reduced.astype(BF16), raised * slope


def places(count, depth):
    shape = (count, PAD, depth)
    row = lax.broadcasted_iota(jnp.int32, shape, 0).reshape(count * PAD, depth)
    col = lax.broadcasted_iota(jnp.int32, shape, 1).reshape(count * PAD, depth)
    return row, col


def flatten_rows(d0, d1, flat, start):
    pairs = d0.shape[0] // 2
    left_even, left_odd = d0[pl.ds(0, pairs, stride=2)], d0[pl.ds(1, pairs, stride=2)]
    right_even, right_odd = d1[pl.ds(0, pairs, stride=2)], d1[pl.ds(1, pairs, stride=2)]
    near = lax.broadcasted_iota(jnp.int32, left_even.shape, 1) < 64
    turned = pltpu.roll(left_odd, 64, 1)
    flat[pl.ds(start, pairs, stride=3)] = left_even
    flat[pl.ds(start + 1, pairs, stride=3)] = jnp.where(near, right_even, turned)
    flat[pl.ds(start + 2, pairs, stride=3)] = jnp.where(near, turned, pltpu.roll(right_odd, 64, 1))


def across(left, right):
    return lax.dot_general(left, right, (((0,), (0,)), ((), ())), preferred_element_type=F32)


def grads_kernel(
    ext, y0, y1, flat_up, flat_down, in_grad, up_flat, down_flat, field, even_taps, odd_taps, sums, d0, d1, products, fine
):
    rows = ext.shape[1]
    wide = ext.shape[2]
    half_rows, half_cols = rows // 2, (wide - 16) // 2
    count = half_rows + 1
    before, after = rims(y0, y1)
    tx, ty = lax.axis_index("tx"), lax.axis_index("ty")
    has_below, has_right = tx < lax.axis_size("tx") - 1, ty < lax.axis_size("ty") - 1

    def fill(kind, top, bottom):
        field[0, 0:wide] = before(top)
        for row in range(rows):
            field[row + 1, 0:wide] = ext[kind, row].astype(F32)
        for k, spot in enumerate(bottom):
            field[rows + 1 + k, 0:wide] = after(spot)

    reduced, pre_grad = sweep(
        wide,
        field,
        even_taps,
        odd_taps,
        sums,
        flat_up,
        flat_down,
        count,
        lambda: fill(1, 1, (3, 4)),
        lambda: fill(0, 0, (0, 1, 2)),
    )
    depth = reduced.shape[1]
    row, col = places(count, depth)
    inside = ((row < half_rows) | has_below) & ((col < half_cols) | (has_right & (col == half_cols)))
    pre_grad = jnp.where(inside, pre_grad, 0.0).astype(BF16).reshape(count, PAD, depth)
    base = lambda row_id: ext[0, row_id, LEFT : wide - 8]
    input_grad(pre_grad, flat_down, base, products, fine, in_grad)
    cells = half_rows * half_cols
    own = lambda value: value[:half_rows, :half_cols].reshape(cells, value.shape[-1])
    reduced, own_grad = own(reduced.reshape(count, PAD, depth)), own(pre_grad)
    terms = across(reduced, own(sums))
    for tap in range(9):
        up_flat[tap * depth : tap * depth + depth] = terms[:, tap * 128 : tap * 128 + 128]
    span = 3 * 128
    for a, view in enumerate((even_taps, odd_taps, even_taps)):
        taps = view[a // 2 : a // 2 + half_rows, 0:half_cols].reshape(cells, span)
        term = across(taps, own_grad)
        d0[a * span : a * span + span] = term[:, 0:128]
        d1[a * span : a * span + span, 0:64] = term[:, 128:192]
    flatten_rows(d0, d1, down_flat, 0)


def paired_kernel(
    st, grad, st_far, grad_far, rim, rim_far, flat_up, flat_down, in_grad, own_sum, send1, send2, send3, *scratch
):
    field, even_taps, odd_taps, sums, d0, d1, up_flat, down_flat, grads, products, fine = scratch
    rows, breadth = grad.shape[0], grad.shape[1]
    wide = breadth + 16
    count, half_cols = rows, breadth // 2
    tx, ty = lax.axis_index("tx"), lax.axis_index("ty")
    has_right = ty < lax.axis_size("ty") - 1

    def fill(here_rows, there_rows, turn_before, turn_after):
        blank = jnp.zeros((wide, 128), F32)
        field[0, 0:wide] = blank
        field[2 * rows + 1, 0:wide] = blank
        here, there = 1 + rows * tx, 1 + rows * (1 - tx)
        for start, source, sides in ((here, here_rows, rim), (there, there_rows, rim_far)):
            for row in range(rows):
                field[start + row, LEFT : LEFT + breadth] = source(row).astype(F32)
            sides = sides[...].astype(F32)
            turned = lambda turn: pltpu.roll(sides, turn, 1) if turn else sides
            field[pl.ds(start, rows), 0:8] = turned(turn_before)
            field[pl.ds(start, rows), LEFT + breadth : wide] = turned(turn_after)

    reduced, pre_grad = sweep(
        wide,
        field,
        even_taps,
        odd_taps,
        sums,
        flat_up,
        flat_down,
        count,
        lambda: fill(lambda row: st[row], lambda row: st_far[0, row], 1, 5),
        lambda: fill(lambda row: grad[row], lambda row: grad_far[row], 0, 0),
    )
    depth = reduced.shape[1]
    _, col = places(count, depth)
    inside = (col < half_cols) | (has_right & (col == half_cols))
    pre_grad = jnp.where(inside, pre_grad, 0.0).astype(BF16).reshape(count, PAD, depth)
    grads[0:count] = pre_grad
    grads[count] = jnp.zeros((PAD, depth), BF16)
    base = lambda row: grad[row]
    input_grad(grads[pl.ds(rows // 2 * tx, rows // 2 + 1)], flat_down, base, products, fine, in_grad)
    cells = count * half_cols
    own = lambda value: value[:, :half_cols].reshape(cells, value.shape[-1])
    reduced, own_grad = own(reduced.reshape(count, PAD, depth)), own(pre_grad)
    half = up_flat.shape[0] - depth // 2
    lanes = pl.ds(pl.multiple_of(tx * 512, 128), 640)
    terms = across(reduced, sums[:, 0:half_cols, lanes].reshape(cells, 640))
    for tap in range(5):
        up_flat[tap * depth : tap * depth + depth] = terms[:, tap * 128 : tap * 128 + 128]
    span = 3 * 128
    outer = across(even_taps[pl.ds(tx, count), 0:half_cols].reshape(cells, span), own_grad)
    middle = across(odd_taps[0:count, 0:half_cols].reshape(cells, span), own_grad)
    outer_at = pl.multiple_of(tx * (span // 2), 8)
    middle_at = pl.multiple_of((1 - tx) * span, 8)
    middle_half = jnp.where(tx == 0, middle[0 : span // 2], middle[span // 2 : span])
    d0[pl.ds(outer_at, span)] = outer[:, 0:128]
    d1[pl.ds(outer_at, span), 0:64] = outer[:, 128:192]
    d0[pl.ds(middle_at, span // 2)] = middle_half[:, 0:128]
    d1[pl.ds(middle_at, span // 2), 0:64] = middle_half[:, 128:192]
    flatten_rows(d0, d1, down_flat, 0)
    piece = half // 4
    up_start = tx * (depth // 2)
    for distance, target in enumerate((own_sum, send1, send2, send3)):
        place = (ty ^ distance) * piece
        both = [
            up_flat[pl.ds(pl.multiple_of(up_start + place, 8), piece)],
            down_flat[pl.ds(pl.multiple_of(place, 8), piece)],
        ]
        target[...] = jnp.concatenate(both, axis=0).astype(target.dtype)


def input_grad(grads, down, base, products, fine, target):
    half_rows, half_cols = fine.shape[0] // 2, fine.shape[1] // 2
    count = half_rows + 1
    flat = grads.reshape(count * PAD, grads.shape[2])
    moved = lax.dot(flat, down[...], preferred_element_type=F32)
    products[...] = moved.reshape(count, PAD, 9 * 128)

    def part(p, a, b, offset):
        tap = 3 * a + b
        return products[p, offset : offset + half_cols, tap * 128 : tap * 128 + 128]

    for p in range(half_rows):
        fine[2 * p, pl.ds(0, half_cols, stride=2), :] = part(p, 1, 1, 0)
        fine[2 * p, pl.ds(1, half_cols, stride=2), :] = part(p, 1, 2, 0) + part(p, 1, 0, 1)
        fine[2 * p + 1, pl.ds(0, half_cols, stride=2), :] = part(p, 2, 1, 0) + part(p + 1, 0, 1, 0)
        fine[2 * p + 1, pl.ds(1, half_cols, stride=2), :] = (
            part(p, 2, 2, 0) + part(p, 2, 0, 1) + part(p + 1, 0, 2, 0) + part(p + 1, 0, 0, 1)
        )
    for row in range(fine.shape[0]):
        target[row] = (base(row).astype(F32) + fine[row]).astype(BF16)


def forward_kernel(merged, blocks, *rest):
    ys, rest = (rest[:1], rest[1:]) if merged else (rest[:2], rest[2:])
    in_grad, flat_up, flat_down, near, far, field, even_taps, odd_taps, products, mixed, fine = rest
    ext = blocks if merged else blocks.at[2]
    rows, wide = ext.shape[0], ext.shape[1]
    breadth = wide - 16
    half_rows, half_cols = rows // 2, breadth // 2
    depth = flat_down.shape[0]
    tx, ty = lax.axis_index("tx"), lax.axis_index("ty")
    has_above, has_below = tx > 0, tx < lax.axis_size("tx") - 1
    has_right = ty < lax.axis_size("ty") - 1
    position = lax.axis_index("segment")
    count = half_rows + 2
    field[:, wide:] = jnp.zeros((field.shape[0], field.shape[1] - wide, 128), F32)
    if merged:
        def row_of(k, valid):
            tiles = [ys[0][9 * k + part].astype(F32) for part in range(breadth // 8 + 1)]
            line = jnp.concatenate([tiles[-1]] + tiles, axis=0)
            return jnp.where(valid, line, 0.0)

        before, after = (lambda k: row_of(k, has_above)), (lambda k: row_of(k, has_below))
        top, bottom = 0, 0
    else:
        before, after = rims(*ys)
        top, bottom = 2, 5
    for k in range(3):
        field[k, 0:wide] = before(top + k)
    for row in range(rows):
        field[row + 3, 0:wide] = ext[row].astype(F32)
    for k in range(2):
        field[rows + 3 + k, 0:wide] = after(bottom + k)
    spread_taps(field, even_taps, odd_taps, 2 * count + 1, LEFT - 3)
    pre_down = lower(even_taps, odd_taps, count, flat_down)
    reduced = pre_down / (1.0 + jnp.exp(-pre_down))
    row_id, col_id = places(count, depth)
    inside = ((row_id <= half_rows) | has_below) & ((col_id <= half_cols) | has_right)
    reduced = jnp.where(inside, reduced, 0.0).astype(BF16)
    raised = lax.dot(reduced, flat_up[...], preferred_element_type=F32)
    products[...] = raised.reshape(count, PAD, 9 * 128)

    def tap_rows(p, dy, b):
        at = lambda q, a: products[q, :, (3 * a + b) * 128 : (3 * a + b) * 128 + 128]
        if dy == 0:
            return at(p, 0) + at(p + 1, 1) + at(p + 1, 2)
        return at(p + 1, 0) + at(p + 1, 1) + at(p + 2, 2)

    for p in range(half_rows):
        for dy in range(2):
            col = [tap_rows(p, dy, b) for b in range(3)]
            mixed[0, 0:PAD], mixed[1, 0:PAD] = col[0], col[1] + col[2]
            mixed[2, 0:PAD], mixed[3, 0:PAD] = col[0] + col[1], col[2]
            line = 2 * p + dy
            fine[line, pl.ds(0, half_cols, stride=2), :] = mixed[0, 0:half_cols] + mixed[1, 1 : half_cols + 1]
            fine[line, pl.ds(1, half_cols, stride=2), :] = (
                mixed[2, 1 : half_cols + 1] + mixed[3, 2 : half_cols + 2]
            )
    for row in range(rows):
        value = (ext[row, LEFT : LEFT + breadth].astype(F32) + fine[row]).astype(BF16)
        near[row] = jnp.where(position % 2 == 0, value, in_grad[row])
        far[row] = jnp.where(position < lax.axis_size("segment") // 2, value, in_grad[row])


def swaps(axis):
    size = lax.axis_size(axis)
    pairs = [(i, i + 1) for i in range(0, size - 1, 2)]
    other = [(i, i + 1) for i in range(1, size - 1, 2)]
    both = lambda pairs: pairs + [(j, i) for i, j in pairs]
    return both(pairs), both(other)


def crossed(axis, distance):
    return [(i, i ^ distance) for i in range(lax.axis_size(axis))]


def total_kernel(scaling, own, first, second, third, up_sum, down_sum):
    total = own[...] + first[...].astype(F32) + second[...].astype(F32) + third[...].astype(F32)
    piece = up_sum.shape[0]
    up_sum[...] = total[0:piece] * scaling
    down_sum[...] = total[piece:] * scaling


def shape(dims, kind):
    return jax.ShapeDtypeStruct(tuple(dims), kind)


def local(
    act_in,
    partner_in,
    stashed,
    grad_in,
    down_weights,
    up_weights,
    coarse,
    nest_owner,
    nest_cell,
    land_weight,
):
    height, breadth, channels = act_in.shape[1:]
    depth = down_weights.shape[-1]
    half_rows = height // 2
    n_tx, n_ty = lax.axis_size("tx"), lax.axis_size("ty")
    position, segments = lax.axis_index("segment"), lax.axis_size("segment")
    scaling = 1.0 / math.sqrt(height * breadth * n_tx * n_ty)
    down_taps = jnp.swapaxes(down_weights, 3, 4).reshape(9, depth, channels)
    up_taps = up_weights.reshape(9, depth, channels)

    owners = nest_owner.reshape(-1)
    tile = shape((height, breadth, channels), BF16)
    pay = shape((height + 1 + coarse.shape[0] // 8, 8, channels), BF16)
    merged = n_ty == 4 and n_tx == 2
    if merged:
        st_far = lax.ppermute(stashed, "tx", crossed("tx", 1))
    side = pltpu.VMEM((height, 16, channels), BF16)
    full = pltpu.VMEM((height, breadth, channels), BF16)
    grad_own, z_pay0, z_pay1 = call(
        edge_kernel,
        (tile, pay, pay),
        [HBM] * 8,
        [side] * 4
        + [full] * 2
        + [pltpu.VMEM((height // 4, breadth, channels), F32), pltpu.VMEM(coarse.shape, BF16)]
        + [pltpu.SMEM(scalars.shape, jnp.int32) for scalars in (owners, nest_cell, land_weight)]
        + [pltpu.SemaphoreType.DMA((10,))],
        flops=1000,
        moved=1000,
    )(*in_hbm(owners, nest_cell, land_weight, act_in, partner_in, stashed, grad_in, coarse))
    pairs, others = swaps("ty")
    if merged:
        others = crossed("ty", 3)
        grad_far = lax.ppermute(grad_own, "tx", crossed("tx", 1))
    z0 = lax.ppermute(z_pay0, "ty", pairs)
    z1 = lax.ppermute(z_pay1, "ty", others)
    if merged:
        table_parts = (coarse, lax.ppermute(coarse, "ty", crossed("ty", 2)))
    else:
        table_parts = (lax.all_gather(coarse, "ty", tiled=True),)
    flat = shape((depth, 9 * channels), BF16)
    taps_room = pltpu.VMEM((9, depth, channels), BF16)
    base, stash, flat_up, flat_down = call(
        prepare_kernel,
        (shape((height, breadth, channels), F32), tile, flat, flat),
        [HBM] * 5,
        [full, full, taps_room, taps_room, pltpu.SemaphoreType.DMA((5,))],
        flops=1000,
        moved=1000,
    )(*in_hbm(act_in, partner_in, stashed, up_taps, down_taps))
    operands = (base, z0, z1, *table_parts)
    rooms = [
        pltpu.VMEM((n_ty * coarse.shape[0], channels), F32),
        pltpu.VMEM((height // 4, breadth, channels), F32),
    ]
    pairs, others = swaps("tx")
    if merged:
        rim = call(
            rim_kernel,
            shape((height, 8, channels), BF16),
            [VMEM] * 2 + [pl.BlockSpec(memory_space=pl.ANY)] * 2,
            flops=1000,
            moved=1000,
        )(z0, z1, flat_up, st_far)
        rim_far = lax.ppermute(rim, "tx", pairs)
        pay, blocks = call(
            functools.partial(condition_kernel, True),
            (shape((3 * (breadth // 8 + 1), 8, channels), BF16), shape((height, breadth + 16, channels), BF16)),
            [SMEM] * 2 + [VMEM] * len(operands),
            rooms,
            flops=6_000_000_000,
            moved=1000,
        )(owners, nest_cell, *operands)
        ys = [lax.ppermute(pay, "tx", pairs)]
    else:
        pay = shape((STRIP_ROWS, breadth + 16, channels), BF16)
        *pays, blocks = call(
            functools.partial(condition_kernel, False),
            (pay, pay, shape((3, height, breadth + 16, channels), BF16)),
            [SMEM] * 2 + [VMEM] * (len(operands) + 2),
            rooms,
        )(owners, nest_cell, *operands, stash, grad_own)
        ys = [lax.ppermute(pays[0], "tx", pairs), lax.ppermute(pays[1], "tx", others) if others else pays[1]]

    wide = 2 * PAD + 16
    rows_flat = 9 * depth

    def tap_rooms(count):
        room = pltpu.VMEM((count + 1, PAD, 3 * channels), BF16)
        return [pltpu.VMEM((2 * count + 2, wide, channels), F32), room, room]

    fine = pltpu.VMEM((height, breadth, channels), F32)
    products = lambda count: pltpu.VMEM((count, PAD, 9 * channels), F32)
    if merged:
        piece = rows_flat // (n_tx * n_ty)
        part = shape((2 * piece, channels), BF16)
        flat_half = rows_flat // 2
        in_grad, own_sum, *sends = call(
            paired_kernel,
            (tile, shape((2 * piece, channels), F32), part, part, part),
            [VMEM] * 8,
            tap_rooms(height)
            + [
                pltpu.VMEM((height, PAD, 9 * channels), BF16),
                pltpu.VMEM((9 * channels // 2, 128), F32),
                pltpu.VMEM((9 * channels // 2, 128), F32),
                pltpu.VMEM((5 * depth, channels), F32),
                pltpu.VMEM((flat_half, channels), F32),
                pltpu.VMEM((height + 1, PAD, depth), BF16),
                products(half_rows + 1),
                fine,
            ],
            flops=900_000_000,
            moved=4_000_000,
        )(stash, grad_own, st_far, grad_far, rim, rim_far, flat_up, flat_down)
        arrived = [lax.ppermute(sends[d - 1], "ty", crossed("ty", d)) for d in (3, 2, 1)]
        summed = shape((piece, channels), F32)
        up_sum, down_sum = call(
            functools.partial(total_kernel, scaling), (summed, summed), [VMEM] * 4, flops=10_000_000_000
        )(own_sum, *arrived)
        up_sum, down_sum = up_sum.reshape(1, -1), down_sum.reshape(1, -1)
    else:
        whole = shape((rows_flat, channels), F32)
        in_grad, up_flat, down_flat = call(
            grads_kernel,
            (tile, whole, whole),
            [VMEM] * 5,
            tap_rooms(half_rows + 1)
            + [
                pltpu.VMEM((half_rows + 1, PAD, 9 * channels), BF16),
                pltpu.VMEM((9 * channels, 128), F32),
                pltpu.VMEM((9 * channels, 128), F32),
                products(half_rows + 1),
                fine,
            ],
            flops=500_000_000,
            moved=4_000_000,
        )(blocks, *ys, flat_up, flat_down)
        pooled = lambda flat: lax.psum_scatter(
            flat.reshape(-1) * scaling, ("tx", "ty"), scatter_dimension=0, tiled=True
        )[None]
        down_sum, up_sum = pooled(down_flat), pooled(up_flat)

    count = half_rows + 2
    near, far = call(
        functools.partial(forward_kernel, merged),
        (tile, tile),
        [VMEM] * (4 + len(ys)),
        tap_rooms(count) + [products(count), pltpu.VMEM((4, PAD, channels), F32), fine],
        flops=600_000_000,
        moved=4_000_000,
    )(blocks, *ys, in_grad, flat_up, flat_down)
    from_far = lax.ppermute(far, "segment", [(i, segments - 1 - i) for i in range(segments)])
    from_near = lax.ppermute(near, "segment", crossed("segment", 1))
    blank = jnp.zeros_like(from_near)
    odd = position % 2 == 1
    act_out = jnp.where(position == 0, blank, jnp.where(odd, from_near, from_far))
    grad_out = jnp.where(position == segments - 1, blank, jnp.where(odd, from_far, from_near))
    partner_out = jnp.where(position < segments, from_far, blank)
    return (act_out[None], grad_out[None], partner_out[None], down_sum, up_sum)


def solution(mesh):
    tile = P("segment", "tx", "ty", None)
    weights = P("segment", None, None, None, None)
    grads = P("segment", ("tx", "ty"))
    rows = P(("tx", "ty"))
    return jax.shard_map(
        local,
        mesh=mesh,
        in_specs=(tile,) * 4 + (weights,) * 2 + (P(("tx", "ty"), None),) * 2 + (rows, P("tx", "ty")),
        out_specs=(tile,) * 3 + (grads,) * 2,
        check_vma=False,
    )
```

time: 49.9 us -> 37 us (0.74)
  local copies, waits for them, and re-layouts: 4.83 us -> 0.02 us
  waiting for transfers between devices: 15 us -> 10.2 us
  starting transfers between devices: 19.5 us -> 15.5 us
  Pallas kernels: 8.63 us -> 9.47 us
    unnamed x20 -> x6, local copies, waits for them, and re-layouts: 4.83 us -> 0.02 us
    ppermute x1, waiting for transfers between devices: 4.53 us -> 0.58 us  [local(): table_parts = (coarse, lax.ppermute(coarse, 'ty', crossed('ty', 2)))]
    ppermute x11 -> x9, starting transfers between devices: 13.8 us -> 11.2 us  [the longest x3 4.45 us: local(): lax.ppermute(sends[d - 1], 'ty', crossed('ty', d))]
    ppermute x11 -> x9, waiting for transfers between devices: 10.4 us -> 8.44 us  [the longest x1 3.88 us: local(): lax.ppermute(far, 'segment', [(i, segments - 1 - i) for i in range(segmen...]
    ppermute x1, starting transfers between devices: 3.09 us -> 1.64 us  [local(): z0 = lax.ppermute(z_pay0, 'ty', pairs)]
    ppermute x1, waiting for transfers between devices: 0.01 us -> 1.19 us  [local(): z1 = lax.ppermute(z_pay1, 'ty', others)]
    pallas_call x9 -> x7, Pallas kernels: 8.63 us -> 9.47 us  [the longest x1 3.25 us: local(): call(paired_kernel, (tile, shape((2 * piece, channels), F32), part, part,...]
  transfers between devices with their start and end apart: 14 -> 12, of which waited for: 5 -> 6; matrix products, arithmetic and copies ran while one was open for 2% -> 0% of each run, Pallas kernels for 6% -> 26%
where the time goes in v2:
time: 37 us; the launch traced here: 36.8 us
  starting transfers between devices  15.5 us (42%)
  waiting for transfers between devices  10.2 us (28%)
  Pallas kernels  9.47 us (26%)
  other arithmetic  0.93 us (3%)
  between operations  0.72 us (2%)
    ppermute x3, starting transfers between devices, local(): lax.ppermute(sends[d - 1], 'ty', crossed('ty', d))  4.45 us
    ppermute x1, waiting for transfers between devices, local(): lax.ppermute(far, 'segment', [(i, segments - 1 - i) for i in range(segmen...  3.88 us
    pallas_call x1, Pallas kernels, local(): call(paired_kernel, (tile, shape((2 * piece, channels), F32), part, part,...  3.25 us
    ppermute x1, starting transfers between devices, local(): st_far = lax.ppermute(stashed, 'tx', crossed('tx', 1))  3.03 us
    ppermute x1, starting transfers between devices, local(): z1 = lax.ppermute(z_pay1, 'ty', others)  2.47 us
    ppermute x3, waiting for transfers between devices, local(): lax.ppermute(sends[d - 1], 'ty', crossed('ty', d))  2.38 us
    ppermute x1, waiting for transfers between devices, local(): grad_far = lax.ppermute(grad_own, 'tx', crossed('tx', 1))  1.82 us
    pallas_call x1, Pallas kernels, local(): call(functools.partial(forward_kernel, merged), (tile, tile), [VMEM] * (4...  1.78 us
  transfers between devices with their start and end apart: 12, of which 6 were waited for; matrix products, arithmetic and copies ran while one was open for 0% of the time, Pallas kernels for 26%

profile of v2, /device:TPU:0, one launch (start us, length us, event | category | flops | bytes accessed | tf_op | source)
XLA Modules:
  0.0 36.8 jit_solution(18368704219697420830)
XLA Ops:
  0.6 3.0 %collective-permute-start.4 = (bf16[1,16,64,128]{3,2,1,0:T(8,128)(2,1)}, bf16[1,16,64,128]{3,2,1,0:T(8,128)(2,1)S(1)}, u32[]{:S(2)}, u32[]{:S(2)}) collective-permute-start(bf16[1,16,64,128]{3,2,1,0:T(8,128)(2,1)} %st.3), channel_id=1, source_target_pairs={{0,4},{4,0},{1,5},{5,1},{2,6},{6,2},{3,7},{7,3},{8,12},{12,8},{9,1... | collective-permute-start | bytes 786440 | tf_op jit(solution)/shard_map/ppermute | solution.py:586
  3.7 0.0 copy-start
  3.7 1.3 %shard_map.138 = (bf16[16,64,128]{2,1,0:T(8,128)(2,1)S(1)}, bf16[25,8,128]{2,1,0:T(8,128)(2,1)S(1)}, bf16[25,8,128]{2,1,0:T(8,128)(2,1)S(1)}) custom-call(s32[64]{0:T(128)} %bitcast.13, s32[64]{0:T(128)} %cell.1, s32[4,16]{1,0:T(4,128)} %land_in.1, bf16[1,16,64,128]{3,2,1,0:T(8,128)(2,1)} %act.3, bf16[1,16,64,128]{3,2,1,0:T(8,128)(2,1)} %par.3, ...), custom_call_target="tpu_custom_call" | custom-call | flops 1000 | bytes 1000 | tf_op jit(solution)/shard_map/pallas_call | solution.py:589
  5.0 1.6 %collective-permute-start = (bf16[25,8,128]{2,1,0:T(8,128)(2,1)S(1)}, bf16[25,8,128]{2,1,0:T(8,128)(2,1)S(1)}, u32[]{:S(2)}, u32[]{:S(2)}) collective-permute-start(bf16[25,8,128]{2,1,0:T(8,128)(2,1)S(1)} %get-tuple-element.24), channel_id=1, source_target_pairs={{0,1},{2,3},{1,0},{3,2},{4,5},{6,7},{5,4},{7,6},{8,9},{10,11},{9,8... | collective-permute-start | bytes 153608 | tf_op jit(solution)/shard_map/ppermute | solution.py:605
  6.6 2.5 %collective-permute-start.1 = (bf16[25,8,128]{2,1,0:T(8,128)(2,1)S(1)}, bf16[25,8,128]{2,1,0:T(8,128)(2,1)S(1)}, u32[]{:S(2)}, u32[]{:S(2)}) collective-permute-start(bf16[25,8,128]{2,1,0:T(8,128)(2,1)S(1)} %get-tuple-element.25), channel_id=1, source_target_pairs={{0,3},{1,2},{2,1},{3,0},{4,7},{5,6},{6,5},{7,4},{8,11},{9,10},{10,... | collective-permute-start | bytes 153608 | tf_op jit(solution)/shard_map/ppermute | solution.py:606
  9.1 0.0 copy-done
  9.1 0.1 collective-permute-start.2
  9.2 0.5 %collective-permute-start.5 = (bf16[16,64,128]{2,1,0:T(8,128)(2,1)S(1)}, bf16[16,64,128]{2,1,0:T(8,128)(2,1)S(1)}, u32[]{:S(2)}, u32[]{:S(2)}) collective-permute-start(bf16[16,64,128]{2,1,0:T(8,128)(2,1)S(1)} %get-tuple-element.29.grad), channel_id=1, source_target_pairs={{0,4},{4,0},{1,5},{5,1},{2,6},{6,2},{3,7},{7,3},{8,12},{12,8},{9,1... | collective-permute-start | bytes 786440 | tf_op jit(solution)/shard_map/ppermute | solution.py:604
  9.7 1.6 %shard_map.137 = (f32[16,64,128]{2,1,0:T(8,128)S(1)}, bf16[16,64,128]{2,1,0:T(8,128)(2,1)S(1)}, bf16[192,1152]{1,0:T(8,128)(2,1)S(1)}, bf16[192,1152]{1,0:T(8,128)(2,1)S(1)}) custom-call(bf16[1,16,64,128]{3,2,1,0:T(8,128)(2,1)} %act.3, bf16[1,16,64,128]{3,2,1,0:T(8,128)(2,1)} %par.3, bf16[1,16,64,128]{3,2,1,0:T(8,128)(2,1)} %st.3, ...), custom_call_target="tpu_custom_call" | custom-call | flops 1000 | bytes 1000 | tf_op jit(solution)/shard_map/pallas_call | solution.py:613
  11.3 0.0 collective-permute-done.z0
  11.4 1.2 %collective-permute-done.1.z1 = bf16[25,8,128]{2,1,0:T(8,128)(2,1)S(1)} collective-permute-done((bf16[25,8,128]{2,1,0:T(8,128)(2,1)S(1)}, bf16[25,8,128]{2,1,0:T(8,128)(2,1)S(1)}, u32[]{:S(2)}, u32[]{:S(2)}) %collective-permute-start.1) | collective-permute-done | bytes 51232 | tf_op jit(solution)/shard_map/ppermute | solution.py:606
  12.5 0.0 collective-permute-done.4._stash.st_far
  12.6 0.0 copy-start.1
  12.6 0.0 copy-start.2
  12.6 0.6 %collective-permute-start.6 = (bf16[16,8,128]{2,1,0:T(8,128)(2,1)S(1)}, bf16[16,8,128]{2,1,0:T(8,128)(2,1)S(1)}, u32[]{:S(2)}, u32[]{:S(2)}) collective-permute-start(bf16[16,8,128]{2,1,0:T(8,128)(2,1)S(1)} %shard_map.140.rim), channel_id=1, source_target_pairs={{0,4},{4,0},{1,5},{5,1},{2,6},{6,2},{3,7},{7,3},{8,12},{12,8},{9,1... | collective-permute-start | bytes 98312 | tf_op jit(solution)/shard_map/ppermute | solution.py:635
  13.2 0.6 %collective-permute-done.2.rest_0_ = bf16[64,128]{1,0:T(8,128)(2,1)S(1)} collective-permute-done((bf16[64,128]{1,0:T(8,128)(2,1)S(1)}, bf16[64,128]{1,0:T(8,128)(2,1)S(1)}, u32[]{:S(2)}, u32[]{:S(2)}) %collective-permute-start.2) | collective-permute-done | bytes 16416 | tf_op jit(solution)/shard_map/ppermute | solution.py:608
  13.8 0.0 copy-done.1
  13.8 0.0 copy-done.2
  13.8 0.8 %shard_map.139 = (bf16[27,8,128]{2,1,0:T(8,128)(2,1)S(1)}, bf16[16,80,128]{2,1,0:T(8,128)(2,1)S(1)}) custom-call(s32[64]{0:T(128)S(1)} %bitcast.14, s32[64]{0:T(128)S(1)} %copy-done.2, f32[16,64,128]{2,1,0:T(8,128)S(1)} %get-tuple-element.23.base, bf16[25,8,128]{2,1,0:T(8,128)(2,1)S(1)} %collective-permute-done.z0, ...), custom_call_target="tpu_custom_call" | custom-call | flops 6000000000 | bytes 1000 | tf_op jit(solution)/shard_map/pallas_call | solution.py:636
  14.5 1.0 %collective-permute-start.3 = (bf16[27,8,128]{2,1,0:T(8,128)(2,1)S(1)}, bf16[27,8,128]{2,1,0:T(8,128)(2,1)S(1)}, u32[]{:S(2)}, u32[]{:S(2)}) collective-permute-start(bf16[27,8,128]{2,1,0:T(8,128)(2,1)S(1)} %get-tuple-element.27), channel_id=1, source_target_pairs={{0,4},{4,0},{1,5},{5,1},{2,6},{6,2},{3,7},{7,3},{8,12},{12,8},{9,1... | collective-permute-start | bytes 165896 | tf_op jit(solution)/shard_map/ppermute | solution.py:644
  15.6 1.8 %collective-permute-done.5.grad_far = bf16[16,64,128]{2,1,0:T(8,128)(2,1)S(1)} collective-permute-done((bf16[16,64,128]{2,1,0:T(8,128)(2,1)S(1)}, bf16[16,64,128]{2,1,0:T(8,128)(2,1)S(1)}, u32[]{:S(2)}, u32[]{:S(2)}) %collective-permute-start.5) | collective-permute-done | bytes 262176 | tf_op jit(solution)/shard_map/ppermute | solution.py:604
  17.4 0.4 collective-permute-done.6.rim_far
  17.7 3.3 %shard_map.141 = (bf16[16,64,128]{2,1,0:T(8,128)(2,1)S(1)}, f32[432,128]{1,0:T(8,128)S(1)}, bf16[432,128]{1,0:T(8,128)(2,1)S(1)}, bf16[432,128]{1,0:T(8,128)(2,1)S(1)}, bf16[432,128]{1,0:T(8,128)(2,1)S(1)}) custom-call(bf16[16,64,128]{2,1,0:T(8,128)(2,1)S(1)} %get-tuple-element.28.st, bf16[16,64,128]{2,1,0:T(8,128)(2,1)S(1)} %get-tuple-element.29.grad, ...), custom_call_target="tpu_custom_call" | custom-call | flops 900000000 | bytes 4000000 | tf_op jit(solution)/shard_map/pallas_call | solution.py:668
  21.0 3.2 %collective-permute-start.9 = (bf16[432,128]{1,0:T(8,128)(2,1)S(1)}, bf16[432,128]{1,0:T(8,128)(2,1)S(1)}, u32[]{:S(2)}, u32[]{:S(2)}) collective-permute-start(bf16[432,128]{1,0:T(8,128)(2,1)S(1)} %get-tuple-element.36), channel_id=1, source_target_pairs={{0,3},{1,2},{2,1},{3,0},{4,7},{5,6},{6,5},{7,4},{8,11},{9,10},{10,... | collective-permute-start | bytes 331784 | tf_op jit(solution)/shard_map/ppermute | solution.py:686
  24.2 0.0 collective-permute-start.10
  24.2 1.2 %collective-permute-start.11 = (bf16[432,128]{1,0:T(8,128)(2,1)S(1)}, bf16[432,128]{1,0:T(8,128)(2,1)S(1)}, u32[]{:S(2)}, u32[]{:S(2)}) collective-permute-start(bf16[432,128]{1,0:T(8,128)(2,1)S(1)} %get-tuple-element.38), channel_id=1, source_target_pairs={{0,1},{1,0},{2,3},{3,2},{4,5},{5,4},{6,7},{7,6},{8,9},{9,8},{10,11... | collective-permute-start | bytes 331784 | tf_op jit(solution)/shard_map/ppermute | solution.py:686
  25.4 0.0 collective-permute-done.3.rest_0_
  25.4 1.8 %shard_map.142 = (bf16[16,64,128]{2,1,0:T(8,128)(2,1)S(1)}, bf16[16,64,128]{2,1,0:T(8,128)(2,1)S(1)}) custom-call(bf16[16,80,128]{2,1,0:T(8,128)(2,1)S(1)} %get-tuple-element.26.blocks, bf16[27,8,128]{2,1,0:T(8,128)(2,1)S(1)} %collective-permute-done.3.rest_0_, bf16[16,64,128]{2,1,0:T(8,128)(2,1)S(1)} %get-tuple-element.32.rest_1_, ...), custom_call_target="tpu_custom_call" | custom-call | flops 600000000 | bytes 4000000 | tf_op jit(solution)/shard_map/pallas_call | solution.py:715
  27.2 0.1 collective-permute-start.8
  27.3 1.6 %collective-permute-start.7 = (bf16[16,64,128]{2,1,0:T(8,128)(2,1)S(1)}, bf16[16,64,128]{2,1,0:T(8,128)(2,1)S(1)}, u32[]{:S(2)}, u32[]{:S(2)}) collective-permute-start(bf16[16,64,128]{2,1,0:T(8,128)(2,1)S(1)} %get-tuple-element.33), channel_id=1, source_target_pairs={{0,8},{8,0},{16,24},{24,16},{1,9},{9,1},{17,25},{25,17},{2,10},{10... | collective-permute-start | bytes 786440 | tf_op jit(solution)/shard_map/ppermute | solution.py:724
  28.9 0.0 collective-permute-done.9.first
  28.9 2.4 %collective-permute-done.10.second = bf16[432,128]{1,0:T(8,128)(2,1)S(1)} collective-permute-done((bf16[432,128]{1,0:T(8,128)(2,1)S(1)}, bf16[432,128]{1,0:T(8,128)(2,1)S(1)}, u32[]{:S(2)}, u32[]{:S(2)}) %collective-permute-start.10) | collective-permute-done | bytes 110624 | tf_op jit(solution)/shard_map/ppermute | solution.py:686
  31.3 0.0 collective-permute-done.11.third
  31.3 0.7 %shard_map.143 = (f32[216,128]{1,0:T(8,128)}, f32[216,128]{1,0:T(8,128)}) custom-call(f32[432,128]{1,0:T(8,128)S(1)} %get-tuple-element.35.own, bf16[432,128]{1,0:T(8,128)(2,1)S(1)} %collective-permute-done.9.first, bf16[432,128]{1,0:T(8,128)(2,1)S(1)} %collective-permute-done.10.second, bf16[432,128]{1,0:T(8,128)(2,1)S(1)} %collective-permute-done.11.third), custom_call_target="tpu_custom_call" | custom-call | flops 10000000000 | tf_op jit(solution)/shard_map/pallas_call | solution.py:688
  32.0 3.9 %collective-permute-done.8 = bf16[16,64,128]{2,1,0:T(8,128)(2,1)S(1)} collective-permute-done((bf16[16,64,128]{2,1,0:T(8,128)(2,1)S(1)}, bf16[16,64,128]{2,1,0:T(8,128)(2,1)S(1)}, u32[]{:S(2)}, u32[]{:S(2)}) %collective-permute-start.8) | collective-permute-done | bytes 262176 | tf_op jit(solution)/shard_map/ppermute | solution.py:723
  35.9 0.0 collective-permute-done.7
  35.9 0.9 %select_bitcast_fusion.1 = (bf16[1,16,64,128]{3,2,1,0:T(8,128)(2,1)}, bf16[1,16,64,128]{3,2,1,0:T(8,128)(2,1)}, bf16[1,16,64,128]{3,2,1,0:T(8,128)(2,1)}) fusion(bf16[16,64,128]{2,1,0:T(8,128)(2,1)S(1)} %collective-permute-done.8, bf16[16,64,128]{2,1,0:T(8,128)(2,1)S(1)} %collective-permute-done.7, pred[]{:T(512)S(6)} %eq.13, pred[]{:T(512)S(6)} %eq.12, ...), kind=kLoop, calls=%fused_computation.1 | loop fusion | flops 655360 | bytes 1310724 | tf_op jit(solution)/shard_map/broadcast_in_dim | solution.py:730
  (1 shorter events, 0.0 us)
Async XLA Ops:
  0.6 11.9 %collective-permute-start.4 = (bf16[1,16,64,128]{3,2,1,0:T(8,128)(2,1)}, bf16[1,16,64,128]{3,2,1,0:T(8,128)(2,1)S(1)}, u32[]{:S(2)}, u32[]{:S(2)}) collective-permute-start(bf16[1,16,64,128]{3,2,1,0:T(8,128)(2,1)} %st.3), channel_id=1, source_target_pairs={{0,4},{4,0},{1,5},{5,1},{2,6},{6,2},{3,7},{7,3},{8,12},{12,8},{9,1... | collective-permute-start | bytes 786440 | tf_op jit(solution)/shard_map/ppermute | solution.py:586
  3.7 5.4 %copy-start = (bf16[64,128]{1,0:T(8,128)(2,1)S(1)}, bf16[64,128]{1,0:T(8,128)(2,1)}, u32[]{:S(2)}) copy-start(bf16[64,128]{1,0:T(8,128)(2,1)} %coarse.3) | copy-start | bytes 49156
  5.0 6.4 %collective-permute-start = (bf16[25,8,128]{2,1,0:T(8,128)(2,1)S(1)}, bf16[25,8,128]{2,1,0:T(8,128)(2,1)S(1)}, u32[]{:S(2)}, u32[]{:S(2)}) collective-permute-start(bf16[25,8,128]{2,1,0:T(8,128)(2,1)S(1)} %get-tuple-element.24), channel_id=1, source_target_pairs={{0,1},{2,3},{1,0},{3,2},{4,5},{6,7},{5,4},{7,6},{8,9},{10,11},{9,8... | collective-permute-start | bytes 153608 | tf_op jit(solution)/shard_map/ppermute | solution.py:605
  6.6 5.9 %collective-permute-start.1 = (bf16[25,8,128]{2,1,0:T(8,128)(2,1)S(1)}, bf16[25,8,128]{2,1,0:T(8,128)(2,1)S(1)}, u32[]{:S(2)}, u32[]{:S(2)}) collective-permute-start(bf16[25,8,128]{2,1,0:T(8,128)(2,1)S(1)} %get-tuple-element.25), channel_id=1, source_target_pairs={{0,3},{1,2},{2,1},{3,0},{4,7},{5,6},{6,5},{7,4},{8,11},{9,10},{10,... | collective-permute-start | bytes 153608 | tf_op jit(solution)/shard_map/ppermute | solution.py:606
  9.1 4.6 %collective-permute-start.2 = (bf16[64,128]{1,0:T(8,128)(2,1)S(1)}, bf16[64,128]{1,0:T(8,128)(2,1)S(1)}, u32[]{:S(2)}, u32[]{:S(2)}) collective-permute-start(bf16[64,128]{1,0:T(8,128)(2,1)S(1)} %copy-done), channel_id=1, source_target_pairs={{0,2},{1,3},{2,0},{3,1},{4,6},{5,7},{6,4},{7,5},{8,10},{9,11},{10,... | collective-permute-start | bytes 49160 | tf_op jit(solution)/shard_map/ppermute | solution.py:608
  9.2 8.1 %collective-permute-start.5 = (bf16[16,64,128]{2,1,0:T(8,128)(2,1)S(1)}, bf16[16,64,128]{2,1,0:T(8,128)(2,1)S(1)}, u32[]{:S(2)}, u32[]{:S(2)}) collective-permute-start(bf16[16,64,128]{2,1,0:T(8,128)(2,1)S(1)} %get-tuple-element.29.grad), channel_id=1, source_target_pairs={{0,4},{4,0},{1,5},{5,1},{2,6},{6,2},{3,7},{7,3},{8,12},{12,8},{9,1... | collective-permute-start | bytes 786440 | tf_op jit(solution)/shard_map/ppermute | solution.py:604
  12.6 1.2 %copy-start.1 = (s32[64,1]{0,1:T(1,128)S(1)}, s32[64,1]{0,1:T(1,128)}, u32[]{:S(2)}) copy-start(s32[64,1]{0,1:T(1,128)} %param.17) | copy-start | bytes 772
  12.6 1.2 %copy-start.2 = (s32[64]{0:T(128)S(1)}, s32[64]{0:T(128)}, u32[]{:S(2)}) copy-start(s32[64]{0:T(128)} %cell.1) | copy-start | bytes 772
  12.6 5.1 %collective-permute-start.6 = (bf16[16,8,128]{2,1,0:T(8,128)(2,1)S(1)}, bf16[16,8,128]{2,1,0:T(8,128)(2,1)S(1)}, u32[]{:S(2)}, u32[]{:S(2)}) collective-permute-start(bf16[16,8,128]{2,1,0:T(8,128)(2,1)S(1)} %shard_map.140.rim), channel_id=1, source_target_pairs={{0,4},{4,0},{1,5},{5,1},{2,6},{6,2},{3,7},{7,3},{8,12},{12,8},{9,1... | collective-permute-start | bytes 98312 | tf_op jit(solution)/shard_map/ppermute | solution.py:635
  14.5 10.9 %collective-permute-start.3 = (bf16[27,8,128]{2,1,0:T(8,128)(2,1)S(1)}, bf16[27,8,128]{2,1,0:T(8,128)(2,1)S(1)}, u32[]{:S(2)}, u32[]{:S(2)}) collective-permute-start(bf16[27,8,128]{2,1,0:T(8,128)(2,1)S(1)} %get-tuple-element.27), channel_id=1, source_target_pairs={{0,4},{4,0},{1,5},{5,1},{2,6},{6,2},{3,7},{7,3},{8,12},{12,8},{9,1... | collective-permute-start | bytes 165896 | tf_op jit(solution)/shard_map/ppermute | solution.py:644
  21.0 7.9 %collective-permute-start.9 = (bf16[432,128]{1,0:T(8,128)(2,1)S(1)}, bf16[432,128]{1,0:T(8,128)(2,1)S(1)}, u32[]{:S(2)}, u32[]{:S(2)}) collective-permute-start(bf16[432,128]{1,0:T(8,128)(2,1)S(1)} %get-tuple-element.36), channel_id=1, source_target_pairs={{0,3},{1,2},{2,1},{3,0},{4,7},{5,6},{6,5},{7,4},{8,11},{9,10},{10,... | collective-permute-start | bytes 331784 | tf_op jit(solution)/shard_map/ppermute | solution.py:686
  24.2 7.0 %collective-permute-start.10 = (bf16[432,128]{1,0:T(8,128)(2,1)S(1)}, bf16[432,128]{1,0:T(8,128)(2,1)S(1)}, u32[]{:S(2)}, u32[]{:S(2)}) collective-permute-start(bf16[432,128]{1,0:T(8,128)(2,1)S(1)} %get-tuple-element.37), channel_id=1, source_target_pairs={{0,2},{1,3},{2,0},{3,1},{4,6},{5,7},{6,4},{7,5},{8,10},{9,11},{10,... | collective-permute-start | bytes 331784 | tf_op jit(solution)/shard_map/ppermute | solution.py:686
  24.2 7.0 %collective-permute-start.11 = (bf16[432,128]{1,0:T(8,128)(2,1)S(1)}, bf16[432,128]{1,0:T(8,128)(2,1)S(1)}, u32[]{:S(2)}, u32[]{:S(2)}) collective-permute-start(bf16[432,128]{1,0:T(8,128)(2,1)S(1)} %get-tuple-element.38), channel_id=1, source_target_pairs={{0,1},{1,0},{2,3},{3,2},{4,5},{5,4},{6,7},{7,6},{8,9},{9,8},{10,11... | collective-permute-start | bytes 331784 | tf_op jit(solution)/shard_map/ppermute | solution.py:686
  27.2 8.6 %collective-permute-start.8 = (bf16[16,64,128]{2,1,0:T(8,128)(2,1)S(1)}, bf16[16,64,128]{2,1,0:T(8,128)(2,1)S(1)}, u32[]{:S(2)}, u32[]{:S(2)}) collective-permute-start(bf16[16,64,128]{2,1,0:T(8,128)(2,1)S(1)} %get-tuple-element.34), channel_id=1, source_target_pairs={{0,24},{8,16},{16,8},{24,0},{1,25},{9,17},{17,9},{25,1},{2,26},{10... | collective-permute-start | bytes 786440 | tf_op jit(solution)/shard_map/ppermute | solution.py:723
  27.3 8.6 %collective-permute-start.7 = (bf16[16,64,128]{2,1,0:T(8,128)(2,1)S(1)}, bf16[16,64,128]{2,1,0:T(8,128)(2,1)S(1)}, u32[]{:S(2)}, u32[]{:S(2)}) collective-permute-start(bf16[16,64,128]{2,1,0:T(8,128)(2,1)S(1)} %get-tuple-element.33), channel_id=1, source_target_pairs={{0,8},{8,0},{16,24},{24,16},{1,9},{9,1},{17,25},{25,17},{2,10},{10... | collective-permute-start | bytes 786440 | tf_op jit(solution)/shard_map/ppermute | solution.py:724

commit v3 on v2

--- a/solution.py
+++ b/solution.py
@@ -18,17 +18,31 @@
 STRIP_ROWS = 7
 
 
-def call(body, out_shape, in_specs, scratch=(), flops=0, moved=0, limit=48):
-    out_specs = jax.tree.map(lambda _: VMEM, out_shape)
+def call(body, out_shape, in_specs, scratch=(), flops=0, moved=0, limit=24, out_specs=None, aliases=()):
+    out_specs = out_specs or jax.tree.map(lambda _: VMEM, out_shape)
     return pl.pallas_call(
         body,
         out_shape=out_shape,
         in_specs=in_specs,
         out_specs=out_specs,
         scratch_shapes=list(scratch),
+        input_output_aliases=dict(aliases),
         compiler_params=pltpu.CompilerParams(vmem_limit_bytes=limit * 1024 * 1024),
         cost_estimate=pl.CostEstimate(flops=flops, bytes_accessed=moved, transcendentals=0),
     )
+
+
+def passed_on(arrays, flops, after=()):
+    here = [pl.BlockSpec(memory_space=pl.ANY)] * len(arrays)
+    return list(call(
+        lambda *refs: None,
+        tuple(jax.ShapeDtypeStruct(x.shape, x.dtype) for x in arrays),
+        here + [pl.BlockSpec(memory_space=pl.ANY)] * len(after),
+        flops=flops,
+        moved=1000,
+        out_specs=tuple(here),
+        aliases=[(k, k) for k in range(len(arrays))],
+    )(*arrays, *after))
 
 
 def in_hbm(*operands):
@@ -245,16 +259,17 @@
 
 
 def spread_taps(field, taps, odd_taps, count, first):
+    width = taps.shape[1]
     for row in range(count):
         target = taps if row % 2 == 0 else odd_taps
         for tap in range(3):
-            value = field[row, pl.ds(first + tap, PAD, stride=2), :]
+            value = field[row, pl.ds(first + tap, width, stride=2), :]
             target[row // 2, :, tap * 128 : tap * 128 + 128] = value.astype(BF16)
 
 
 def three_rows(even_taps, odd_taps, count):
     wide = 3 * 128
-    whole = lambda ref, a: ref[a : a + count].reshape(count * PAD, wide)
+    whole = lambda ref, a: ref[a : a + count].reshape(count * ref.shape[1], wide)
     return whole(even_taps, 0), whole(odd_taps, 0), whole(even_taps, 1)
 
 
@@ -278,18 +293,10 @@
         flat[:, tap * 128 : tap * 128 + 128] = taps[tap]
 
 
-def sweep(wide, field, even_taps, odd_taps, sums, flat_up, down, count, fill_stash, fill_grad):
-    field[:, wide:] = jnp.zeros((field.shape[0], field.shape[1] - wide, 128), F32)
-    fill_stash()
-    spread_taps(field, even_taps, odd_taps, 2 * count + 1, LEFT - 1)
-    pre_back = lower(even_taps, odd_taps, count, down)
-    logistic = 1.0 / (1.0 + jnp.exp(-pre_back))
-    reduced = pre_back * logistic
-    slope = logistic * (1.0 + pre_back * (1.0 - logistic))
-    fill_grad()
+def window_sums(plane_of, count, sums):
     previous = None
     for row in range(2 * count + 2):
-        plane = [field[row, pl.ds(LEFT - 1 + k, PAD, stride=2), :] for k in range(4)]
+        plane = [plane_of(row, k) for k in range(4)]
         current = [plane[2] + plane[3], plane[1] + plane[2], plane[0] + plane[1]]
         if row > 0:
             for a in range(3):
@@ -297,8 +304,20 @@
                 if double % 2 == 0 and 0 <= double // 2 < count:
                     for b in range(3):
                         lanes = slice((3 * a + b) * 128, (3 * a + b) * 128 + 128)
-                        sums[double // 2, :, lanes] = (previous[b] + current[b]).astype(BF16)
+                        sums[double // 2, :, lanes] = (previous[b] + current[b]).astype(sums.dtype)
         previous = current
+
+
+def sweep(wide, field, even_taps, odd_taps, sums, flat_up, down, count, fill_stash, fill_grad):
+    field[:, wide:] = jnp.zeros((field.shape[0], field.shape[1] - wide, 128), F32)
+    fill_stash()
+    spread_taps(field, even_taps, odd_taps, 2 * count + 1, LEFT - 1)
+    pre_back = lower(even_taps, odd_taps, count, down)
+    logistic = 0.5 + 0.5 * jnp.tanh(0.5 * pre_back)
+    reduced = pre_back * logistic
+    slope = logistic * (1.0 + pre_back * (1.0 - logistic))
+    fill_grad()
+    window_sums(lambda row, k: field[row, pl.ds(LEFT - 1 + k, PAD, stride=2), :], count, sums)
     windows = sums[...].reshape(count * PAD, 9 * 128)
     raised = lax.dot_general(windows, flat_up[...], (((1,), (1,)), ((), ())), preferred_element_type=F32)
     return reduced.astype(BF16), raised * slope
@@ -361,7 +380,9 @@
     inside = ((row < half_rows) | has_below) & ((col < half_cols) | (has_right & (col == half_cols)))
     pre_grad = jnp.where(inside, pre_grad, 0.0).astype(BF16).reshape(count, PAD, depth)
     base = lambda row_id: ext[0, row_id, LEFT : wide - 8]
-    input_grad(pre_grad, flat_down, base, products, fine, in_grad)
+    moved = lax.dot(pre_grad.reshape(count * PAD, depth), flat_down[...], preferred_element_type=F32)
+    products[...] = moved.reshape(count, PAD, 9 * 128)
+    combine_fine(products, base, fine, in_grad)
     cells = half_rows * half_cols
     own = lambda value: value[:half_rows, :half_cols].reshape(cells, value.shape[-1])
     reduced, own_grad = own(reduced.reshape(count, PAD, depth)), own(pre_grad)
@@ -378,14 +399,19 @@
 
 
 def paired_kernel(
-    st, grad, st_far, grad_far, rim, rim_far, flat_up, flat_down, in_grad, own_sum, send1, send2, send3, *scratch
+    st, grad, st_far, grad_far, rim, rim_far, flat_up, flat_down, value, far, in_grad, *rest
 ):
-    field, even_taps, odd_taps, sums, d0, d1, up_flat, down_flat, grads, products, fine = scratch
+    own_sum, send1, send2, send3, field, even_taps, odd_taps, sums, d0, d1, up_flat, down_flat = rest[:12]
+    grads, products, fine, edge_taps, edge_sums = rest[12:]
     rows, breadth = grad.shape[0], grad.shape[1]
     wide = breadth + 16
-    count, half_cols = rows, breadth // 2
+    count, half_rows, half_cols = rows, rows // 2, breadth // 2
+    cells = count * half_cols
+    edge_count = half_rows + 1
     tx, ty = lax.axis_index("tx"), lax.axis_index("ty")
+    has_below = tx < lax.axis_size("tx") - 1
     has_right = ty < lax.axis_size("ty") - 1
+    first_row = rows * tx
 
     def fill(here_rows, there_rows, turn_before, turn_after):
         blank = jnp.zeros((wide, 128), F32)
@@ -400,37 +426,54 @@
             field[pl.ds(start, rows), 0:8] = turned(turn_before)
             field[pl.ds(start, rows), LEFT + breadth : wide] = turned(turn_after)
 
-    reduced, pre_grad = sweep(
-        wide,
-        field,
-        even_taps,
-        odd_taps,
-        sums,
-        flat_up,
-        flat_down,
-        count,
-        lambda: fill(lambda row: st[row], lambda row: st_far[0, row], 1, 5),
-        lambda: fill(lambda row: grad[row], lambda row: grad_far[row], 0, 0),
-    )
+    def slopes(pre_back):
+        logistic = 0.5 + 0.5 * jnp.tanh(0.5 * pre_back)
+        return logistic, logistic * (1.0 + pre_back * (1.0 - logistic))
+
+    def full_taps(values, weights):
+        return lax.dot_general(values, weights[...], (((1,), (1,)), ((), ())), preferred_element_type=F32)
+
+    edge = lambda row, k: field[first_row + row, pl.ds(LEFT - 1 + k + breadth, 8, stride=2), :]
+    flat_edge = lambda ref: ref[...].reshape(edge_count * 8, 9 * 128).astype(BF16)
+
+    field[:, wide:] = jnp.zeros((field.shape[0], field.shape[1] - wide, 128), F32)
+    fill(lambda row: st[row], lambda row: st_far[0, row], 1, 5)
+    spread_taps(field, even_taps, odd_taps, 2 * count + 1, LEFT - 1)
+    for p in range(edge_count):
+        for tap in range(9):
+            edge_taps[p, :, tap * 128 : tap * 128 + 128] = edge(2 * p + tap // 3, tap % 3)
+    pre_back = lower(even_taps, odd_taps, count, flat_down)
+    logistic, slope = slopes(pre_back)
+    reduced = (pre_back * logistic).astype(BF16)
+    edge_slope = slopes(full_taps(flat_edge(edge_taps), flat_down))[1]
+
+    fill(lambda row: grad[row], lambda row: grad_far[row], 0, 0)
+    window_sums(lambda row, k: field[row, pl.ds(LEFT - 1 + k, half_cols, stride=2), :], count, sums)
+    window_sums(edge, edge_count, edge_sums)
     depth = reduced.shape[1]
-    _, col = places(count, depth)
-    inside = (col < half_cols) | (has_right & (col == half_cols))
-    pre_grad = jnp.where(inside, pre_grad, 0.0).astype(BF16).reshape(count, PAD, depth)
-    grads[0:count] = pre_grad
-    grads[count] = jnp.zeros((PAD, depth), BF16)
-    base = lambda row: grad[row]
-    input_grad(grads[pl.ds(rows // 2 * tx, rows // 2 + 1)], flat_down, base, products, fine, in_grad)
-    cells = count * half_cols
-    own = lambda value: value[:, :half_cols].reshape(cells, value.shape[-1])
-    reduced, own_grad = own(reduced.reshape(count, PAD, depth)), own(pre_grad)
+    coupled = (full_taps(sums[...].reshape(cells, 9 * 128), flat_up) * slope).astype(BF16)
+    edge_shape = (edge_count, 8, depth)
+    row = lax.broadcasted_iota(jnp.int32, edge_shape, 0).reshape(edge_count * 8, depth)
+    inside = has_right & ((row < half_rows) | has_below)
+    edge_grad = jnp.where(inside, full_taps(flat_edge(edge_sums), flat_up) * edge_slope, 0.0).astype(BF16)
+    grads[0:count] = coupled.reshape(count, half_cols, depth)
+    grads[count] = jnp.zeros((half_cols, depth), BF16)
+    own_rows = grads[pl.ds(half_rows * tx, edge_count)].reshape(edge_count * half_cols, depth)
+    moved = lax.dot(own_rows, flat_down[...], preferred_element_type=F32)
+    products[:, 0:half_cols] = moved.reshape(edge_count, half_cols, 9 * 128)
+    moved = lax.dot(edge_grad, flat_down[...], preferred_element_type=F32)
+    products[:, half_cols:] = moved.reshape(edge_count, 8, 9 * 128)
+    combine_fine(products, lambda row: grad[row], fine, in_grad)
+    for row in range(rows):
+        far[row] = relay_choices(value[row], in_grad[row])[1]
     half = up_flat.shape[0] - depth // 2
     lanes = pl.ds(pl.multiple_of(tx * 512, 128), 640)
-    terms = across(reduced, sums[:, 0:half_cols, lanes].reshape(cells, 640))
+    terms = across(reduced, sums[:, :, lanes].reshape(cells, 640))
     for tap in range(5):
         up_flat[tap * depth : tap * depth + depth] = terms[:, tap * 128 : tap * 128 + 128]
     span = 3 * 128
-    outer = across(even_taps[pl.ds(tx, count), 0:half_cols].reshape(cells, span), own_grad)
-    middle = across(odd_taps[0:count, 0:half_cols].reshape(cells, span), own_grad)
+    outer = across(even_taps[pl.ds(tx, count)].reshape(cells, span), coupled)
+    middle = across(odd_taps[0:count].reshape(cells, span), coupled)
     outer_at = pl.multiple_of(tx * (span // 2), 8)
     middle_at = pl.multiple_of((1 - tx) * span, 8)
     middle_half = jnp.where(tx == 0, middle[0 : span // 2], middle[span // 2 : span])
@@ -450,12 +493,8 @@
         target[...] = jnp.concatenate(both, axis=0).astype(target.dtype)
 
 
-def input_grad(grads, down, base, products, fine, target):
+def combine_fine(products, base, fine, target):
     half_rows, half_cols = fine.shape[0] // 2, fine.shape[1] // 2
-    count = half_rows + 1
-    flat = grads.reshape(count * PAD, grads.shape[2])
-    moved = lax.dot(flat, down[...], preferred_element_type=F32)
-    products[...] = moved.reshape(count, PAD, 9 * 128)
 
     def part(p, a, b, offset):
         tap = 3 * a + b
@@ -472,66 +511,147 @@
         target[row] = (base(row).astype(F32) + fine[row]).astype(BF16)
 
 
-def forward_kernel(merged, blocks, *rest):
-    ys, rest = (rest[:1], rest[1:]) if merged else (rest[:2], rest[2:])
-    in_grad, flat_up, flat_down, near, far, field, even_taps, odd_taps, products, mixed, fine = rest
-    ext = blocks if merged else blocks.at[2]
-    rows, wide = ext.shape[0], ext.shape[1]
+def raise_rows(field, even_taps, odd_taps, products, flat_up, flat_down, count, first, valid):
+    spread_taps(field, even_taps, odd_taps, 2 * count + 1, first)
+    pre_down = lower(even_taps, odd_taps, count, flat_down)
+    reduced = pre_down * (0.5 + 0.5 * jnp.tanh(0.5 * pre_down))
+    row, col = places(count, reduced.shape[1])
+    reduced = jnp.where(valid(row, col), reduced, 0.0).astype(BF16)
+    raised = lax.dot(reduced, flat_up[...], preferred_element_type=F32)
+    products[...] = raised.reshape(count, PAD, 9 * 128)
+
+
+def fine_row(products, mixed, target, picks):
+    half_cols = target.shape[0] // 2
+    col = []
+    for b in range(3):
+        terms = [
+            products[q, :, (3 * a + b) * 128 : (3 * a + b) * 128 + 128]
+            for a, q in enumerate(picks)
+            if q is not None
+        ]
+        col.append(sum(terms[1:], terms[0]))
+    mixed[0], mixed[1] = col[0], col[1] + col[2]
+    mixed[2], mixed[3] = col[0] + col[1], col[2]
+    target[pl.ds(0, half_cols, stride=2), :] = mixed[0, 0:half_cols] + mixed[1, 1 : half_cols + 1]
+    target[pl.ds(1, half_cols, stride=2), :] = mixed[2, 1 : half_cols + 1] + mixed[3, 2 : half_cols + 2]
+
+
+def right_edge(half_cols):
+    has_right = lax.axis_index("ty") < lax.axis_size("ty") - 1
+    return lambda row, col: (col <= half_cols) | has_right
+
+
+def relay_choices(value, in_grad):
+    position, segments = lax.axis_index("segment"), lax.axis_size("segment")
+    near = jnp.where(position % 2 == 0, value, in_grad)
+    return near, jnp.where(position < segments // 2, value, in_grad)
+
+
+def forward_kernel(blocks, y0, y1, in_grad, flat_up, flat_down, near, far, *scratch):
+    field, even_taps, odd_taps, products, mixed, fine = scratch
+    rows, wide = blocks.shape[1], blocks.shape[2]
     breadth = wide - 16
     half_rows, half_cols = rows // 2, breadth // 2
-    depth = flat_down.shape[0]
-    tx, ty = lax.axis_index("tx"), lax.axis_index("ty")
-    has_above, has_below = tx > 0, tx < lax.axis_size("tx") - 1
-    has_right = ty < lax.axis_size("ty") - 1
-    position = lax.axis_index("segment")
-    count = half_rows + 2
+    has_below = lax.axis_index("tx") < lax.axis_size("tx") - 1
+    before, after = rims(y0, y1)
     field[:, wide:] = jnp.zeros((field.shape[0], field.shape[1] - wide, 128), F32)
-    if merged:
-        def row_of(k, valid):
-            tiles = [ys[0][9 * k + part].astype(F32) for part in range(breadth // 8 + 1)]
-            line = jnp.concatenate([tiles[-1]] + tiles, axis=0)
-            return jnp.where(valid, line, 0.0)
-
-        before, after = (lambda k: row_of(k, has_above)), (lambda k: row_of(k, has_below))
-        top, bottom = 0, 0
-    else:
-        before, after = rims(*ys)
-        top, bottom = 2, 5
     for k in range(3):
-        field[k, 0:wide] = before(top + k)
+        field[k, 0:wide] = before(2 + k)
     for row in range(rows):
-        field[row + 3, 0:wide] = ext[row].astype(F32)
+        field[row + 3, 0:wide] = blocks[2, row].astype(F32)
     for k in range(2):
-        field[rows + 3 + k, 0:wide] = after(bottom + k)
-    spread_taps(field, even_taps, odd_taps, 2 * count + 1, LEFT - 3)
-    pre_down = lower(even_taps, odd_taps, count, flat_down)
-    reduced = pre_down / (1.0 + jnp.exp(-pre_down))
-    row_id, col_id = places(count, depth)
-    inside = ((row_id <= half_rows) | has_below) & ((col_id <= half_cols) | has_right)
-    reduced = jnp.where(inside, reduced, 0.0).astype(BF16)
-    raised = lax.dot(reduced, flat_up[...], preferred_element_type=F32)
-    products[...] = raised.reshape(count, PAD, 9 * 128)
-
-    def tap_rows(p, dy, b):
-        at = lambda q, a: products[q, :, (3 * a + b) * 128 : (3 * a + b) * 128 + 128]
-        if dy == 0:
-            return at(p, 0) + at(p + 1, 1) + at(p + 1, 2)
-        return at(p + 1, 0) + at(p + 1, 1) + at(p + 2, 2)
-
+        field[rows + 3 + k, 0:wide] = after(5 + k)
+    edge = right_edge(half_cols)
+    valid = lambda row, col: ((row <= half_rows) | has_below) & edge(row, col)
+    raise_rows(field, even_taps, odd_taps, products, flat_up, flat_down, half_rows + 2, LEFT - 3, valid)
     for p in range(half_rows):
-        for dy in range(2):
-            col = [tap_rows(p, dy, b) for b in range(3)]
-            mixed[0, 0:PAD], mixed[1, 0:PAD] = col[0], col[1] + col[2]
-            mixed[2, 0:PAD], mixed[3, 0:PAD] = col[0] + col[1], col[2]
-            line = 2 * p + dy
-            fine[line, pl.ds(0, half_cols, stride=2), :] = mixed[0, 0:half_cols] + mixed[1, 1 : half_cols + 1]
-            fine[line, pl.ds(1, half_cols, stride=2), :] = (
-                mixed[2, 1 : half_cols + 1] + mixed[3, 2 : half_cols + 2]
-            )
+        fine_row(products, mixed, fine.at[2 * p], (p, p + 1, p + 1))
+        fine_row(products, mixed, fine.at[2 * p + 1], (p + 1, p + 1, p + 2))
     for row in range(rows):
-        value = (ext[row, LEFT : LEFT + breadth].astype(F32) + fine[row]).astype(BF16)
-        near[row] = jnp.where(position % 2 == 0, value, in_grad[row])
-        far[row] = jnp.where(position < lax.axis_size("segment") // 2, value, in_grad[row])
+        value = (blocks[2, row, LEFT : LEFT + breadth].astype(F32) + fine[row]).astype(BF16)
+        near[row], far[row] = relay_choices(value, in_grad[row])
+
+
+def inner_kernel(blocks, flat_up, flat_down, value, *scratch):
+    field, even_taps, odd_taps, products, mixed, fine = scratch
+    rows, wide = blocks.shape[0], blocks.shape[1]
+    breadth = wide - 16
+    half_rows, half_cols = rows // 2, breadth // 2
+    field[:, wide:] = jnp.zeros((field.shape[0], field.shape[1] - wide, 128), F32)
+    field[0, 0:wide] = jnp.zeros((wide, 128), F32)
+    for row in range(rows):
+        field[row + 1, 0:wide] = blocks[row].astype(F32)
+    edge = right_edge(half_cols)
+    raise_rows(field, even_taps, odd_taps, products, flat_up, flat_down, half_rows, LEFT - 3, edge)
+    for p in range(half_rows):
+        fine_row(products, mixed, fine.at[2 * p], (p - 1 if p else None, p, p))
+        below = p + 1 if p + 1 < half_rows else None
+        fine_row(products, mixed, fine.at[2 * p + 1], (p, p, below))
+    for row in range(rows):
+        value[row] = (blocks[row, LEFT : LEFT + breadth].astype(F32) + fine[row]).astype(BF16)
+
+
+def border_kernel(blocks, y0, value, in_grad, flat_up, flat_down, near, strip, *scratch):
+    field, even_taps, odd_taps, products, mixed, fine = scratch
+    rows, wide = blocks.shape[0], blocks.shape[1]
+    breadth = wide - 16
+    half_cols = breadth // 2
+    upper = lax.axis_index("tx") == 0
+    field[:, wide:] = jnp.zeros((field.shape[0], field.shape[1] - wide, 128), F32)
+
+    def far_row(k):
+        tiles = [y0[(breadth // 8 + 1) * k + part].astype(F32) for part in range(breadth // 8 + 1)]
+        return jnp.concatenate([tiles[-1]] + tiles, axis=0)
+
+    own = lambda row: blocks[row].astype(F32)
+    for k in range(7):
+        lower_tile = far_row(k) if k < 3 else own(k - 3)
+        upper_tile = own(rows - 5 + k) if k < 5 else far_row(k - 5)
+        field[k, 0:wide] = jnp.where(upper, upper_tile, lower_tile)
+    edge = right_edge(half_cols)
+    raise_rows(field, even_taps, odd_taps, products, flat_up, flat_down, 3, LEFT - 3, edge)
+    fine_row(products, mixed, fine.at[0], (0, 1, 1))
+    fine_row(products, mixed, fine.at[1], (1, 1, 2))
+    fine_row(products, mixed, fine.at[2], (1, 2, 2))
+    repaired = [None] * 3
+    for k in range(3):
+        base = jnp.where(upper, own(rows - 3 + k), own(k))[LEFT : LEFT + breadth]
+        added = jnp.where(upper, fine[max(k - 1, 0)], fine[k])
+        repaired[k] = (base + added).astype(BF16)
+        if k == 0:
+            repaired[k] = jnp.where(upper, value[rows - 3], repaired[k])
+        strip[k] = relay_choices(repaired[k], jnp.where(upper, in_grad[rows - 3 + k], in_grad[k]))[1]
+    for row in range(rows):
+        result = value[row]
+        if row < 3:
+            result = jnp.where(upper, result, repaired[row])
+        if row >= rows - 3:
+            result = jnp.where(upper, repaired[row - (rows - 3)], result)
+        near[row] = relay_choices(result, in_grad[row])[0]
+
+
+def final_kernel(
+    scaling, near, far, strip, own, first, second, third, act_out, grad_out, partner_out, up_sum, down_sum
+):
+    rows = near.shape[0]
+    position, segments = lax.axis_index("segment"), lax.axis_size("segment")
+    upper = lax.axis_index("tx") == 0
+    odd = position % 2 == 1
+    for row in range(rows):
+        from_far = far[row]
+        if row < 3:
+            from_far = jnp.where(upper, from_far, strip[row])
+        if row >= rows - 3:
+            from_far = jnp.where(upper, strip[row - (rows - 3)], from_far)
+        blank = jnp.zeros_like(from_far)
+        partner_out[0, row] = from_far
+        act_out[0, row] = jnp.where(position == 0, blank, jnp.where(odd, near[row], from_far))
+        grad_out[0, row] = jnp.where(position == segments - 1, blank, jnp.where(odd, from_far, near[row]))
+    total = own[...] + first[...].astype(F32) + second[...].astype(F32) + third[...].astype(F32)
+    piece = up_sum.shape[0]
+    up_sum[...] = total[0:piece] * scaling
+    down_sum[...] = total[piece:] * scaling
 
 
 def swaps(axis):
@@ -544,13 +664,6 @@
 
 def crossed(axis, distance):
     return [(i, i ^ distance) for i in range(lax.axis_size(axis))]
-
-
-def total_kernel(scaling, own, first, second, third, up_sum, down_sum):
-    total = own[...] + first[...].astype(F32) + second[...].astype(F32) + third[...].astype(F32)
-    piece = up_sum.shape[0]
-    up_sum[...] = total[0:piece] * scaling
-    down_sum[...] = total[piece:] * scaling
 
 
 def shape(dims, kind):
@@ -638,7 +751,7 @@
             (shape((3 * (breadth // 8 + 1), 8, channels), BF16), shape((height, breadth + 16, channels), BF16)),
             [SMEM] * 2 + [VMEM] * len(operands),
             rooms,
-            flops=6_000_000_000,
+            flops=2_000_000_000,
             moved=1000,
         )(owners, nest_cell, *operands)
         ys = [lax.ppermute(pay, "tx", pairs)]
@@ -661,34 +774,44 @@
 
     fine = pltpu.VMEM((height, breadth, channels), F32)
     products = lambda count: pltpu.VMEM((count, PAD, 9 * channels), F32)
+    forward_rooms = lambda count: tap_rooms(count) + [
+        products(count),
+        pltpu.VMEM((4, PAD, channels), F32),
+        fine,
+    ]
     if merged:
+        value = call(
+            inner_kernel,
+            tile,
+            [VMEM] * 3,
+            forward_rooms(half_rows),
+            flops=1_000,
+            moved=1000,
+        )(blocks, flat_up, flat_down)
         piece = rows_flat // (n_tx * n_ty)
         part = shape((2 * piece, channels), BF16)
-        flat_half = rows_flat // 2
-        in_grad, own_sum, *sends = call(
+        far, in_grad, own_sum, *sends = call(
             paired_kernel,
-            (tile, shape((2 * piece, channels), F32), part, part, part),
-            [VMEM] * 8,
-            tap_rooms(height)
-            + [
-                pltpu.VMEM((height, PAD, 9 * channels), BF16),
+            (tile, tile, shape((2 * piece, channels), F32), part, part, part),
+            [VMEM] * 9,
+            [
+                pltpu.VMEM((2 * height + 4, wide, channels), F32),
+                pltpu.VMEM((height + 1, breadth // 2, 3 * channels), BF16),
+                pltpu.VMEM((height, breadth // 2, 3 * channels), BF16),
+                pltpu.VMEM((height, breadth // 2, 9 * channels), BF16),
                 pltpu.VMEM((9 * channels // 2, 128), F32),
                 pltpu.VMEM((9 * channels // 2, 128), F32),
                 pltpu.VMEM((5 * depth, channels), F32),
-                pltpu.VMEM((flat_half, channels), F32),
-                pltpu.VMEM((height + 1, PAD, depth), BF16),
-                products(half_rows + 1),
+                pltpu.VMEM((rows_flat // 2, channels), F32),
+                pltpu.VMEM((height + 1, breadth // 2, depth), BF16),
+                pltpu.VMEM((half_rows + 1, breadth // 2 + 8, 9 * channels), F32),
                 fine,
+                pltpu.VMEM((half_rows + 1, 8, 9 * channels), F32),
+                pltpu.VMEM((half_rows + 1, 8, 9 * channels), F32),
             ],
-            flops=900_000_000,
+            flops=5_000_000_000,
             moved=4_000_000,
-        )(stash, grad_own, st_far, grad_far, rim, rim_far, flat_up, flat_down)
-        arrived = [lax.ppermute(sends[d - 1], "ty", crossed("ty", d)) for d in (3, 2, 1)]
-        summed = shape((piece, channels), F32)
-        up_sum, down_sum = call(
-            functools.partial(total_kernel, scaling), (summed, summed), [VMEM] * 4, flops=10_000_000_000
-        )(own_sum, *arrived)
-        up_sum, down_sum = up_sum.reshape(1, -1), down_sum.reshape(1, -1)
+        )(stash, grad_own, st_far, grad_far, rim, rim_far, flat_up, flat_down, value)
     else:
         whole = shape((rows_flat, channels), F32)
         in_grad, up_flat, down_flat = call(
@@ -711,23 +834,48 @@
         )[None]
         down_sum, up_sum = pooled(down_flat), pooled(up_flat)
 
-    count = half_rows + 2
+    mirror = [(i, segments - 1 - i) for i in range(segments)]
+    if merged:
+        ys = passed_on(ys, 2_000_000_000)
+        near, strip = call(
+            border_kernel,
+            (tile, shape((3, breadth, channels), BF16)),
+            [VMEM] * 6,
+            forward_rooms(3),
+            flops=600_000_000,
+            moved=4_000_000,
+        )(blocks, ys[0], value, in_grad, flat_up, flat_down)
+        from_far = lax.ppermute(far, "segment", mirror)
+        from_strip = lax.ppermute(strip, "segment", mirror)
+        from_near = lax.ppermute(near, "segment", crossed("segment", 1))
+        arrived = [lax.ppermute(sends[d - 1], "ty", crossed("ty", d)) for d in (2, 3, 1)]
+        arrived = passed_on(arrived[:1], 800_000_000) + arrived[1:]
+        (from_far,) = passed_on([from_far], 100_000_000, arrived[:1])
+        arrived = arrived[:1] + passed_on(arrived[1:], 3_000_000_000, [from_far])
+        summed = shape((piece, channels), F32)
+        act_out, grad_out, partner_out, up_sum, down_sum = call(
+            functools.partial(final_kernel, scaling),
+            (shape(act_in.shape, BF16),) * 3 + (summed, summed),
+            [VMEM] * 7,
+            flops=1_000,
+            moved=1000,
+        )(from_near, from_far, from_strip, own_sum, *arrived)
+        return act_out, grad_out, partner_out, down_sum.reshape(1, -1), up_sum.reshape(1, -1)
     near, far = call(
-        functools.partial(forward_kernel, merged),
+        forward_kernel,
         (tile, tile),
-        [VMEM] * (4 + len(ys)),
-        tap_rooms(count) + [products(count), pltpu.VMEM((4, PAD, channels), F32), fine],
+        [VMEM] * 6,
+        forward_rooms(half_rows + 2),
         flops=600_000_000,
         moved=4_000_000,
     )(blocks, *ys, in_grad, flat_up, flat_down)
-    from_far = lax.ppermute(far, "segment", [(i, segments - 1 - i) for i in range(segments)])
+    from_far = lax.ppermute(far, "segment", mirror)
     from_near = lax.ppermute(near, "segment", crossed("segment", 1))
     blank = jnp.zeros_like(from_near)
     odd = position % 2 == 1
     act_out = jnp.where(position == 0, blank, jnp.where(odd, from_near, from_far))
     grad_out = jnp.where(position == segments - 1, blank, jnp.where(odd, from_far, from_near))
-    partner_out = jnp.where(position < segments, from_far, blank)
-    return (act_out[None], grad_out[None], partner_out[None], down_sum, up_sum)
+    return (act_out[None], grad_out[None], from_far[None], down_sum, up_sum)
 
 
 def solution(mesh):

time: 37 us -> 33.7 us (0.911)
  waiting for transfers between devices: 10.2 us -> 7.38 us
  other arithmetic: 0.93 us -> 0 us
  Pallas kernels: 9.47 us -> 9.93 us
    ppermute x1, waiting for transfers between devices: 1.82 us -> 0.01 us  [local(): grad_far = lax.ppermute(grad_own, 'tx', crossed('tx', 1))]
    ppermute x1, starting transfers between devices: 1.58 us -> 0.01 us  [local(): from_near = lax.ppermute(near, 'segment', crossed('segment', 1))]
    ppermute x1 -> x2, starting transfers between devices: 0.07 us -> 1.39 us  [the longest x1 1.38 us: local(): from_strip = lax.ppermute(strip, 'segment', mirror)]
    ppermute x1, starting transfers between devices: 0.57 us -> 1.58 us  [local(): rim_far = lax.ppermute(rim, 'tx', pairs)]
    broadcast_in_dim x1 -> x0, other arithmetic: 0.93 us -> none  [local(): return (act_out[None], grad_out[None], partner_out[None], down_sum, up_sum)]
    ppermute x3, starting transfers between devices: 4.45 us -> 3.55 us  [local(): lax.ppermute(sends[d - 1], 'ty', crossed('ty', d))]
    ppermute x1, waiting for transfers between devices: 0.58 us -> 0.01 us  [local(): table_parts = (coarse, lax.ppermute(coarse, 'ty', crossed('ty', 2)))]
    ppermute x1, waiting for transfers between devices: 1.19 us -> 1.69 us  [local(): z1 = lax.ppermute(z_pay1, 'ty', others)]
  transfers between devices with their start and end apart: 12 -> 13, of which waited for: 6 -> 4; matrix products, arithmetic and copies ran while one was open for 0% -> 0% of each run, Pallas kernels for 26% -> 26%
where the time goes in v3:
time: 33.7 us; the launch traced here: 33.5 us
  starting transfers between devices  15.4 us (46%)
  Pallas kernels  9.93 us (29%)
  waiting for transfers between devices  7.38 us (22%)
  between operations  0.74 us (2%)
    ppermute x3, starting transfers between devices, local(): lax.ppermute(sends[d - 1], 'ty', crossed('ty', d))  3.55 us
    ppermute x1, waiting for transfers between devices, local(): from_far = lax.ppermute(far, 'segment', mirror)  3.47 us
    ppermute x1, starting transfers between devices, local(): st_far = lax.ppermute(stashed, 'tx', crossed('tx', 1))  3.03 us
    pallas_call x1, Pallas kernels, local(): call(paired_kernel, (tile, tile, shape((2 * piece, channels), F32), part,...  2.75 us
    ppermute x1, starting transfers between devices, local(): z1 = lax.ppermute(z_pay1, 'ty', others)  2.47 us
    ppermute x3, waiting for transfers between devices, local(): lax.ppermute(sends[d - 1], 'ty', crossed('ty', d))  2.2 us
    ppermute x1, starting transfers between devices, local(): z0 = lax.ppermute(z_pay0, 'ty', pairs)  2.06 us
    ppermute x1, waiting for transfers between devices, local(): z1 = lax.ppermute(z_pay1, 'ty', others)  1.69 us
  transfers between devices with their start and end apart: 13, of which 4 were waited for; matrix products, arithmetic and copies ran while one was open for 0% of the time, Pallas kernels for 26%

profile of v3, /device:TPU:0, one launch (start us, length us, event | category | flops | bytes accessed | tf_op | source)
XLA Modules:
  0.0 33.5 jit_solution(8251433236697832344)
XLA Ops:
  0.6 3.0 %collective-permute-start.4 = (bf16[1,16,64,128]{3,2,1,0:T(8,128)(2,1)}, bf16[1,16,64,128]{3,2,1,0:T(8,128)(2,1)S(1)}, u32[]{:S(2)}, u32[]{:S(2)}) collective-permute-start(bf16[1,16,64,128]{3,2,1,0:T(8,128)(2,1)} %st.3), channel_id=1, source_target_pairs={{0,4},{4,0},{1,5},{5,1},{2,6},{6,2},{3,7},{7,3},{8,12},{12,8},{9,1... | collective-permute-start | bytes 786440 | tf_op jit(solution)/shard_map/ppermute | solution.py:699
  3.7 0.0 copy-start
  3.7 1.3 %shard_map.138 = (bf16[16,64,128]{2,1,0:T(8,128)(2,1)S(1)}, bf16[25,8,128]{2,1,0:T(8,128)(2,1)S(1)}, bf16[25,8,128]{2,1,0:T(8,128)(2,1)S(1)}) custom-call(s32[64]{0:T(128)} %bitcast.7, s32[64]{0:T(128)} %cell.1, s32[4,16]{1,0:T(4,128)} %land_in.1, bf16[1,16,64,128]{3,2,1,0:T(8,128)(2,1)} %act.3, bf16[1,16,64,128]{3,2,1,0:T(8,128)(2,1)} %par.3, ...), custom_call_target="tpu_custom_call" | custom-call | flops 1000 | bytes 1000 | tf_op jit(solution)/shard_map/pallas_call | solution.py:702
  5.0 0.1 collective-permute-start.5
  5.1 2.1 %collective-permute-start = (bf16[25,8,128]{2,1,0:T(8,128)(2,1)S(1)}, bf16[25,8,128]{2,1,0:T(8,128)(2,1)S(1)}, u32[]{:S(2)}, u32[]{:S(2)}) collective-permute-start(bf16[25,8,128]{2,1,0:T(8,128)(2,1)S(1)} %get-tuple-element.30), channel_id=1, source_target_pairs={{0,1},{2,3},{1,0},{3,2},{4,5},{6,7},{5,4},{7,6},{8,9},{10,11},{9,8... | collective-permute-start | bytes 153608 | tf_op jit(solution)/shard_map/ppermute | solution.py:718
  7.1 2.5 %collective-permute-start.1 = (bf16[25,8,128]{2,1,0:T(8,128)(2,1)S(1)}, bf16[25,8,128]{2,1,0:T(8,128)(2,1)S(1)}, u32[]{:S(2)}, u32[]{:S(2)}) collective-permute-start(bf16[25,8,128]{2,1,0:T(8,128)(2,1)S(1)} %get-tuple-element.31), channel_id=1, source_target_pairs={{0,3},{1,2},{2,1},{3,0},{4,7},{5,6},{6,5},{7,4},{8,11},{9,10},{10,... | collective-permute-start | bytes 153608 | tf_op jit(solution)/shard_map/ppermute | solution.py:719
  9.6 0.0 copy-done
  9.6 0.1 collective-permute-start.2
  9.7 1.6 %shard_map.137 = (f32[16,64,128]{2,1,0:T(8,128)S(1)}, bf16[16,64,128]{2,1,0:T(8,128)(2,1)S(1)}, bf16[192,1152]{1,0:T(8,128)(2,1)S(1)}, bf16[192,1152]{1,0:T(8,128)(2,1)S(1)}) custom-call(bf16[1,16,64,128]{3,2,1,0:T(8,128)(2,1)} %act.3, bf16[1,16,64,128]{3,2,1,0:T(8,128)(2,1)} %par.3, bf16[1,16,64,128]{3,2,1,0:T(8,128)(2,1)} %st.3, ...), custom_call_target="tpu_custom_call" | custom-call | flops 1000 | bytes 1000 | tf_op jit(solution)/shard_map/pallas_call | solution.py:726
  11.3 0.0 collective-permute-done.z0
  11.4 1.7 %collective-permute-done.1.z1 = bf16[25,8,128]{2,1,0:T(8,128)(2,1)S(1)} collective-permute-done((bf16[25,8,128]{2,1,0:T(8,128)(2,1)S(1)}, bf16[25,8,128]{2,1,0:T(8,128)(2,1)S(1)}, u32[]{:S(2)}, u32[]{:S(2)}) %collective-permute-start.1) | collective-permute-done | bytes 51232 | tf_op jit(solution)/shard_map/ppermute | solution.py:719
  13.0 0.0 collective-permute-done.4._stash.st_far
  13.1 0.0 copy-start.1
  13.1 0.0 copy-start.2
  13.1 1.6 %collective-permute-start.6 = (bf16[16,8,128]{2,1,0:T(8,128)(2,1)S(1)}, bf16[16,8,128]{2,1,0:T(8,128)(2,1)S(1)}, u32[]{:S(2)}, u32[]{:S(2)}) collective-permute-start(bf16[16,8,128]{2,1,0:T(8,128)(2,1)S(1)} %shard_map.142.rim), channel_id=1, source_target_pairs={{0,4},{4,0},{1,5},{5,1},{2,6},{6,2},{3,7},{7,3},{8,12},{12,8},{9,1... | collective-permute-start | bytes 98312 | tf_op jit(solution)/shard_map/ppermute | solution.py:748
  14.7 0.0 collective-permute-done.2.rest_0_
  14.7 0.0 copy-done.1
  14.7 0.0 copy-done.2
  14.7 0.8 %shard_map.139 = (bf16[27,8,128]{2,1,0:T(8,128)(2,1)S(1)}, bf16[16,80,128]{2,1,0:T(8,128)(2,1)S(1)}) custom-call(s32[64]{0:T(128)S(1)} %bitcast.8, s32[64]{0:T(128)S(1)} %copy-done.2, f32[16,64,128]{2,1,0:T(8,128)S(1)} %get-tuple-element.29.base, bf16[25,8,128]{2,1,0:T(8,128)(2,1)S(1)} %collective-permute-done.z0, ...), custom_call_target="tpu_custom_call" | custom-call | flops 2000000000 | bytes 1000 | tf_op jit(solution)/shard_map/pallas_call | solution.py:749
  15.5 1.1 %collective-permute-start.3 = (bf16[27,8,128]{2,1,0:T(8,128)(2,1)S(1)}, bf16[27,8,128]{2,1,0:T(8,128)(2,1)S(1)}, u32[]{:S(2)}, u32[]{:S(2)}) collective-permute-start(bf16[27,8,128]{2,1,0:T(8,128)(2,1)S(1)} %get-tuple-element.33), channel_id=1, source_target_pairs={{0,4},{4,0},{1,5},{5,1},{2,6},{6,2},{3,7},{7,3},{8,12},{12,8},{9,1... | collective-permute-start | bytes 165896 | tf_op jit(solution)/shard_map/ppermute | solution.py:757
  16.6 1.5 %shard_map.141.value = bf16[16,64,128]{2,1,0:T(8,128)(2,1)S(1)} custom-call(bf16[16,80,128]{2,1,0:T(8,128)(2,1)S(1)} %get-tuple-element.32.blocks, bf16[192,1152]{1,0:T(8,128)(2,1)S(1)} %get-tuple-element.34.flat_up._weights, bf16[192,1152]{1,0:T(8,128)(2,1)S(1)} %get-tuple-element.35.flat_down), custom_call_target="tpu_custom_call" | custom-call | flops 1000 | bytes 1000 | tf_op jit(solution)/shard_map/pallas_call | solution.py:783
  18.1 0.0 collective-permute-done.5.grad_far
  18.1 0.0 collective-permute-done.6.rim_far
  18.1 2.7 %shard_map.143 = (bf16[16,64,128]{2,1,0:T(8,128)(2,1)S(1)}, bf16[16,64,128]{2,1,0:T(8,128)(2,1)S(1)}, f32[432,128]{1,0:T(8,128)S(1)}, bf16[432,128]{1,0:T(8,128)...) custom-call(bf16[16,64,128]{2,1,0:T(8,128)(2,1)S(1)} %get-tuple-element.36.st, ...), custom_call_target="tpu_custom_call" | custom-call | flops 5000000000 | bytes 4000000 | tf_op jit(solution)/shard_map/pallas_call | solution.py:793
  20.9 1.8 %collective-permute-start.9 = (bf16[432,128]{1,0:T(8,128)(2,1)S(1)}, bf16[432,128]{1,0:T(8,128)(2,1)S(1)}, u32[]{:S(2)}, u32[]{:S(2)}) collective-permute-start(bf16[432,128]{1,0:T(8,128)(2,1)S(1)} %get-tuple-element.41), channel_id=1, source_target_pairs={{0,2},{1,3},{2,0},{3,1},{4,6},{5,7},{6,4},{7,5},{8,10},{9,11},{10,... | collective-permute-start | bytes 331784 | tf_op jit(solution)/shard_map/ppermute | solution.py:851
  22.7 0.0 collective-permute-start.8
  22.7 0.0 collective-permute-done.3.refs_0_
  22.7 1.3 %collective-permute-start.11 = (bf16[432,128]{1,0:T(8,128)(2,1)S(1)}, bf16[432,128]{1,0:T(8,128)(2,1)S(1)}, u32[]{:S(2)}, u32[]{:S(2)}) collective-permute-start(bf16[432,128]{1,0:T(8,128)(2,1)S(1)} %get-tuple-element.44), channel_id=1, source_target_pairs={{0,3},{1,2},{2,1},{3,0},{4,7},{5,6},{6,5},{7,4},{8,11},{9,10},{10,... | collective-permute-start | bytes 331784 | tf_op jit(solution)/shard_map/ppermute | solution.py:851
  24.1 0.4 %collective-permute-start.12 = (bf16[432,128]{1,0:T(8,128)(2,1)S(1)}, bf16[432,128]{1,0:T(8,128)(2,1)S(1)}, u32[]{:S(2)}, u32[]{:S(2)}) collective-permute-start(bf16[432,128]{1,0:T(8,128)(2,1)S(1)} %get-tuple-element.45), channel_id=1, source_target_pairs={{0,1},{1,0},{2,3},{3,2},{4,5},{5,4},{6,7},{7,6},{8,9},{9,8},{10,11... | collective-permute-start | bytes 331784 | tf_op jit(solution)/shard_map/ppermute | solution.py:851
  24.5 0.8 %shard_map.144 = (bf16[16,64,128]{2,1,0:T(8,128)(2,1)S(1)}, bf16[3,64,128]{2,1,0:T(8,128)(2,1)S(1)}) custom-call(bf16[16,80,128]{2,1,0:T(8,128)(2,1)S(1)} %get-tuple-element.32.blocks, bf16[27,8,128]{2,1,0:T(8,128)(2,1)S(1)} %shard_map.140.y0, bf16[16,64,128]{2,1,0:T(8,128)(2,1)S(1)} %shard_map.141.value, ...), custom_call_target="tpu_custom_call" | custom-call | flops 600000000 | bytes 4000000 | tf_op jit(solution)/shard_map/pallas_call | solution.py:840
  25.3 1.4 %collective-permute-start.10 = (bf16[3,64,128]{2,1,0:T(8,128)(2,1)S(1)}, bf16[3,64,128]{2,1,0:T(8,128)(2,1)S(1)}, u32[]{:S(2)}, u32[]{:S(2)}) collective-permute-start(bf16[3,64,128]{2,1,0:T(8,128)(2,1)S(1)} %get-tuple-element.42), channel_id=1, source_target_pairs={{0,24},{8,16},{16,8},{24,0},{1,25},{9,17},{17,9},{25,1},{2,26},{10... | collective-permute-start | bytes 147464 | tf_op jit(solution)/shard_map/ppermute | solution.py:849
  26.7 1.1 %collective-permute-done.9.refs_0_ = bf16[432,128]{1,0:T(8,128)(2,1)S(1)} collective-permute-done((bf16[432,128]{1,0:T(8,128)(2,1)S(1)}, bf16[432,128]{1,0:T(8,128)(2,1)S(1)}, u32[]{:S(2)}, u32[]{:S(2)}) %collective-permute-start.9) | collective-permute-done | bytes 110624 | tf_op jit(solution)/shard_map/ppermute | solution.py:851
  27.8 0.0 collective-permute-start.7
  27.8 3.5 %collective-permute-done.8.refs_0_ = bf16[16,64,128]{2,1,0:T(8,128)(2,1)S(1)} collective-permute-done((bf16[16,64,128]{2,1,0:T(8,128)(2,1)S(1)}, bf16[16,64,128]{2,1,0:T(8,128)(2,1)S(1)}, u32[]{:S(2)}, u32[]{:S(2)}) %collective-permute-start.8) | collective-permute-done | bytes 262176 | tf_op jit(solution)/shard_map/ppermute | solution.py:848
  31.3 0.0 collective-permute-done.11.refs_0_
  31.3 1.0 %collective-permute-done.12.refs_1_ = bf16[432,128]{1,0:T(8,128)(2,1)S(1)} collective-permute-done((bf16[432,128]{1,0:T(8,128)(2,1)S(1)}, bf16[432,128]{1,0:T(8,128)(2,1)S(1)}, u32[]{:S(2)}, u32[]{:S(2)}) %collective-permute-start.12) | collective-permute-done | bytes 110624 | tf_op jit(solution)/shard_map/ppermute | solution.py:851
  32.3 0.0 collective-permute-done.10.strip
  32.3 0.0 collective-permute-done.7.near
  32.3 1.2 %shard_map.148 = (bf16[1,16,64,128]{3,2,1,0:T(8,128)(2,1)}, bf16[1,16,64,128]{3,2,1,0:T(8,128)(2,1)}, bf16[1,16,64,128]{3,2,1,0:T(8,128)(2,1)}, f32[216,128]{1,0:T(8,128)}, f32[216,128]{1,0:T(8,128)}) custom-call(bf16[16,64,128]{2,1,0:T(8,128)(2,1)S(1)} %collective-permute-done.7.near, bf16[16,64,128]{2,1,0:T(8,128)(2,1)S(1)} %shard_map.146.refs_2_.far, ...), custom_call_target="tpu_custom_call" | custom-call | flops 1000 | bytes 1000 | tf_op jit(solution)/shard_map/pallas_call | solution.py:856
  (5 shorter events, 0.0 us)
Async XLA Ops:
  0.6 12.4 %collective-permute-start.4 = (bf16[1,16,64,128]{3,2,1,0:T(8,128)(2,1)}, bf16[1,16,64,128]{3,2,1,0:T(8,128)(2,1)S(1)}, u32[]{:S(2)}, u32[]{:S(2)}) collective-permute-start(bf16[1,16,64,128]{3,2,1,0:T(8,128)(2,1)} %st.3), channel_id=1, source_target_pairs={{0,4},{4,0},{1,5},{5,1},{2,6},{6,2},{3,7},{7,3},{8,12},{12,8},{9,1... | collective-permute-start | bytes 786440 | tf_op jit(solution)/shard_map/ppermute | solution.py:699
  3.7 5.9 %copy-start = (bf16[64,128]{1,0:T(8,128)(2,1)S(1)}, bf16[64,128]{1,0:T(8,128)(2,1)}, u32[]{:S(2)}) copy-start(bf16[64,128]{1,0:T(8,128)(2,1)} %coarse.3) | copy-start | bytes 49156
  5.0 13.1 %collective-permute-start.5 = (bf16[16,64,128]{2,1,0:T(8,128)(2,1)S(1)}, bf16[16,64,128]{2,1,0:T(8,128)(2,1)S(1)}, u32[]{:S(2)}, u32[]{:S(2)}) collective-permute-start(bf16[16,64,128]{2,1,0:T(8,128)(2,1)S(1)} %get-tuple-element.37.grad), channel_id=1, source_target_pairs={{0,4},{4,0},{1,5},{5,1},{2,6},{6,2},{3,7},{7,3},{8,12},{12,8},{9,1... | collective-permute-start | bytes 786440 | tf_op jit(solution)/shard_map/ppermute | solution.py:717
  5.1 6.3 %collective-permute-start = (bf16[25,8,128]{2,1,0:T(8,128)(2,1)S(1)}, bf16[25,8,128]{2,1,0:T(8,128)(2,1)S(1)}, u32[]{:S(2)}, u32[]{:S(2)}) collective-permute-start(bf16[25,8,128]{2,1,0:T(8,128)(2,1)S(1)} %get-tuple-element.30), channel_id=1, source_target_pairs={{0,1},{2,3},{1,0},{3,2},{4,5},{6,7},{5,4},{7,6},{8,9},{10,11},{9,8... | collective-permute-start | bytes 153608 | tf_op jit(solution)/shard_map/ppermute | solution.py:718
  7.1 5.9 %collective-permute-start.1 = (bf16[25,8,128]{2,1,0:T(8,128)(2,1)S(1)}, bf16[25,8,128]{2,1,0:T(8,128)(2,1)S(1)}, u32[]{:S(2)}, u32[]{:S(2)}) collective-permute-start(bf16[25,8,128]{2,1,0:T(8,128)(2,1)S(1)} %get-tuple-element.31), channel_id=1, source_target_pairs={{0,3},{1,2},{2,1},{3,0},{4,7},{5,6},{6,5},{7,4},{8,11},{9,10},{10,... | collective-permute-start | bytes 153608 | tf_op jit(solution)/shard_map/ppermute | solution.py:719
  9.6 5.1 %collective-permute-start.2 = (bf16[64,128]{1,0:T(8,128)(2,1)S(1)}, bf16[64,128]{1,0:T(8,128)(2,1)S(1)}, u32[]{:S(2)}, u32[]{:S(2)}) collective-permute-start(bf16[64,128]{1,0:T(8,128)(2,1)S(1)} %copy-done), channel_id=1, source_target_pairs={{0,2},{1,3},{2,0},{3,1},{4,6},{5,7},{6,4},{7,5},{8,10},{9,11},{10,... | collective-permute-start | bytes 49160 | tf_op jit(solution)/shard_map/ppermute | solution.py:721
  13.1 1.6 %copy-start.1 = (s32[64,1]{0,1:T(1,128)S(1)}, s32[64,1]{0,1:T(1,128)}, u32[]{:S(2)}) copy-start(s32[64,1]{0,1:T(1,128)} %param.17) | copy-start | bytes 772
  13.1 1.6 %copy-start.2 = (s32[64]{0:T(128)S(1)}, s32[64]{0:T(128)}, u32[]{:S(2)}) copy-start(s32[64]{0:T(128)} %cell.1) | copy-start | bytes 772
  13.1 5.0 %collective-permute-start.6 = (bf16[16,8,128]{2,1,0:T(8,128)(2,1)S(1)}, bf16[16,8,128]{2,1,0:T(8,128)(2,1)S(1)}, u32[]{:S(2)}, u32[]{:S(2)}) collective-permute-start(bf16[16,8,128]{2,1,0:T(8,128)(2,1)S(1)} %shard_map.142.rim), channel_id=1, source_target_pairs={{0,4},{4,0},{1,5},{5,1},{2,6},{6,2},{3,7},{7,3},{8,12},{12,8},{9,1... | collective-permute-start | bytes 98312 | tf_op jit(solution)/shard_map/ppermute | solution.py:748
  15.5 7.2 %collective-permute-start.3 = (bf16[27,8,128]{2,1,0:T(8,128)(2,1)S(1)}, bf16[27,8,128]{2,1,0:T(8,128)(2,1)S(1)}, u32[]{:S(2)}, u32[]{:S(2)}) collective-permute-start(bf16[27,8,128]{2,1,0:T(8,128)(2,1)S(1)} %get-tuple-element.33), channel_id=1, source_target_pairs={{0,4},{4,0},{1,5},{5,1},{2,6},{6,2},{3,7},{7,3},{8,12},{12,8},{9,1... | collective-permute-start | bytes 165896 | tf_op jit(solution)/shard_map/ppermute | solution.py:757
  20.9 6.9 %collective-permute-start.9 = (bf16[432,128]{1,0:T(8,128)(2,1)S(1)}, bf16[432,128]{1,0:T(8,128)(2,1)S(1)}, u32[]{:S(2)}, u32[]{:S(2)}) collective-permute-start(bf16[432,128]{1,0:T(8,128)(2,1)S(1)} %get-tuple-element.41), channel_id=1, source_target_pairs={{0,2},{1,3},{2,0},{3,1},{4,6},{5,7},{6,4},{7,5},{8,10},{9,11},{10,... | collective-permute-start | bytes 331784 | tf_op jit(solution)/shard_map/ppermute | solution.py:851
  22.7 8.6 %collective-permute-start.8 = (bf16[16,64,128]{2,1,0:T(8,128)(2,1)S(1)}, bf16[16,64,128]{2,1,0:T(8,128)(2,1)S(1)}, u32[]{:S(2)}, u32[]{:S(2)}) collective-permute-start(bf16[16,64,128]{2,1,0:T(8,128)(2,1)S(1)} %get-tuple-element.40), channel_id=1, source_target_pairs={{0,24},{8,16},{16,8},{24,0},{1,25},{9,17},{17,9},{25,1},{2,26},{10... | collective-permute-start | bytes 786440 | tf_op jit(solution)/shard_map/ppermute | solution.py:848
  22.7 8.6 %collective-permute-start.11 = (bf16[432,128]{1,0:T(8,128)(2,1)S(1)}, bf16[432,128]{1,0:T(8,128)(2,1)S(1)}, u32[]{:S(2)}, u32[]{:S(2)}) collective-permute-start(bf16[432,128]{1,0:T(8,128)(2,1)S(1)} %get-tuple-element.44), channel_id=1, source_target_pairs={{0,3},{1,2},{2,1},{3,0},{4,7},{5,6},{6,5},{7,4},{8,11},{9,10},{10,... | collective-permute-start | bytes 331784 | tf_op jit(solution)/shard_map/ppermute | solution.py:851
  24.1 8.3 %collective-permute-start.12 = (bf16[432,128]{1,0:T(8,128)(2,1)S(1)}, bf16[432,128]{1,0:T(8,128)(2,1)S(1)}, u32[]{:S(2)}, u32[]{:S(2)}) collective-permute-start(bf16[432,128]{1,0:T(8,128)(2,1)S(1)} %get-tuple-element.45), channel_id=1, source_target_pairs={{0,1},{1,0},{2,3},{3,2},{4,5},{5,4},{6,7},{7,6},{8,9},{9,8},{10,11... | collective-permute-start | bytes 331784 | tf_op jit(solution)/shard_map/ppermute | solution.py:851
  25.3 7.1 %collective-permute-start.10 = (bf16[3,64,128]{2,1,0:T(8,128)(2,1)S(1)}, bf16[3,64,128]{2,1,0:T(8,128)(2,1)S(1)}, u32[]{:S(2)}, u32[]{:S(2)}) collective-permute-start(bf16[3,64,128]{2,1,0:T(8,128)(2,1)S(1)} %get-tuple-element.42), channel_id=1, source_target_pairs={{0,24},{8,16},{16,8},{24,0},{1,25},{9,17},{17,9},{25,1},{2,26},{10... | collective-permute-start | bytes 147464 | tf_op jit(solution)/shard_map/ppermute | solution.py:849
  27.8 4.5 %collective-permute-start.7 = (bf16[16,64,128]{2,1,0:T(8,128)(2,1)S(1)}, bf16[16,64,128]{2,1,0:T(8,128)(2,1)S(1)}, u32[]{:S(2)}, u32[]{:S(2)}) collective-permute-start(bf16[16,64,128]{2,1,0:T(8,128)(2,1)S(1)} %get-tuple-element.39), channel_id=1, source_target_pairs={{0,8},{8,0},{16,24},{24,16},{1,9},{9,1},{17,25},{25,17},{2,10},{10... | collective-permute-start | bytes 786440 | tf_op jit(solution)/shard_map/ppermute | solution.py:850

commit v4 on v3

--- a/solution.py
+++ b/solution.py
@@ -15,6 +15,7 @@
 HBM = pl.BlockSpec(memory_space=pltpu.HBM)
 LEFT = 8
 PAD = 48
+BORDER = 3
 STRIP_ROWS = 7
 
 
@@ -45,6 +46,17 @@
     )(*arrays, *after))
 
 
+def copies_in_parts(pairs, arrived):
+    copies = []
+    for source, target, parts in pairs:
+        length = source.shape[0] // parts
+        for part in range(parts):
+            rows = pl.ds(part * length, length)
+            views = (source.at[rows], target.at[rows]) if parts > 1 else (source, target)
+            copies.append(pltpu.make_async_copy(*views, arrived.at[len(copies)]))
+    return copies
+
+
 def in_hbm(*operands):
     return [pltpu.with_memory_space_constraint(x, pltpu.HBM) for x in operands]
 
@@ -68,26 +80,22 @@
     act_l, act_r, st_l, st_r, par_v, gr_v, plane, held_v, owner, cell, land, arrived = scratch
     rows, breadth = gr.shape[1], gr.shape[2]
     first, final = pl.ds(0, 16), pl.ds(breadth - 16, 16)
-    copies = [
-        pltpu.make_async_copy(source, target, arrived.at[k])
-        for k, (source, target) in enumerate(
-            (
-                (gr.at[0], gr_v),
-                (par.at[0], par_v),
-                (act.at[0, :, first], act_l),
-                (act.at[0, :, final], act_r),
-                (st.at[0, :, first], st_l),
-                (st.at[0, :, final], st_r),
-                (coarse, held_v),
-                (owner_in, owner),
-                (cell_in, cell),
-                (land_in, land),
-            )
-        )
-    ]
-    for copy in copies:
+    scalars = copies_in_parts(((owner_in, owner, 1), (cell_in, cell, 1), (land_in, land, 1)), arrived)
+    copies = copies_in_parts(
+        (
+            (gr.at[0], gr_v, 1),
+            (par.at[0], par_v, 1),
+            (act.at[0, :, first], act_l, 1),
+            (act.at[0, :, final], act_r, 1),
+            (st.at[0, :, first], st_l, 1),
+            (st.at[0, :, final], st_r, 1),
+            (coarse, held_v, 1),
+        ),
+        arrived.at[pl.ds(3, 13)],
+    )
+    for copy in scalars + copies:
         copy.start()
-    for copy in copies[7:]:
+    for copy in scalars:
         copy.wait()
     decoder, encoder, last = traits()
     groups = rows // 4
@@ -108,7 +116,7 @@
         return tile
 
     left_ids, right_ids = ids(0), ids(per_row - 1)
-    for copy in copies[:7]:
+    for copy in copies:
         copy.wait()
     for row in range(rows):
         grad = gr_v[row].astype(F32) + encoder * par_v[row].astype(F32)
@@ -140,8 +148,8 @@
 
 def prepare_kernel(act, par, st, up, down, base, stash, flat_up, flat_down, *scratch):
     act_v, par_v, up_v, down_v, arrived = scratch
-    pairs = (act.at[0], act_v), (par.at[0], par_v), (up, up_v), (down, down_v), (st.at[0], stash)
-    copies = [pltpu.make_async_copy(*pair, arrived.at[k]) for k, pair in enumerate(pairs)]
+    tiles = (act.at[0], act_v, 1), (par.at[0], par_v, 1), (st.at[0], stash, 1)
+    copies = copies_in_parts(tiles + ((up, up_v, 1), (down, down_v, 1)), arrived)
     for copy in copies:
         copy.start()
     decoder, _, _ = traits()
@@ -402,7 +410,7 @@
     st, grad, st_far, grad_far, rim, rim_far, flat_up, flat_down, value, far, in_grad, *rest
 ):
     own_sum, send1, send2, send3, field, even_taps, odd_taps, sums, d0, d1, up_flat, down_flat = rest[:12]
-    grads, products, fine, edge_taps, edge_sums = rest[12:]
+    grads, products, fine, edge_taps, edge_sums, grad_field = rest[12:]
     rows, breadth = grad.shape[0], grad.shape[1]
     wide = breadth + 16
     count, half_rows, half_cols = rows, rows // 2, breadth // 2
@@ -413,7 +421,7 @@
     has_right = ty < lax.axis_size("ty") - 1
     first_row = rows * tx
 
-    def fill(here_rows, there_rows, turn_before, turn_after):
+    def fill(field, here_rows, there_rows, turn_before, turn_after):
         blank = jnp.zeros((wide, 128), F32)
         field[0, 0:wide] = blank
         field[2 * rows + 1, 0:wide] = blank
@@ -433,39 +441,30 @@
     def full_taps(values, weights):
         return lax.dot_general(values, weights[...], (((1,), (1,)), ((), ())), preferred_element_type=F32)
 
-    edge = lambda row, k: field[first_row + row, pl.ds(LEFT - 1 + k + breadth, 8, stride=2), :]
+    edge = lambda field, row, k: field[first_row + row, pl.ds(LEFT - 1 + k + breadth, 8, stride=2), :]
     flat_edge = lambda ref: ref[...].reshape(edge_count * 8, 9 * 128).astype(BF16)
 
-    field[:, wide:] = jnp.zeros((field.shape[0], field.shape[1] - wide, 128), F32)
-    fill(lambda row: st[row], lambda row: st_far[0, row], 1, 5)
+    for each in (field, grad_field):
+        each[:, wide:] = jnp.zeros((each.shape[0], each.shape[1] - wide, 128), F32)
+    fill(field, lambda row: st[row], lambda row: st_far[0, row], 1, 5)
     spread_taps(field, even_taps, odd_taps, 2 * count + 1, LEFT - 1)
     for p in range(edge_count):
         for tap in range(9):
-            edge_taps[p, :, tap * 128 : tap * 128 + 128] = edge(2 * p + tap // 3, tap % 3)
+            edge_taps[p, :, tap * 128 : tap * 128 + 128] = edge(field, 2 * p + tap // 3, tap % 3)
     pre_back = lower(even_taps, odd_taps, count, flat_down)
     logistic, slope = slopes(pre_back)
     reduced = (pre_back * logistic).astype(BF16)
     edge_slope = slopes(full_taps(flat_edge(edge_taps), flat_down))[1]
 
-    fill(lambda row: grad[row], lambda row: grad_far[row], 0, 0)
-    window_sums(lambda row, k: field[row, pl.ds(LEFT - 1 + k, half_cols, stride=2), :], count, sums)
-    window_sums(edge, edge_count, edge_sums)
+    fill(grad_field, lambda row: grad[row], lambda row: grad_far[row], 0, 0)
+    window_sums(lambda row, k: grad_field[row, pl.ds(LEFT - 1 + k, half_cols, stride=2), :], count, sums)
+    window_sums(lambda row, k: edge(grad_field, row, k), edge_count, edge_sums)
     depth = reduced.shape[1]
     coupled = (full_taps(sums[...].reshape(cells, 9 * 128), flat_up) * slope).astype(BF16)
     edge_shape = (edge_count, 8, depth)
     row = lax.broadcasted_iota(jnp.int32, edge_shape, 0).reshape(edge_count * 8, depth)
     inside = has_right & ((row < half_rows) | has_below)
     edge_grad = jnp.where(inside, full_taps(flat_edge(edge_sums), flat_up) * edge_slope, 0.0).astype(BF16)
-    grads[0:count] = coupled.reshape(count, half_cols, depth)
-    grads[count] = jnp.zeros((half_cols, depth), BF16)
-    own_rows = grads[pl.ds(half_rows * tx, edge_count)].reshape(edge_count * half_cols, depth)
-    moved = lax.dot(own_rows, flat_down[...], preferred_element_type=F32)
-    products[:, 0:half_cols] = moved.reshape(edge_count, half_cols, 9 * 128)
-    moved = lax.dot(edge_grad, flat_down[...], preferred_element_type=F32)
-    products[:, half_cols:] = moved.reshape(edge_count, 8, 9 * 128)
-    combine_fine(products, lambda row: grad[row], fine, in_grad)
-    for row in range(rows):
-        far[row] = relay_choices(value[row], in_grad[row])[1]
     half = up_flat.shape[0] - depth // 2
     lanes = pl.ds(pl.multiple_of(tx * 512, 128), 640)
     terms = across(reduced, sums[:, :, lanes].reshape(cells, 640))
@@ -491,6 +490,17 @@
             down_flat[pl.ds(pl.multiple_of(place, 8), piece)],
         ]
         target[...] = jnp.concatenate(both, axis=0).astype(target.dtype)
+    grads[0:count] = coupled.reshape(count, half_cols, depth)
+    grads[count] = jnp.zeros((half_cols, depth), BF16)
+    own_rows = grads[pl.ds(half_rows * tx, edge_count)].reshape(edge_count * half_cols, depth)
+    moved = lax.dot(own_rows, flat_down[...], preferred_element_type=F32)
+    products[:, 0:half_cols] = moved.reshape(edge_count, half_cols, 9 * 128)
+    moved = lax.dot(edge_grad, flat_down[...], preferred_element_type=F32)
+    products[:, half_cols:] = moved.reshape(edge_count, 8, 9 * 128)
+    combine_fine(products, lambda row: grad[row], fine, in_grad)
+    for row in range(far.shape[0]):
+        here = row + (rows - far.shape[0]) * tx
+        far[row] = relay_choices(value[here], in_grad[here])[1]
 
 
 def combine_fine(products, base, fine, target):
@@ -634,20 +644,18 @@
 def final_kernel(
     scaling, near, far, strip, own, first, second, third, act_out, grad_out, partner_out, up_sum, down_sum
 ):
-    rows = near.shape[0]
-    position, segments = lax.axis_index("segment"), lax.axis_size("segment")
+    rows, border = near.shape[0], strip.shape[0]
+    position, last = lax.axis_index("segment"), lax.axis_size("segment") - 1
     upper = lax.axis_index("tx") == 0
     odd = position % 2 == 1
     for row in range(rows):
-        from_far = far[row]
-        if row < 3:
-            from_far = jnp.where(upper, from_far, strip[row])
-        if row >= rows - 3:
-            from_far = jnp.where(upper, strip[row - (rows - 3)], from_far)
+        from_upper = far[row] if row < rows - border else strip[row - (rows - border)]
+        from_lower = strip[row] if row < border else far[row - border]
+        from_far = jnp.where(upper, from_upper, from_lower)
         blank = jnp.zeros_like(from_far)
         partner_out[0, row] = from_far
         act_out[0, row] = jnp.where(position == 0, blank, jnp.where(odd, near[row], from_far))
-        grad_out[0, row] = jnp.where(position == segments - 1, blank, jnp.where(odd, from_far, near[row]))
+        grad_out[0, row] = jnp.where(position == last, blank, jnp.where(odd, from_far, near[row]))
     total = own[...] + first[...].astype(F32) + second[...].astype(F32) + third[...].astype(F32)
     piece = up_sum.shape[0]
     up_sum[...] = total[0:piece] * scaling
@@ -707,7 +715,7 @@
         + [full] * 2
         + [pltpu.VMEM((height // 4, breadth, channels), F32), pltpu.VMEM(coarse.shape, BF16)]
         + [pltpu.SMEM(scalars.shape, jnp.int32) for scalars in (owners, nest_cell, land_weight)]
-        + [pltpu.SemaphoreType.DMA((10,))],
+        + [pltpu.SemaphoreType.DMA((16,))],
         flops=1000,
         moved=1000,
     )(*in_hbm(owners, nest_cell, land_weight, act_in, partner_in, stashed, grad_in, coarse))
@@ -727,7 +735,7 @@
         prepare_kernel,
         (shape((height, breadth, channels), F32), tile, flat, flat),
         [HBM] * 5,
-        [full, full, taps_room, taps_room, pltpu.SemaphoreType.DMA((5,))],
+        [full, full, taps_room, taps_room, pltpu.SemaphoreType.DMA((30,))],
         flops=1000,
         moved=1000,
     )(*in_hbm(act_in, partner_in, stashed, up_taps, down_taps))
@@ -792,7 +800,7 @@
         part = shape((2 * piece, channels), BF16)
         far, in_grad, own_sum, *sends = call(
             paired_kernel,
-            (tile, tile, shape((2 * piece, channels), F32), part, part, part),
+            (shape((height - BORDER, breadth, channels), BF16), tile, shape((2 * piece, channels), F32), part, part, part),
             [VMEM] * 9,
             [
                 pltpu.VMEM((2 * height + 4, wide, channels), F32),
@@ -808,6 +816,7 @@
                 fine,
                 pltpu.VMEM((half_rows + 1, 8, 9 * channels), F32),
                 pltpu.VMEM((half_rows + 1, 8, 9 * channels), F32),
+                pltpu.VMEM((2 * height + 4, wide, channels), F32),
             ],
             flops=5_000_000_000,
             moved=4_000_000,
@@ -839,7 +848,7 @@
         ys = passed_on(ys, 2_000_000_000)
         near, strip = call(
             border_kernel,
-            (tile, shape((3, breadth, channels), BF16)),
+            (tile, shape((BORDER, breadth, channels), BF16)),
             [VMEM] * 6,
             forward_rooms(3),
             flops=600_000_000,
@@ -848,7 +857,7 @@
         from_far = lax.ppermute(far, "segment", mirror)
         from_strip = lax.ppermute(strip, "segment", mirror)
         from_near = lax.ppermute(near, "segment", crossed("segment", 1))
-        arrived = [lax.ppermute(sends[d - 1], "ty", crossed("ty", d)) for d in (2, 3, 1)]
+        arrived = [lax.ppermute(sends[d - 1], "ty", crossed("ty", d)) for d in (2, 1, 3)]
         arrived = passed_on(arrived[:1], 800_000_000) + arrived[1:]
         (from_far,) = passed_on([from_far], 100_000_000, arrived[:1])
         arrived = arrived[:1] + passed_on(arrived[1:], 3_000_000_000, [from_far])

time: 33.7 us -> 33 us (0.979)
  waiting for transfers between devices: 7.38 us -> 5.88 us
  starting transfers between devices: 15.4 us -> 16.2 us
    ppermute x1, waiting for transfers between devices: 3.47 us -> 2.27 us  [local(): from_far = lax.ppermute(far, 'segment', mirror)]
    ppermute x3, starting transfers between devices: 3.55 us -> 4.45 us  [local(): lax.ppermute(sends[d - 1], 'ty', crossed('ty', d))]
  transfers between devices with their start and end apart: 13 -> 13, of which waited for: 4 -> 4; matrix products, arithmetic and copies ran while one was open for 0% -> 0% of each run, Pallas kernels for 26% -> 27%
where the time goes in v4:
time: 33 us; the launch traced here: 32.8 us
  starting transfers between devices  16.2 us (49%)
  Pallas kernels  9.94 us (30%)
  waiting for transfers between devices  5.88 us (18%)
  between operations  0.74 us (2%)
    ppermute x3, starting transfers between devices, local(): lax.ppermute(sends[d - 1], 'ty', crossed('ty', d))  4.45 us
    ppermute x1, starting transfers between devices, local(): st_far = lax.ppermute(stashed, 'tx', crossed('tx', 1))  3.03 us
    pallas_call x1, Pallas kernels, local(): call(paired_kernel, (shape((height - BORDER, breadth, channels), BF16), t...  2.49 us
    ppermute x1, starting transfers between devices, local(): z1 = lax.ppermute(z_pay1, 'ty', others)  2.47 us
    ppermute x1, waiting for transfers between devices, local(): from_far = lax.ppermute(far, 'segment', mirror)  2.27 us
    ppermute x3, waiting for transfers between devices, local(): lax.ppermute(sends[d - 1], 'ty', crossed('ty', d))  2.12 us
    ppermute x1, starting transfers between devices, local(): z0 = lax.ppermute(z_pay0, 'ty', pairs)  2.06 us
    pallas_call x1, Pallas kernels, local(): call(prepare_kernel, (shape((height, breadth, channels), F32), tile, flat...  1.84 us
  transfers between devices with their start and end apart: 13, of which 4 were waited for; matrix products, arithmetic and copies ran while one was open for 0% of the time, Pallas kernels for 27%

profile of v4, /device:TPU:0, one launch (start us, length us, event | category | flops | bytes accessed | tf_op | source)
XLA Modules:
  0.0 32.8 jit_solution(3485478034280770374)
XLA Ops:
  0.6 3.0 %collective-permute-start.4 = (bf16[1,16,64,128]{3,2,1,0:T(8,128)(2,1)}, bf16[1,16,64,128]{3,2,1,0:T(8,128)(2,1)S(1)}, u32[]{:S(2)}, u32[]{:S(2)}) collective-permute-start(bf16[1,16,64,128]{3,2,1,0:T(8,128)(2,1)} %st.3), channel_id=1, source_target_pairs={{0,4},{4,0},{1,5},{5,1},{2,6},{6,2},{3,7},{7,3},{8,12},{12,8},{9,1... | collective-permute-start | bytes 786440 | tf_op jit(solution)/shard_map/ppermute | solution.py:707
  3.7 0.0 copy-start
  3.7 1.4 %shard_map.138 = (bf16[16,64,128]{2,1,0:T(8,128)(2,1)S(1)}, bf16[25,8,128]{2,1,0:T(8,128)(2,1)S(1)}, bf16[25,8,128]{2,1,0:T(8,128)(2,1)S(1)}) custom-call(s32[64]{0:T(128)} %bitcast.7, s32[64]{0:T(128)} %cell.1, s32[4,16]{1,0:T(4,128)} %land_in.1, bf16[1,16,64,128]{3,2,1,0:T(8,128)(2,1)} %act.3, bf16[1,16,64,128]{3,2,1,0:T(8,128)(2,1)} %par.3, ...), custom_call_target="tpu_custom_call" | custom-call | flops 1000 | bytes 1000 | tf_op jit(solution)/shard_map/pallas_call | solution.py:710
  5.0 0.1 collective-permute-start.5
  5.1 2.1 %collective-permute-start = (bf16[25,8,128]{2,1,0:T(8,128)(2,1)S(1)}, bf16[25,8,128]{2,1,0:T(8,128)(2,1)S(1)}, u32[]{:S(2)}, u32[]{:S(2)}) collective-permute-start(bf16[25,8,128]{2,1,0:T(8,128)(2,1)S(1)} %get-tuple-element.30), channel_id=1, source_target_pairs={{0,1},{2,3},{1,0},{3,2},{4,5},{6,7},{5,4},{7,6},{8,9},{10,11},{9,8... | collective-permute-start | bytes 153608 | tf_op jit(solution)/shard_map/ppermute | solution.py:726
  7.2 2.5 %collective-permute-start.1 = (bf16[25,8,128]{2,1,0:T(8,128)(2,1)S(1)}, bf16[25,8,128]{2,1,0:T(8,128)(2,1)S(1)}, u32[]{:S(2)}, u32[]{:S(2)}) collective-permute-start(bf16[25,8,128]{2,1,0:T(8,128)(2,1)S(1)} %get-tuple-element.31), channel_id=1, source_target_pairs={{0,3},{1,2},{2,1},{3,0},{4,7},{5,6},{6,5},{7,4},{8,11},{9,10},{10,... | collective-permute-start | bytes 153608 | tf_op jit(solution)/shard_map/ppermute | solution.py:727
  9.7 0.0 copy-done
  9.7 0.1 collective-permute-start.2
  9.8 1.8 %shard_map.137 = (f32[16,64,128]{2,1,0:T(8,128)S(1)}, bf16[16,64,128]{2,1,0:T(8,128)(2,1)S(1)}, bf16[192,1152]{1,0:T(8,128)(2,1)S(1)}, bf16[192,1152]{1,0:T(8,128)(2,1)S(1)}) custom-call(bf16[1,16,64,128]{3,2,1,0:T(8,128)(2,1)} %act.3, bf16[1,16,64,128]{3,2,1,0:T(8,128)(2,1)} %par.3, bf16[1,16,64,128]{3,2,1,0:T(8,128)(2,1)} %st.3, ...), custom_call_target="tpu_custom_call" | custom-call | flops 1000 | bytes 1000 | tf_op jit(solution)/shard_map/pallas_call | solution.py:734
  11.6 0.0 collective-permute-done.z0
  11.6 1.5 %collective-permute-done.1.z1 = bf16[25,8,128]{2,1,0:T(8,128)(2,1)S(1)} collective-permute-done((bf16[25,8,128]{2,1,0:T(8,128)(2,1)S(1)}, bf16[25,8,128]{2,1,0:T(8,128)(2,1)S(1)}, u32[]{:S(2)}, u32[]{:S(2)}) %collective-permute-start.1) | collective-permute-done | bytes 51232 | tf_op jit(solution)/shard_map/ppermute | solution.py:727
  13.1 0.0 collective-permute-done.4._stash.st_far
  13.1 0.0 copy-start.1
  13.2 0.0 copy-start.2
  13.2 1.6 %collective-permute-start.6 = (bf16[16,8,128]{2,1,0:T(8,128)(2,1)S(1)}, bf16[16,8,128]{2,1,0:T(8,128)(2,1)S(1)}, u32[]{:S(2)}, u32[]{:S(2)}) collective-permute-start(bf16[16,8,128]{2,1,0:T(8,128)(2,1)S(1)} %shard_map.142.rim), channel_id=1, source_target_pairs={{0,4},{4,0},{1,5},{5,1},{2,6},{6,2},{3,7},{7,3},{8,12},{12,8},{9,1... | collective-permute-start | bytes 98312 | tf_op jit(solution)/shard_map/ppermute | solution.py:756
  14.8 0.0 collective-permute-done.2.rest_0_
  14.8 0.0 copy-done.1
  14.8 0.0 copy-done.2
  14.8 0.8 %shard_map.139 = (bf16[27,8,128]{2,1,0:T(8,128)(2,1)S(1)}, bf16[16,80,128]{2,1,0:T(8,128)(2,1)S(1)}) custom-call(s32[64]{0:T(128)S(1)} %bitcast.8, s32[64]{0:T(128)S(1)} %copy-done.2, f32[16,64,128]{2,1,0:T(8,128)S(1)} %get-tuple-element.29.base, bf16[25,8,128]{2,1,0:T(8,128)(2,1)S(1)} %collective-permute-done.z0, ...), custom_call_target="tpu_custom_call" | custom-call | flops 2000000000 | bytes 1000 | tf_op jit(solution)/shard_map/pallas_call | solution.py:757
  15.5 1.1 %collective-permute-start.3 = (bf16[27,8,128]{2,1,0:T(8,128)(2,1)S(1)}, bf16[27,8,128]{2,1,0:T(8,128)(2,1)S(1)}, u32[]{:S(2)}, u32[]{:S(2)}) collective-permute-start(bf16[27,8,128]{2,1,0:T(8,128)(2,1)S(1)} %get-tuple-element.33), channel_id=1, source_target_pairs={{0,4},{4,0},{1,5},{5,1},{2,6},{6,2},{3,7},{7,3},{8,12},{12,8},{9,1... | collective-permute-start | bytes 165896 | tf_op jit(solution)/shard_map/ppermute | solution.py:765
  16.7 1.5 %shard_map.141.value = bf16[16,64,128]{2,1,0:T(8,128)(2,1)S(1)} custom-call(bf16[16,80,128]{2,1,0:T(8,128)(2,1)S(1)} %get-tuple-element.32.blocks, bf16[192,1152]{1,0:T(8,128)(2,1)S(1)} %get-tuple-element.34.flat_up._weights, bf16[192,1152]{1,0:T(8,128)(2,1)S(1)} %get-tuple-element.35.flat_down), custom_call_target="tpu_custom_call" | custom-call | flops 1000 | bytes 1000 | tf_op jit(solution)/shard_map/pallas_call | solution.py:791
  18.2 0.0 collective-permute-done.5.grad_far
  18.2 0.0 collective-permute-done.6.rim_far
  18.2 2.5 %shard_map.143 = (bf16[13,64,128]{2,1,0:T(8,128)(2,1)S(1)}, bf16[16,64,128]{2,1,0:T(8,128)(2,1)S(1)}, f32[432,128]{1,0:T(8,128)S(1)}, bf16[432,128]{1,0:T(8,128)...) custom-call(bf16[16,64,128]{2,1,0:T(8,128)(2,1)S(1)} %get-tuple-element.36.st, ...), custom_call_target="tpu_custom_call" | custom-call | flops 5000000000 | bytes 4000000 | tf_op jit(solution)/shard_map/pallas_call | solution.py:801
  20.7 1.8 %collective-permute-start.9 = (bf16[432,128]{1,0:T(8,128)(2,1)S(1)}, bf16[432,128]{1,0:T(8,128)(2,1)S(1)}, u32[]{:S(2)}, u32[]{:S(2)}) collective-permute-start(bf16[432,128]{1,0:T(8,128)(2,1)S(1)} %get-tuple-element.41), channel_id=1, source_target_pairs={{0,2},{1,3},{2,0},{3,1},{4,6},{5,7},{6,4},{7,5},{8,10},{9,11},{10,... | collective-permute-start | bytes 331784 | tf_op jit(solution)/shard_map/ppermute | solution.py:860
  22.5 0.0 collective-permute-start.8
  22.5 0.0 collective-permute-done.3.refs_0_
  22.5 1.6 %collective-permute-start.11 = (bf16[432,128]{1,0:T(8,128)(2,1)S(1)}, bf16[432,128]{1,0:T(8,128)(2,1)S(1)}, u32[]{:S(2)}, u32[]{:S(2)}) collective-permute-start(bf16[432,128]{1,0:T(8,128)(2,1)S(1)} %get-tuple-element.44), channel_id=1, source_target_pairs={{0,1},{1,0},{2,3},{3,2},{4,5},{5,4},{6,7},{7,6},{8,9},{9,8},{10,11... | collective-permute-start | bytes 331784 | tf_op jit(solution)/shard_map/ppermute | solution.py:860
  24.0 1.1 %collective-permute-start.12 = (bf16[432,128]{1,0:T(8,128)(2,1)S(1)}, bf16[432,128]{1,0:T(8,128)(2,1)S(1)}, u32[]{:S(2)}, u32[]{:S(2)}) collective-permute-start(bf16[432,128]{1,0:T(8,128)(2,1)S(1)} %get-tuple-element.45), channel_id=1, source_target_pairs={{0,3},{1,2},{2,1},{3,0},{4,7},{5,6},{6,5},{7,4},{8,11},{9,10},{10,... | collective-permute-start | bytes 331784 | tf_op jit(solution)/shard_map/ppermute | solution.py:860
  25.2 0.8 %shard_map.144 = (bf16[16,64,128]{2,1,0:T(8,128)(2,1)S(1)}, bf16[3,64,128]{2,1,0:T(8,128)(2,1)S(1)}) custom-call(bf16[16,80,128]{2,1,0:T(8,128)(2,1)S(1)} %get-tuple-element.32.blocks, bf16[27,8,128]{2,1,0:T(8,128)(2,1)S(1)} %shard_map.140.y0, bf16[16,64,128]{2,1,0:T(8,128)(2,1)S(1)} %shard_map.141.value, ...), custom_call_target="tpu_custom_call" | custom-call | flops 600000000 | bytes 4000000 | tf_op jit(solution)/shard_map/pallas_call | solution.py:849
  26.0 1.2 %collective-permute-start.10 = (bf16[3,64,128]{2,1,0:T(8,128)(2,1)S(1)}, bf16[3,64,128]{2,1,0:T(8,128)(2,1)S(1)}, u32[]{:S(2)}, u32[]{:S(2)}) collective-permute-start(bf16[3,64,128]{2,1,0:T(8,128)(2,1)S(1)} %get-tuple-element.42), channel_id=1, source_target_pairs={{0,24},{8,16},{16,8},{24,0},{1,25},{9,17},{17,9},{25,1},{2,26},{10... | collective-permute-start | bytes 147464 | tf_op jit(solution)/shard_map/ppermute | solution.py:858
  27.2 0.5 %collective-permute-done.9.refs_0_ = bf16[432,128]{1,0:T(8,128)(2,1)S(1)} collective-permute-done((bf16[432,128]{1,0:T(8,128)(2,1)S(1)}, bf16[432,128]{1,0:T(8,128)(2,1)S(1)}, u32[]{:S(2)}, u32[]{:S(2)}) %collective-permute-start.9) | collective-permute-done | bytes 110624 | tf_op jit(solution)/shard_map/ppermute | solution.py:860
  27.7 0.0 collective-permute-start.7
  27.7 2.3 %collective-permute-done.8.refs_0_ = bf16[13,64,128]{2,1,0:T(8,128)(2,1)S(1)} collective-permute-done((bf16[13,64,128]{2,1,0:T(8,128)(2,1)S(1)}, bf16[13,64,128]{2,1,0:T(8,128)(2,1)S(1)}, u32[]{:S(2)}, u32[]{:S(2)}) %collective-permute-start.8) | collective-permute-done | bytes 213024 | tf_op jit(solution)/shard_map/ppermute | solution.py:857
  30.0 0.0 collective-permute-done.11.refs_0_
  30.0 1.6 %collective-permute-done.12.refs_1_ = bf16[432,128]{1,0:T(8,128)(2,1)S(1)} collective-permute-done((bf16[432,128]{1,0:T(8,128)(2,1)S(1)}, bf16[432,128]{1,0:T(8,128)(2,1)S(1)}, u32[]{:S(2)}, u32[]{:S(2)}) %collective-permute-start.12) | collective-permute-done | bytes 110624 | tf_op jit(solution)/shard_map/ppermute | solution.py:860
  31.6 0.0 collective-permute-done.10.strip
  31.6 0.0 collective-permute-done.7.near
  31.6 1.2 %shard_map.148 = (bf16[1,16,64,128]{3,2,1,0:T(8,128)(2,1)}, bf16[1,16,64,128]{3,2,1,0:T(8,128)(2,1)}, bf16[1,16,64,128]{3,2,1,0:T(8,128)(2,1)}, f32[216,128]{1,0:T(8,128)}, f32[216,128]{1,0:T(8,128)}) custom-call(bf16[16,64,128]{2,1,0:T(8,128)(2,1)S(1)} %collective-permute-done.7.near, bf16[13,64,128]{2,1,0:T(8,128)(2,1)S(1)} %shard_map.146.refs_2_.far, ...), custom_call_target="tpu_custom_call" | custom-call | flops 1000 | bytes 1000 | tf_op jit(solution)/shard_map/pallas_call | solution.py:865
  (5 shorter events, 0.0 us)
Async XLA Ops:
  0.6 12.5 %collective-permute-start.4 = (bf16[1,16,64,128]{3,2,1,0:T(8,128)(2,1)}, bf16[1,16,64,128]{3,2,1,0:T(8,128)(2,1)S(1)}, u32[]{:S(2)}, u32[]{:S(2)}) collective-permute-start(bf16[1,16,64,128]{3,2,1,0:T(8,128)(2,1)} %st.3), channel_id=1, source_target_pairs={{0,4},{4,0},{1,5},{5,1},{2,6},{6,2},{3,7},{7,3},{8,12},{12,8},{9,1... | collective-permute-start | bytes 786440 | tf_op jit(solution)/shard_map/ppermute | solution.py:707
  3.7 6.0 %copy-start = (bf16[64,128]{1,0:T(8,128)(2,1)S(1)}, bf16[64,128]{1,0:T(8,128)(2,1)}, u32[]{:S(2)}) copy-start(bf16[64,128]{1,0:T(8,128)(2,1)} %coarse.3) | copy-start | bytes 49156
  5.0 13.1 %collective-permute-start.5 = (bf16[16,64,128]{2,1,0:T(8,128)(2,1)S(1)}, bf16[16,64,128]{2,1,0:T(8,128)(2,1)S(1)}, u32[]{:S(2)}, u32[]{:S(2)}) collective-permute-start(bf16[16,64,128]{2,1,0:T(8,128)(2,1)S(1)} %get-tuple-element.37.grad), channel_id=1, source_target_pairs={{0,4},{4,0},{1,5},{5,1},{2,6},{6,2},{3,7},{7,3},{8,12},{12,8},{9,1... | collective-permute-start | bytes 786440 | tf_op jit(solution)/shard_map/ppermute | solution.py:725
  5.1 6.5 %collective-permute-start = (bf16[25,8,128]{2,1,0:T(8,128)(2,1)S(1)}, bf16[25,8,128]{2,1,0:T(8,128)(2,1)S(1)}, u32[]{:S(2)}, u32[]{:S(2)}) collective-permute-start(bf16[25,8,128]{2,1,0:T(8,128)(2,1)S(1)} %get-tuple-element.30), channel_id=1, source_target_pairs={{0,1},{2,3},{1,0},{3,2},{4,5},{6,7},{5,4},{7,6},{8,9},{10,11},{9,8... | collective-permute-start | bytes 153608 | tf_op jit(solution)/shard_map/ppermute | solution.py:726
  7.2 5.9 %collective-permute-start.1 = (bf16[25,8,128]{2,1,0:T(8,128)(2,1)S(1)}, bf16[25,8,128]{2,1,0:T(8,128)(2,1)S(1)}, u32[]{:S(2)}, u32[]{:S(2)}) collective-permute-start(bf16[25,8,128]{2,1,0:T(8,128)(2,1)S(1)} %get-tuple-element.31), channel_id=1, source_target_pairs={{0,3},{1,2},{2,1},{3,0},{4,7},{5,6},{6,5},{7,4},{8,11},{9,10},{10,... | collective-permute-start | bytes 153608 | tf_op jit(solution)/shard_map/ppermute | solution.py:727
  9.7 5.1 %collective-permute-start.2 = (bf16[64,128]{1,0:T(8,128)(2,1)S(1)}, bf16[64,128]{1,0:T(8,128)(2,1)S(1)}, u32[]{:S(2)}, u32[]{:S(2)}) collective-permute-start(bf16[64,128]{1,0:T(8,128)(2,1)S(1)} %copy-done), channel_id=1, source_target_pairs={{0,2},{1,3},{2,0},{3,1},{4,6},{5,7},{6,4},{7,5},{8,10},{9,11},{10,... | collective-permute-start | bytes 49160 | tf_op jit(solution)/shard_map/ppermute | solution.py:729
  13.1 1.6 %copy-start.1 = (s32[64,1]{0,1:T(1,128)S(1)}, s32[64,1]{0,1:T(1,128)}, u32[]{:S(2)}) copy-start(s32[64,1]{0,1:T(1,128)} %param.17) | copy-start | bytes 772
  13.2 1.6 %copy-start.2 = (s32[64]{0:T(128)S(1)}, s32[64]{0:T(128)}, u32[]{:S(2)}) copy-start(s32[64]{0:T(128)} %cell.1) | copy-start | bytes 772
  13.2 5.0 %collective-permute-start.6 = (bf16[16,8,128]{2,1,0:T(8,128)(2,1)S(1)}, bf16[16,8,128]{2,1,0:T(8,128)(2,1)S(1)}, u32[]{:S(2)}, u32[]{:S(2)}) collective-permute-start(bf16[16,8,128]{2,1,0:T(8,128)(2,1)S(1)} %shard_map.142.rim), channel_id=1, source_target_pairs={{0,4},{4,0},{1,5},{5,1},{2,6},{6,2},{3,7},{7,3},{8,12},{12,8},{9,1... | collective-permute-start | bytes 98312 | tf_op jit(solution)/shard_map/ppermute | solution.py:756
  15.5 6.9 %collective-permute-start.3 = (bf16[27,8,128]{2,1,0:T(8,128)(2,1)S(1)}, bf16[27,8,128]{2,1,0:T(8,128)(2,1)S(1)}, u32[]{:S(2)}, u32[]{:S(2)}) collective-permute-start(bf16[27,8,128]{2,1,0:T(8,128)(2,1)S(1)} %get-tuple-element.33), channel_id=1, source_target_pairs={{0,4},{4,0},{1,5},{5,1},{2,6},{6,2},{3,7},{7,3},{8,12},{12,8},{9,1... | collective-permute-start | bytes 165896 | tf_op jit(solution)/shard_map/ppermute | solution.py:765
  20.7 7.0 %collective-permute-start.9 = (bf16[432,128]{1,0:T(8,128)(2,1)S(1)}, bf16[432,128]{1,0:T(8,128)(2,1)S(1)}, u32[]{:S(2)}, u32[]{:S(2)}) collective-permute-start(bf16[432,128]{1,0:T(8,128)(2,1)S(1)} %get-tuple-element.41), channel_id=1, source_target_pairs={{0,2},{1,3},{2,0},{3,1},{4,6},{5,7},{6,4},{7,5},{8,10},{9,11},{10,... | collective-permute-start | bytes 331784 | tf_op jit(solution)/shard_map/ppermute | solution.py:860
  22.5 7.5 %collective-permute-start.8 = (bf16[13,64,128]{2,1,0:T(8,128)(2,1)S(1)}, bf16[13,64,128]{2,1,0:T(8,128)(2,1)S(1)}, u32[]{:S(2)}, u32[]{:S(2)}) collective-permute-start(bf16[13,64,128]{2,1,0:T(8,128)(2,1)S(1)} %get-tuple-element.40), channel_id=1, source_target_pairs={{0,24},{8,16},{16,8},{24,0},{1,25},{9,17},{17,9},{25,1},{2,26},{10... | collective-permute-start | bytes 638984 | tf_op jit(solution)/shard_map/ppermute | solution.py:857
  22.5 7.5 %collective-permute-start.11 = (bf16[432,128]{1,0:T(8,128)(2,1)S(1)}, bf16[432,128]{1,0:T(8,128)(2,1)S(1)}, u32[]{:S(2)}, u32[]{:S(2)}) collective-permute-start(bf16[432,128]{1,0:T(8,128)(2,1)S(1)} %get-tuple-element.44), channel_id=1, source_target_pairs={{0,1},{1,0},{2,3},{3,2},{4,5},{5,4},{6,7},{7,6},{8,9},{9,8},{10,11... | collective-permute-start | bytes 331784 | tf_op jit(solution)/shard_map/ppermute | solution.py:860
  24.0 7.6 %collective-permute-start.12 = (bf16[432,128]{1,0:T(8,128)(2,1)S(1)}, bf16[432,128]{1,0:T(8,128)(2,1)S(1)}, u32[]{:S(2)}, u32[]{:S(2)}) collective-permute-start(bf16[432,128]{1,0:T(8,128)(2,1)S(1)} %get-tuple-element.45), channel_id=1, source_target_pairs={{0,3},{1,2},{2,1},{3,0},{4,7},{5,6},{6,5},{7,4},{8,11},{9,10},{10,... | collective-permute-start | bytes 331784 | tf_op jit(solution)/shard_map/ppermute | solution.py:860
  26.0 5.7 %collective-permute-start.10 = (bf16[3,64,128]{2,1,0:T(8,128)(2,1)S(1)}, bf16[3,64,128]{2,1,0:T(8,128)(2,1)S(1)}, u32[]{:S(2)}, u32[]{:S(2)}) collective-permute-start(bf16[3,64,128]{2,1,0:T(8,128)(2,1)S(1)} %get-tuple-element.42), channel_id=1, source_target_pairs={{0,24},{8,16},{16,8},{24,0},{1,25},{9,17},{17,9},{25,1},{2,26},{10... | collective-permute-start | bytes 147464 | tf_op jit(solution)/shard_map/ppermute | solution.py:858
  27.7 3.9 %collective-permute-start.7 = (bf16[16,64,128]{2,1,0:T(8,128)(2,1)S(1)}, bf16[16,64,128]{2,1,0:T(8,128)(2,1)S(1)}, u32[]{:S(2)}, u32[]{:S(2)}) collective-permute-start(bf16[16,64,128]{2,1,0:T(8,128)(2,1)S(1)} %get-tuple-element.39), channel_id=1, source_target_pairs={{0,8},{8,0},{16,24},{24,16},{1,9},{9,1},{17,25},{25,17},{2,10},{10... | collective-permute-start | bytes 786440 | tf_op jit(solution)/shard_map/ppermute | solution.py:859

commit v5 on v4

--- a/solution.py
+++ b/solution.py
@@ -409,8 +409,8 @@
 def paired_kernel(
     st, grad, st_far, grad_far, rim, rim_far, flat_up, flat_down, value, far, in_grad, *rest
 ):
-    own_sum, send1, send2, send3, field, even_taps, odd_taps, sums, d0, d1, up_flat, down_flat = rest[:12]
-    grads, products, fine, edge_taps, edge_sums, grad_field = rest[12:]
+    own_sum, send1, send2, send3, field, taps, sums, d0, d1, up_flat = rest[:10]
+    grads, products, fine, edge_taps, edge_sums, grad_field = rest[10:]
     rows, breadth = grad.shape[0], grad.shape[1]
     wide = breadth + 16
     count, half_rows, half_cols = rows, rows // 2, breadth // 2
@@ -447,11 +447,12 @@
     for each in (field, grad_field):
         each[:, wide:] = jnp.zeros((each.shape[0], each.shape[1] - wide, 128), F32)
     fill(field, lambda row: st[row], lambda row: st_far[0, row], 1, 5)
-    spread_taps(field, even_taps, odd_taps, 2 * count + 1, LEFT - 1)
+    spread_taps(field, taps.at[:, :, 0:384], taps.at[:, :, 384:768], 2 * count + 1, LEFT - 1)
     for p in range(edge_count):
         for tap in range(9):
             edge_taps[p, :, tap * 128 : tap * 128 + 128] = edge(field, 2 * p + tap // 3, tap % 3)
-    pre_back = lower(even_taps, odd_taps, count, flat_down)
+    pre_back = full_taps(taps[0:count].reshape(cells, 768), flat_down.at[:, 0:768])
+    pre_back += full_taps(taps[1 : count + 1, :, 0:384].reshape(cells, 384), flat_down.at[:, 768:1152])
     logistic, slope = slopes(pre_back)
     reduced = (pre_back * logistic).astype(BF16)
     edge_slope = slopes(full_taps(flat_edge(edge_taps), flat_down))[1]
@@ -471,8 +472,8 @@
     for tap in range(5):
         up_flat[tap * depth : tap * depth + depth] = terms[:, tap * 128 : tap * 128 + 128]
     span = 3 * 128
-    outer = across(even_taps[pl.ds(tx, count)].reshape(cells, span), coupled)
-    middle = across(odd_taps[0:count].reshape(cells, span), coupled)
+    outer = across(taps[pl.ds(tx, count), :, 0:span].reshape(cells, span), coupled)
+    middle = across(taps[0:count, :, span : 2 * span].reshape(cells, span), coupled)
     outer_at = pl.multiple_of(tx * (span // 2), 8)
     middle_at = pl.multiple_of((1 - tx) * span, 8)
     middle_half = jnp.where(tx == 0, middle[0 : span // 2], middle[span // 2 : span])
@@ -480,16 +481,16 @@
     d1[pl.ds(outer_at, span), 0:64] = outer[:, 128:192]
     d0[pl.ds(middle_at, span // 2)] = middle_half[:, 0:128]
     d1[pl.ds(middle_at, span // 2), 0:64] = middle_half[:, 128:192]
-    flatten_rows(d0, d1, down_flat, 0)
-    piece = half // 4
+    piece, tall = half // 4, d0.shape[0] // 4
     up_start = tx * (depth // 2)
+    near = lax.broadcasted_iota(jnp.int32, (tall // 2, 128), 1) < 64
     for distance, target in enumerate((own_sum, send1, send2, send3)):
-        place = (ty ^ distance) * piece
-        both = [
-            up_flat[pl.ds(pl.multiple_of(up_start + place, 8), piece)],
-            down_flat[pl.ds(pl.multiple_of(place, 8), piece)],
-        ]
-        target[...] = jnp.concatenate(both, axis=0).astype(target.dtype)
+        peer = ty ^ distance
+        start = pl.multiple_of(peer * tall, 8)
+        later = pl.multiple_of(peer * tall + tall // 2, 8)
+        rests = jnp.where(near, d1[pl.ds(start, tall // 2)], pltpu.roll(d1[pl.ds(later, tall // 2)], 64, 1))
+        parts = [up_flat[pl.ds(pl.multiple_of(up_start + peer * piece, 8), piece)], d0[pl.ds(start, tall)], rests]
+        target[...] = jnp.concatenate(parts, axis=0).astype(target.dtype)
     grads[0:count] = coupled.reshape(count, half_cols, depth)
     grads[count] = jnp.zeros((half_cols, depth), BF16)
     own_rows = grads[pl.ds(half_rows * tx, edge_count)].reshape(edge_count * half_cols, depth)
@@ -642,7 +643,7 @@
 
 
 def final_kernel(
-    scaling, near, far, strip, own, first, second, third, act_out, grad_out, partner_out, up_sum, down_sum
+    scaling, near, far, strip, own, first, second, third, act_out, grad_out, partner_out, up_sum, down_sum, d0, d1
 ):
     rows, border = near.shape[0], strip.shape[0]
     position, last = lax.axis_index("segment"), lax.axis_size("segment") - 1
@@ -659,7 +660,12 @@
     total = own[...] + first[...].astype(F32) + second[...].astype(F32) + third[...].astype(F32)
     piece = up_sum.shape[0]
     up_sum[...] = total[0:piece] * scaling
-    down_sum[...] = total[piece:] * scaling
+    tall = d0.shape[0]
+    rests = total[piece + tall :] * scaling
+    d0[...] = total[piece : piece + tall] * scaling
+    d1[0 : tall // 2] = rests
+    d1[tall // 2 :] = pltpu.roll(rests, 64, 1)
+    flatten_rows(d0, d1, down_sum, 0)
 
 
 def swaps(axis):
@@ -804,13 +810,11 @@
             [VMEM] * 9,
             [
                 pltpu.VMEM((2 * height + 4, wide, channels), F32),
-                pltpu.VMEM((height + 1, breadth // 2, 3 * channels), BF16),
-                pltpu.VMEM((height, breadth // 2, 3 * channels), BF16),
+                pltpu.VMEM((height + 1, breadth // 2, 6 * channels), BF16),
                 pltpu.VMEM((height, breadth // 2, 9 * channels), BF16),
                 pltpu.VMEM((9 * channels // 2, 128), F32),
                 pltpu.VMEM((9 * channels // 2, 128), F32),
                 pltpu.VMEM((5 * depth, channels), F32),
-                pltpu.VMEM((rows_flat // 2, channels), F32),
                 pltpu.VMEM((height + 1, breadth // 2, depth), BF16),
                 pltpu.VMEM((half_rows + 1, breadth // 2 + 8, 9 * channels), F32),
                 fine,
@@ -866,6 +870,7 @@
             functools.partial(final_kernel, scaling),
             (shape(act_in.shape, BF16),) * 3 + (summed, summed),
             [VMEM] * 7,
+            [pltpu.VMEM((2 * piece // 3, 128), F32)] * 2,
             flops=1_000,
             moved=1000,
         )(from_near, from_far, from_strip, own_sum, *arrived)

time: 33 us -> 32.8 us (level)
  transfers between devices with their start and end apart: 13 -> 13, of which waited for: 4 -> 4; matrix products, arithmetic and copies ran while one was open for 0% -> 0% of each run, Pallas kernels for 27% -> 26%
where the time goes in v5:
time: 32.8 us; the launch traced here: 32.7 us
  starting transfers between devices  16.2 us (49%)
  Pallas kernels  9.81 us (30%)
  waiting for transfers between devices  5.89 us (18%)
  between operations  0.74 us (2%)
    ppermute x3, starting transfers between devices, local(): lax.ppermute(sends[d - 1], 'ty', crossed('ty', d))  4.45 us
    ppermute x1, starting transfers between devices, local(): st_far = lax.ppermute(stashed, 'tx', crossed('tx', 1))  3.03 us
    ppermute x1, starting transfers between devices, local(): z1 = lax.ppermute(z_pay1, 'ty', others)  2.47 us
    pallas_call x1, Pallas kernels, local(): call(paired_kernel, (shape((height - BORDER, breadth, channels), BF16), t...  2.34 us
    ppermute x1, waiting for transfers between devices, local(): from_far = lax.ppermute(far, 'segment', mirror)  2.26 us
    ppermute x3, waiting for transfers between devices, local(): lax.ppermute(sends[d - 1], 'ty', crossed('ty', d))  2.15 us
    ppermute x1, starting transfers between devices, local(): z0 = lax.ppermute(z_pay0, 'ty', pairs)  2.06 us
    pallas_call x1, Pallas kernels, local(): call(prepare_kernel, (shape((height, breadth, channels), F32), tile, flat...  1.84 us
  transfers between devices with their start and end apart: 13, of which 4 were waited for; matrix products, arithmetic and copies ran while one was open for 0% of the time, Pallas kernels for 26%

profile of v5, /device:TPU:0, one launch (start us, length us, event | category | flops | bytes accessed | tf_op | source)
XLA Modules:
  0.0 32.7 jit_solution(4923446390925851063)
XLA Ops:
  0.6 3.0 %collective-permute-start.4 = (bf16[1,16,64,128]{3,2,1,0:T(8,128)(2,1)}, bf16[1,16,64,128]{3,2,1,0:T(8,128)(2,1)S(1)}, u32[]{:S(2)}, u32[]{:S(2)}) collective-permute-start(bf16[1,16,64,128]{3,2,1,0:T(8,128)(2,1)} %st.3), channel_id=1, source_target_pairs={{0,4},{4,0},{1,5},{5,1},{2,6},{6,2},{3,7},{7,3},{8,12},{12,8},{9,1... | collective-permute-start | bytes 786440 | tf_op jit(solution)/shard_map/ppermute | solution.py:713
  3.7 0.0 copy-start
  3.7 1.4 %shard_map.138 = (bf16[16,64,128]{2,1,0:T(8,128)(2,1)S(1)}, bf16[25,8,128]{2,1,0:T(8,128)(2,1)S(1)}, bf16[25,8,128]{2,1,0:T(8,128)(2,1)S(1)}) custom-call(s32[64]{0:T(128)} %bitcast.7, s32[64]{0:T(128)} %cell.1, s32[4,16]{1,0:T(4,128)} %land_in.1, bf16[1,16,64,128]{3,2,1,0:T(8,128)(2,1)} %act.3, bf16[1,16,64,128]{3,2,1,0:T(8,128)(2,1)} %par.3, ...), custom_call_target="tpu_custom_call" | custom-call | flops 1000 | bytes 1000 | tf_op jit(solution)/shard_map/pallas_call | solution.py:716
  5.0 0.1 collective-permute-start.5
  5.1 2.1 %collective-permute-start = (bf16[25,8,128]{2,1,0:T(8,128)(2,1)S(1)}, bf16[25,8,128]{2,1,0:T(8,128)(2,1)S(1)}, u32[]{:S(2)}, u32[]{:S(2)}) collective-permute-start(bf16[25,8,128]{2,1,0:T(8,128)(2,1)S(1)} %get-tuple-element.30), channel_id=1, source_target_pairs={{0,1},{2,3},{1,0},{3,2},{4,5},{6,7},{5,4},{7,6},{8,9},{10,11},{9,8... | collective-permute-start | bytes 153608 | tf_op jit(solution)/shard_map/ppermute | solution.py:732
  7.2 2.5 %collective-permute-start.1 = (bf16[25,8,128]{2,1,0:T(8,128)(2,1)S(1)}, bf16[25,8,128]{2,1,0:T(8,128)(2,1)S(1)}, u32[]{:S(2)}, u32[]{:S(2)}) collective-permute-start(bf16[25,8,128]{2,1,0:T(8,128)(2,1)S(1)} %get-tuple-element.31), channel_id=1, source_target_pairs={{0,3},{1,2},{2,1},{3,0},{4,7},{5,6},{6,5},{7,4},{8,11},{9,10},{10,... | collective-permute-start | bytes 153608 | tf_op jit(solution)/shard_map/ppermute | solution.py:733
  9.7 0.0 copy-done
  9.7 0.1 collective-permute-start.2
  9.8 1.8 %shard_map.137 = (f32[16,64,128]{2,1,0:T(8,128)S(1)}, bf16[16,64,128]{2,1,0:T(8,128)(2,1)S(1)}, bf16[192,1152]{1,0:T(8,128)(2,1)S(1)}, bf16[192,1152]{1,0:T(8,128)(2,1)S(1)}) custom-call(bf16[1,16,64,128]{3,2,1,0:T(8,128)(2,1)} %act.3, bf16[1,16,64,128]{3,2,1,0:T(8,128)(2,1)} %par.3, bf16[1,16,64,128]{3,2,1,0:T(8,128)(2,1)} %st.3, ...), custom_call_target="tpu_custom_call" | custom-call | flops 1000 | bytes 1000 | tf_op jit(solution)/shard_map/pallas_call | solution.py:740
  11.6 0.0 collective-permute-done.z0
  11.6 1.5 %collective-permute-done.1.z1 = bf16[25,8,128]{2,1,0:T(8,128)(2,1)S(1)} collective-permute-done((bf16[25,8,128]{2,1,0:T(8,128)(2,1)S(1)}, bf16[25,8,128]{2,1,0:T(8,128)(2,1)S(1)}, u32[]{:S(2)}, u32[]{:S(2)}) %collective-permute-start.1) | collective-permute-done | bytes 51232 | tf_op jit(solution)/shard_map/ppermute | solution.py:733
  13.1 0.0 collective-permute-done.4._stash.st_far
  13.1 0.0 copy-start.1
  13.2 0.0 copy-start.2
  13.2 1.6 %collective-permute-start.6 = (bf16[16,8,128]{2,1,0:T(8,128)(2,1)S(1)}, bf16[16,8,128]{2,1,0:T(8,128)(2,1)S(1)}, u32[]{:S(2)}, u32[]{:S(2)}) collective-permute-start(bf16[16,8,128]{2,1,0:T(8,128)(2,1)S(1)} %shard_map.142.rim), channel_id=1, source_target_pairs={{0,4},{4,0},{1,5},{5,1},{2,6},{6,2},{3,7},{7,3},{8,12},{12,8},{9,1... | collective-permute-start | bytes 98312 | tf_op jit(solution)/shard_map/ppermute | solution.py:762
  14.8 0.0 collective-permute-done.2.rest_0_
  14.8 0.0 copy-done.1
  14.8 0.0 copy-done.2
  14.8 0.8 %shard_map.139 = (bf16[27,8,128]{2,1,0:T(8,128)(2,1)S(1)}, bf16[16,80,128]{2,1,0:T(8,128)(2,1)S(1)}) custom-call(s32[64]{0:T(128)S(1)} %bitcast.8, s32[64]{0:T(128)S(1)} %copy-done.2, f32[16,64,128]{2,1,0:T(8,128)S(1)} %get-tuple-element.29.base, bf16[25,8,128]{2,1,0:T(8,128)(2,1)S(1)} %collective-permute-done.z0, ...), custom_call_target="tpu_custom_call" | custom-call | flops 2000000000 | bytes 1000 | tf_op jit(solution)/shard_map/pallas_call | solution.py:763
  15.5 1.1 %collective-permute-start.3 = (bf16[27,8,128]{2,1,0:T(8,128)(2,1)S(1)}, bf16[27,8,128]{2,1,0:T(8,128)(2,1)S(1)}, u32[]{:S(2)}, u32[]{:S(2)}) collective-permute-start(bf16[27,8,128]{2,1,0:T(8,128)(2,1)S(1)} %get-tuple-element.33), channel_id=1, source_target_pairs={{0,4},{4,0},{1,5},{5,1},{2,6},{6,2},{3,7},{7,3},{8,12},{12,8},{9,1... | collective-permute-start | bytes 165896 | tf_op jit(solution)/shard_map/ppermute | solution.py:771
  16.7 1.5 %shard_map.141.value = bf16[16,64,128]{2,1,0:T(8,128)(2,1)S(1)} custom-call(bf16[16,80,128]{2,1,0:T(8,128)(2,1)S(1)} %get-tuple-element.32.blocks, bf16[192,1152]{1,0:T(8,128)(2,1)S(1)} %get-tuple-element.34.flat_up._weights, bf16[192,1152]{1,0:T(8,128)(2,1)S(1)} %get-tuple-element.35.flat_down), custom_call_target="tpu_custom_call" | custom-call | flops 1000 | bytes 1000 | tf_op jit(solution)/shard_map/pallas_call | solution.py:797
  18.2 0.0 collective-permute-done.5.grad_far
  18.2 0.0 collective-permute-done.6.rim_far
  18.2 2.3 %shard_map.143 = (bf16[13,64,128]{2,1,0:T(8,128)(2,1)S(1)}, bf16[16,64,128]{2,1,0:T(8,128)(2,1)S(1)}, f32[432,128]{1,0:T(8,128)S(1)}, bf16[432,128]{1,0:T(8,128)...) custom-call(bf16[16,64,128]{2,1,0:T(8,128)(2,1)S(1)} %get-tuple-element.36.st, ...), custom_call_target="tpu_custom_call" | custom-call | flops 5000000000 | bytes 4000000 | tf_op jit(solution)/shard_map/pallas_call | solution.py:807
  20.5 1.8 %collective-permute-start.9 = (bf16[432,128]{1,0:T(8,128)(2,1)S(1)}, bf16[432,128]{1,0:T(8,128)(2,1)S(1)}, u32[]{:S(2)}, u32[]{:S(2)}) collective-permute-start(bf16[432,128]{1,0:T(8,128)(2,1)S(1)} %get-tuple-element.41), channel_id=1, source_target_pairs={{0,2},{1,3},{2,0},{3,1},{4,6},{5,7},{6,4},{7,5},{8,10},{9,11},{10,... | collective-permute-start | bytes 331784 | tf_op jit(solution)/shard_map/ppermute | solution.py:864
  22.3 0.0 collective-permute-start.8
  22.3 0.0 collective-permute-done.3.refs_0_
  22.3 1.6 %collective-permute-start.11 = (bf16[432,128]{1,0:T(8,128)(2,1)S(1)}, bf16[432,128]{1,0:T(8,128)(2,1)S(1)}, u32[]{:S(2)}, u32[]{:S(2)}) collective-permute-start(bf16[432,128]{1,0:T(8,128)(2,1)S(1)} %get-tuple-element.44), channel_id=1, source_target_pairs={{0,1},{1,0},{2,3},{3,2},{4,5},{5,4},{6,7},{7,6},{8,9},{9,8},{10,11... | collective-permute-start | bytes 331784 | tf_op jit(solution)/shard_map/ppermute | solution.py:864
  23.9 1.1 %collective-permute-start.12 = (bf16[432,128]{1,0:T(8,128)(2,1)S(1)}, bf16[432,128]{1,0:T(8,128)(2,1)S(1)}, u32[]{:S(2)}, u32[]{:S(2)}) collective-permute-start(bf16[432,128]{1,0:T(8,128)(2,1)S(1)} %get-tuple-element.45), channel_id=1, source_target_pairs={{0,3},{1,2},{2,1},{3,0},{4,7},{5,6},{6,5},{7,4},{8,11},{9,10},{10,... | collective-permute-start | bytes 331784 | tf_op jit(solution)/shard_map/ppermute | solution.py:864
  25.0 0.8 %shard_map.144 = (bf16[16,64,128]{2,1,0:T(8,128)(2,1)S(1)}, bf16[3,64,128]{2,1,0:T(8,128)(2,1)S(1)}) custom-call(bf16[16,80,128]{2,1,0:T(8,128)(2,1)S(1)} %get-tuple-element.32.blocks, bf16[27,8,128]{2,1,0:T(8,128)(2,1)S(1)} %shard_map.140.y0, bf16[16,64,128]{2,1,0:T(8,128)(2,1)S(1)} %shard_map.141.value, ...), custom_call_target="tpu_custom_call" | custom-call | flops 600000000 | bytes 4000000 | tf_op jit(solution)/shard_map/pallas_call | solution.py:853
  25.8 1.2 %collective-permute-start.10 = (bf16[3,64,128]{2,1,0:T(8,128)(2,1)S(1)}, bf16[3,64,128]{2,1,0:T(8,128)(2,1)S(1)}, u32[]{:S(2)}, u32[]{:S(2)}) collective-permute-start(bf16[3,64,128]{2,1,0:T(8,128)(2,1)S(1)} %get-tuple-element.42), channel_id=1, source_target_pairs={{0,24},{8,16},{16,8},{24,0},{1,25},{9,17},{17,9},{25,1},{2,26},{10... | collective-permute-start | bytes 147464 | tf_op jit(solution)/shard_map/ppermute | solution.py:862
  27.1 0.5 %collective-permute-done.9.refs_0_ = bf16[432,128]{1,0:T(8,128)(2,1)S(1)} collective-permute-done((bf16[432,128]{1,0:T(8,128)(2,1)S(1)}, bf16[432,128]{1,0:T(8,128)(2,1)S(1)}, u32[]{:S(2)}, u32[]{:S(2)}) %collective-permute-start.9) | collective-permute-done | bytes 110624 | tf_op jit(solution)/shard_map/ppermute | solution.py:864
  27.6 0.0 collective-permute-start.7
  27.6 2.3 %collective-permute-done.8.refs_0_ = bf16[13,64,128]{2,1,0:T(8,128)(2,1)S(1)} collective-permute-done((bf16[13,64,128]{2,1,0:T(8,128)(2,1)S(1)}, bf16[13,64,128]{2,1,0:T(8,128)(2,1)S(1)}, u32[]{:S(2)}, u32[]{:S(2)}) %collective-permute-start.8) | collective-permute-done | bytes 213024 | tf_op jit(solution)/shard_map/ppermute | solution.py:861
  29.8 0.0 collective-permute-done.11.refs_0_
  29.8 1.7 %collective-permute-done.12.refs_1_ = bf16[432,128]{1,0:T(8,128)(2,1)S(1)} collective-permute-done((bf16[432,128]{1,0:T(8,128)(2,1)S(1)}, bf16[432,128]{1,0:T(8,128)(2,1)S(1)}, u32[]{:S(2)}, u32[]{:S(2)}) %collective-permute-start.12) | collective-permute-done | bytes 110624 | tf_op jit(solution)/shard_map/ppermute | solution.py:864
  31.5 0.0 collective-permute-done.10.strip
  31.5 0.0 collective-permute-done.7.near
  31.5 1.2 %shard_map.148 = (bf16[1,16,64,128]{3,2,1,0:T(8,128)(2,1)}, bf16[1,16,64,128]{3,2,1,0:T(8,128)(2,1)}, bf16[1,16,64,128]{3,2,1,0:T(8,128)(2,1)}, f32[216,128]{1,0:T(8,128)}, f32[216,128]{1,0:T(8,128)}) custom-call(bf16[16,64,128]{2,1,0:T(8,128)(2,1)S(1)} %collective-permute-done.7.near, bf16[13,64,128]{2,1,0:T(8,128)(2,1)S(1)} %shard_map.146.refs_2_.far, ...), custom_call_target="tpu_custom_call" | custom-call | flops 1000 | bytes 1000 | tf_op jit(solution)/shard_map/pallas_call | solution.py:869
  (5 shorter events, 0.0 us)
Async XLA Ops:
  0.6 12.5 %collective-permute-start.4 = (bf16[1,16,64,128]{3,2,1,0:T(8,128)(2,1)}, bf16[1,16,64,128]{3,2,1,0:T(8,128)(2,1)S(1)}, u32[]{:S(2)}, u32[]{:S(2)}) collective-permute-start(bf16[1,16,64,128]{3,2,1,0:T(8,128)(2,1)} %st.3), channel_id=1, source_target_pairs={{0,4},{4,0},{1,5},{5,1},{2,6},{6,2},{3,7},{7,3},{8,12},{12,8},{9,1... | collective-permute-start | bytes 786440 | tf_op jit(solution)/shard_map/ppermute | solution.py:713
  3.7 6.0 %copy-start = (bf16[64,128]{1,0:T(8,128)(2,1)S(1)}, bf16[64,128]{1,0:T(8,128)(2,1)}, u32[]{:S(2)}) copy-start(bf16[64,128]{1,0:T(8,128)(2,1)} %coarse.3) | copy-start | bytes 49156
  5.0 13.1 %collective-permute-start.5 = (bf16[16,64,128]{2,1,0:T(8,128)(2,1)S(1)}, bf16[16,64,128]{2,1,0:T(8,128)(2,1)S(1)}, u32[]{:S(2)}, u32[]{:S(2)}) collective-permute-start(bf16[16,64,128]{2,1,0:T(8,128)(2,1)S(1)} %get-tuple-element.37.grad), channel_id=1, source_target_pairs={{0,4},{4,0},{1,5},{5,1},{2,6},{6,2},{3,7},{7,3},{8,12},{12,8},{9,1... | collective-permute-start | bytes 786440 | tf_op jit(solution)/shard_map/ppermute | solution.py:731
  5.1 6.5 %collective-permute-start = (bf16[25,8,128]{2,1,0:T(8,128)(2,1)S(1)}, bf16[25,8,128]{2,1,0:T(8,128)(2,1)S(1)}, u32[]{:S(2)}, u32[]{:S(2)}) collective-permute-start(bf16[25,8,128]{2,1,0:T(8,128)(2,1)S(1)} %get-tuple-element.30), channel_id=1, source_target_pairs={{0,1},{2,3},{1,0},{3,2},{4,5},{6,7},{5,4},{7,6},{8,9},{10,11},{9,8... | collective-permute-start | bytes 153608 | tf_op jit(solution)/shard_map/ppermute | solution.py:732
  7.2 5.9 %collective-permute-start.1 = (bf16[25,8,128]{2,1,0:T(8,128)(2,1)S(1)}, bf16[25,8,128]{2,1,0:T(8,128)(2,1)S(1)}, u32[]{:S(2)}, u32[]{:S(2)}) collective-permute-start(bf16[25,8,128]{2,1,0:T(8,128)(2,1)S(1)} %get-tuple-element.31), channel_id=1, source_target_pairs={{0,3},{1,2},{2,1},{3,0},{4,7},{5,6},{6,5},{7,4},{8,11},{9,10},{10,... | collective-permute-start | bytes 153608 | tf_op jit(solution)/shard_map/ppermute | solution.py:733
  9.7 5.1 %collective-permute-start.2 = (bf16[64,128]{1,0:T(8,128)(2,1)S(1)}, bf16[64,128]{1,0:T(8,128)(2,1)S(1)}, u32[]{:S(2)}, u32[]{:S(2)}) collective-permute-start(bf16[64,128]{1,0:T(8,128)(2,1)S(1)} %copy-done), channel_id=1, source_target_pairs={{0,2},{1,3},{2,0},{3,1},{4,6},{5,7},{6,4},{7,5},{8,10},{9,11},{10,... | collective-permute-start | bytes 49160 | tf_op jit(solution)/shard_map/ppermute | solution.py:735
  13.1 1.6 %copy-start.1 = (s32[64,1]{0,1:T(1,128)S(1)}, s32[64,1]{0,1:T(1,128)}, u32[]{:S(2)}) copy-start(s32[64,1]{0,1:T(1,128)} %param.17) | copy-start | bytes 772
  13.2 1.6 %copy-start.2 = (s32[64]{0:T(128)S(1)}, s32[64]{0:T(128)}, u32[]{:S(2)}) copy-start(s32[64]{0:T(128)} %cell.1) | copy-start | bytes 772
  13.2 5.0 %collective-permute-start.6 = (bf16[16,8,128]{2,1,0:T(8,128)(2,1)S(1)}, bf16[16,8,128]{2,1,0:T(8,128)(2,1)S(1)}, u32[]{:S(2)}, u32[]{:S(2)}) collective-permute-start(bf16[16,8,128]{2,1,0:T(8,128)(2,1)S(1)} %shard_map.142.rim), channel_id=1, source_target_pairs={{0,4},{4,0},{1,5},{5,1},{2,6},{6,2},{3,7},{7,3},{8,12},{12,8},{9,1... | collective-permute-start | bytes 98312 | tf_op jit(solution)/shard_map/ppermute | solution.py:762
  15.5 6.8 %collective-permute-start.3 = (bf16[27,8,128]{2,1,0:T(8,128)(2,1)S(1)}, bf16[27,8,128]{2,1,0:T(8,128)(2,1)S(1)}, u32[]{:S(2)}, u32[]{:S(2)}) collective-permute-start(bf16[27,8,128]{2,1,0:T(8,128)(2,1)S(1)} %get-tuple-element.33), channel_id=1, source_target_pairs={{0,4},{4,0},{1,5},{5,1},{2,6},{6,2},{3,7},{7,3},{8,12},{12,8},{9,1... | collective-permute-start | bytes 165896 | tf_op jit(solution)/shard_map/ppermute | solution.py:771
  20.5 7.0 %collective-permute-start.9 = (bf16[432,128]{1,0:T(8,128)(2,1)S(1)}, bf16[432,128]{1,0:T(8,128)(2,1)S(1)}, u32[]{:S(2)}, u32[]{:S(2)}) collective-permute-start(bf16[432,128]{1,0:T(8,128)(2,1)S(1)} %get-tuple-element.41), channel_id=1, source_target_pairs={{0,2},{1,3},{2,0},{3,1},{4,6},{5,7},{6,4},{7,5},{8,10},{9,11},{10,... | collective-permute-start | bytes 331784 | tf_op jit(solution)/shard_map/ppermute | solution.py:864
  22.3 7.5 %collective-permute-start.8 = (bf16[13,64,128]{2,1,0:T(8,128)(2,1)S(1)}, bf16[13,64,128]{2,1,0:T(8,128)(2,1)S(1)}, u32[]{:S(2)}, u32[]{:S(2)}) collective-permute-start(bf16[13,64,128]{2,1,0:T(8,128)(2,1)S(1)} %get-tuple-element.40), channel_id=1, source_target_pairs={{0,24},{8,16},{16,8},{24,0},{1,25},{9,17},{17,9},{25,1},{2,26},{10... | collective-permute-start | bytes 638984 | tf_op jit(solution)/shard_map/ppermute | solution.py:861
  22.3 7.5 %collective-permute-start.11 = (bf16[432,128]{1,0:T(8,128)(2,1)S(1)}, bf16[432,128]{1,0:T(8,128)(2,1)S(1)}, u32[]{:S(2)}, u32[]{:S(2)}) collective-permute-start(bf16[432,128]{1,0:T(8,128)(2,1)S(1)} %get-tuple-element.44), channel_id=1, source_target_pairs={{0,1},{1,0},{2,3},{3,2},{4,5},{5,4},{6,7},{7,6},{8,9},{9,8},{10,11... | collective-permute-start | bytes 331784 | tf_op jit(solution)/shard_map/ppermute | solution.py:864
  23.9 7.6 %collective-permute-start.12 = (bf16[432,128]{1,0:T(8,128)(2,1)S(1)}, bf16[432,128]{1,0:T(8,128)(2,1)S(1)}, u32[]{:S(2)}, u32[]{:S(2)}) collective-permute-start(bf16[432,128]{1,0:T(8,128)(2,1)S(1)} %get-tuple-element.45), channel_id=1, source_target_pairs={{0,3},{1,2},{2,1},{3,0},{4,7},{5,6},{6,5},{7,4},{8,11},{9,10},{10,... | collective-permute-start | bytes 331784 | tf_op jit(solution)/shard_map/ppermute | solution.py:864
  25.8 5.7 %collective-permute-start.10 = (bf16[3,64,128]{2,1,0:T(8,128)(2,1)S(1)}, bf16[3,64,128]{2,1,0:T(8,128)(2,1)S(1)}, u32[]{:S(2)}, u32[]{:S(2)}) collective-permute-start(bf16[3,64,128]{2,1,0:T(8,128)(2,1)S(1)} %get-tuple-element.42), channel_id=1, source_target_pairs={{0,24},{8,16},{16,8},{24,0},{1,25},{9,17},{17,9},{25,1},{2,26},{10... | collective-permute-start | bytes 147464 | tf_op jit(solution)/shard_map/ppermute | solution.py:862
  27.6 3.9 %collective-permute-start.7 = (bf16[16,64,128]{2,1,0:T(8,128)(2,1)S(1)}, bf16[16,64,128]{2,1,0:T(8,128)(2,1)S(1)}, u32[]{:S(2)}, u32[]{:S(2)}) collective-permute-start(bf16[16,64,128]{2,1,0:T(8,128)(2,1)S(1)} %get-tuple-element.39), channel_id=1, source_target_pairs={{0,8},{8,0},{16,24},{24,16},{1,9},{9,1},{17,25},{25,17},{2,10},{10... | collective-permute-start | bytes 786440 | tf_op jit(solution)/shard_map/ppermute | solution.py:863

commit v6 on v5

--- a/solution.py
+++ b/solution.py
@@ -170,9 +170,36 @@
     return before, after
 
 
-def rim_kernel(z0, z1, _weights, _stash, rim):
+def rim_kernel(z0, z1, _weights, _stash, rim, pack):
     before, after = side_rims(z0, z1, rim.shape[0])
-    rim[...] = jnp.where(sublane(rim.shape) < 5, after, before).astype(BF16)
+    whole = jnp.where(sublane(rim.shape) < 5, after, before)
+    rim[...] = whole.astype(BF16)
+    rows, half = rim.shape[0], rim.shape[0] // 2
+    turned = pltpu.roll(whole, 4, 1)
+    spot = sublane((half, 8, 128))
+    first = jnp.where(spot < 2, whole[:half], turned[:half])
+    second = jnp.where(spot < 6, turned[half:], whole[half:])
+    pack[0:half] = jnp.where(spot < 4, first, second).astype(BF16)
+    upper = lax.axis_index("tx") == 0
+    for k in range(BORDER):
+        pack[half + k] = jnp.where(upper, whole[rows - BORDER + k], whole[k]).astype(BF16)
+
+
+def unpacked_rims(pack):
+    packed = pack[...].astype(F32)
+    half = packed.shape[0] - BORDER
+    rows = 2 * half
+    turned = pltpu.roll(packed, 4, 1)
+    low = sublane((half, 8, 128)) < 4
+    first = jnp.where(low, packed[:half], turned[:half])
+    second = jnp.where(low, turned[:half], packed[:half])
+    tiles = [first[k] for k in range(half)] + [second[k] for k in range(half)]
+    upper = lax.axis_index("tx") == 0
+    for k in range(BORDER):
+        tiles[k] = jnp.where(upper, packed[half + k], tiles[k])
+        here = rows - BORDER + k
+        tiles[here] = jnp.where(upper, tiles[here], packed[half + k])
+    return jnp.concatenate([tile[None] for tile in tiles], axis=0)
 
 
 def condition_kernel(merged, owner, cell, base, z0, z1, coarse, *rest):
@@ -184,7 +211,7 @@
     ty = lax.axis_index("ty")
     low = sublane((8, 128)) < 4
     if merged:
-        z2, pay, ext, table, plane = rest
+        z2, pay, ext, table, plane, named_here = rest
         table[pl.ds(pl.multiple_of(ty * cells, 8), cells)] = coarse[...].astype(F32)
         others = (
             (ty ^ 1, z0[rows + 1 :].astype(F32).reshape(cells, 128)),
@@ -214,6 +241,8 @@
     ext[:, 0:8] = rim.astype(BF16)
     rim = pltpu.roll(after[0:rows], 3, 1) + rim_condition(after, ty < lax.axis_size("ty") - 1)
     ext[:, wide : wide + 8] = rim.astype(BF16)
+    if merged:
+        named_here()
     for group in range(groups):
         for part in range(breadth // 8):
             spots = [group * per_row + 2 * part + k for k in range(2)]
@@ -421,15 +450,16 @@
     has_right = ty < lax.axis_size("ty") - 1
     first_row = rows * tx
 
+    rim_here, rim_there = rim[...].astype(F32), unpacked_rims(rim_far)
+
     def fill(field, here_rows, there_rows, turn_before, turn_after):
         blank = jnp.zeros((wide, 128), F32)
         field[0, 0:wide] = blank
         field[2 * rows + 1, 0:wide] = blank
         here, there = 1 + rows * tx, 1 + rows * (1 - tx)
-        for start, source, sides in ((here, here_rows, rim), (there, there_rows, rim_far)):
+        for start, source, sides in ((here, here_rows, rim_here), (there, there_rows, rim_there)):
             for row in range(rows):
                 field[start + row, LEFT : LEFT + breadth] = source(row).astype(F32)
-            sides = sides[...].astype(F32)
             turned = lambda turn: pltpu.roll(sides, turn, 1) if turn else sides
             field[pl.ds(start, rows), 0:8] = turned(turn_before)
             field[pl.ds(start, rows), LEFT + breadth : wide] = turned(turn_after)
@@ -603,6 +633,22 @@
         value[row] = (blocks[row, LEFT : LEFT + breadth].astype(F32) + fine[row]).astype(BF16)
 
 
+def condition_inner_kernel(
+    owner_in, cell_in, base, z0, z1, coarse, z2, flat_up, flat_down, pay, ext, value, *scratch
+):
+    table, plane, owner, cell, arrived = scratch[:5]
+    copies = copies_in_parts(((owner_in, owner, 1), (cell_in, cell, 1)), arrived)
+    for copy in copies:
+        copy.start()
+
+    def named():
+        for copy in copies:
+            copy.wait()
+
+    condition_kernel(True, owner, cell, base, z0, z1, coarse, z2, pay, ext, table, plane, named)
+    inner_kernel(ext, flat_up, flat_down, value, *scratch[5:])
+
+
 def border_kernel(blocks, y0, value, in_grad, flat_up, flat_down, near, strip, *scratch):
     field, even_taps, odd_taps, products, mixed, fine = scratch
     rows, wide = blocks.shape[0], blocks.shape[1]
@@ -745,6 +791,20 @@
         flops=1000,
         moved=1000,
     )(*in_hbm(act_in, partner_in, stashed, up_taps, down_taps))
+    wide = 2 * PAD + 16
+    rows_flat = 9 * depth
+
+    def tap_rooms(count):
+        room = pltpu.VMEM((count + 1, PAD, 3 * channels), BF16)
+        return [pltpu.VMEM((2 * count + 2, wide, channels), F32), room, room]
+
+    fine = pltpu.VMEM((height, breadth, channels), F32)
+    products = lambda count: pltpu.VMEM((count, PAD, 9 * channels), F32)
+    forward_rooms = lambda count: tap_rooms(count) + [
+        products(count),
+        pltpu.VMEM((4, PAD, channels), F32),
+        fine,
+    ]
     operands = (base, z0, z1, *table_parts)
     rooms = [
         pltpu.VMEM((n_ty * coarse.shape[0], channels), F32),
@@ -752,22 +812,29 @@
     ]
     pairs, others = swaps("tx")
     if merged:
-        rim = call(
+        rim, pack = call(
             rim_kernel,
-            shape((height, 8, channels), BF16),
+            (shape((height, 8, channels), BF16), shape((height // 2 + BORDER, 8, channels), BF16)),
             [VMEM] * 2 + [pl.BlockSpec(memory_space=pl.ANY)] * 2,
             flops=1000,
             moved=1000,
         )(z0, z1, flat_up, st_far)
-        rim_far = lax.ppermute(rim, "tx", pairs)
-        pay, blocks = call(
-            functools.partial(condition_kernel, True),
-            (shape((3 * (breadth // 8 + 1), 8, channels), BF16), shape((height, breadth + 16, channels), BF16)),
-            [SMEM] * 2 + [VMEM] * len(operands),
-            rooms,
+        rim_far = lax.ppermute(pack, "tx", pairs)
+        pay, blocks, value = call(
+            condition_inner_kernel,
+            (
+                shape((3 * (breadth // 8 + 1), 8, channels), BF16),
+                shape((height, breadth + 16, channels), BF16),
+                tile,
+            ),
+            [HBM] * 2 + [VMEM] * (len(operands) + 2),
+            rooms
+            + [pltpu.SMEM(owners.shape, jnp.int32), pltpu.SMEM(nest_cell.shape, jnp.int32)]
+            + [pltpu.SemaphoreType.DMA((2,))]
+            + forward_rooms(half_rows),
             flops=2_000_000_000,
             moved=1000,
-        )(owners, nest_cell, *operands)
+        )(*in_hbm(owners, nest_cell), *operands, flat_up, flat_down)
         ys = [lax.ppermute(pay, "tx", pairs)]
     else:
         pay = shape((STRIP_ROWS, breadth + 16, channels), BF16)
@@ -779,29 +846,7 @@
         )(owners, nest_cell, *operands, stash, grad_own)
         ys = [lax.ppermute(pays[0], "tx", pairs), lax.ppermute(pays[1], "tx", others) if others else pays[1]]
 
-    wide = 2 * PAD + 16
-    rows_flat = 9 * depth
-
-    def tap_rooms(count):
-        room = pltpu.VMEM((count + 1, PAD, 3 * channels), BF16)
-        return [pltpu.VMEM((2 * count + 2, wide, channels), F32), room, room]
-
-    fine = pltpu.VMEM((height, breadth, channels), F32)
-    products = lambda count: pltpu.VMEM((count, PAD, 9 * channels), F32)
-    forward_rooms = lambda count: tap_rooms(count) + [
-        products(count),
-        pltpu.VMEM((4, PAD, channels), F32),
-        fine,
-    ]
     if merged:
-        value = call(
-            inner_kernel,
-            tile,
-            [VMEM] * 3,
-            forward_rooms(half_rows),
-            flops=1_000,
-            moved=1000,
-        )(blocks, flat_up, flat_down)
         piece = rows_flat // (n_tx * n_ty)
         part = shape((2 * piece, channels), BF16)
         far, in_grad, own_sum, *sends = call(

time: 32.8 us -> 32.4 us (0.988)
    ppermute x1, waiting for transfers between devices: 2.26 us -> 1.32 us  [local(): from_far = lax.ppermute(far, 'segment', mirror)]
    ppermute x3, waiting for transfers between devices: 2.15 us -> 2.78 us  [local(): lax.ppermute(sends[d - 1], 'ty', crossed('ty', d))]
    pallas_call x3 -> x2, Pallas kernels: 2.28 us -> 2.23 us  [the longest x1 2.2 us: local(): call(condition_inner_kernel, (shape((3 * (breadth // 8 + 1), 8, channels)...]
  transfers between devices with their start and end apart: 13 -> 13, of which waited for: 4 -> 4; matrix products, arithmetic and copies ran while one was open for 0% -> 0% of each run, Pallas kernels for 26% -> 27%
where the time goes in v6:
time: 32.4 us; the launch traced here: 32.2 us
  starting transfers between devices  16.2 us (50%)
  Pallas kernels  9.72 us (30%)
  waiting for transfers between devices  5.58 us (17%)
  between operations  0.7 us (2%)
    ppermute x3, starting transfers between devices, local(): lax.ppermute(sends[d - 1], 'ty', crossed('ty', d))  4.45 us
    ppermute x1, starting transfers between devices, local(): st_far = lax.ppermute(stashed, 'tx', crossed('tx', 1))  3.03 us
    ppermute x3, waiting for transfers between devices, local(): lax.ppermute(sends[d - 1], 'ty', crossed('ty', d))  2.78 us
    ppermute x1, starting transfers between devices, local(): z1 = lax.ppermute(z_pay1, 'ty', others)  2.47 us
    pallas_call x1, Pallas kernels, local(): call(paired_kernel, (shape((height - BORDER, breadth, channels), BF16), t...  2.31 us
    pallas_call x1, Pallas kernels, local(): call(condition_inner_kernel, (shape((3 * (breadth // 8 + 1), 8, channels)...  2.2 us
    ppermute x1, starting transfers between devices, local(): z0 = lax.ppermute(z_pay0, 'ty', pairs)  2.06 us
    pallas_call x1, Pallas kernels, local(): call(prepare_kernel, (shape((height, breadth, channels), F32), tile, flat...  1.84 us
  transfers between devices with their start and end apart: 13, of which 4 were waited for; matrix products, arithmetic and copies ran while one was open for 0% of the time, Pallas kernels for 27%

profile of v6, /device:TPU:0, one launch (start us, length us, event | category | flops | bytes accessed | tf_op | source)
XLA Modules:
  0.0 32.2 jit_solution(12080908612128249851)
XLA Ops:
  0.6 3.0 %collective-permute-start.4 = (bf16[1,16,64,128]{3,2,1,0:T(8,128)(2,1)}, bf16[1,16,64,128]{3,2,1,0:T(8,128)(2,1)S(1)}, u32[]{:S(2)}, u32[]{:S(2)}) collective-permute-start(bf16[1,16,64,128]{3,2,1,0:T(8,128)(2,1)} %st.3), channel_id=1, source_target_pairs={{0,4},{4,0},{1,5},{5,1},{2,6},{6,2},{3,7},{7,3},{8,12},{12,8},{9,1... | collective-permute-start | bytes 786440 | tf_op jit(solution)/shard_map/ppermute | solution.py:759
  3.7 0.0 copy-start
  3.7 1.4 %shard_map.138 = (bf16[16,64,128]{2,1,0:T(8,128)(2,1)S(1)}, bf16[25,8,128]{2,1,0:T(8,128)(2,1)S(1)}, bf16[25,8,128]{2,1,0:T(8,128)(2,1)S(1)}) custom-call(s32[64]{0:T(128)} %bitcast.9, s32[64]{0:T(128)} %cell_in.3, s32[4,16]{1,0:T(4,128)} %land_in.1, bf16[1,16,64,128]{3,2,1,0:T(8,128)(2,1)} %act.3, bf16[1,16,64,128]{3,2,1,0:T(8,128)(2,1)} %par.3, ...), custom_call_target="tpu_custom_call" | custom-call | flops 1000 | bytes 1000 | tf_op jit(solution)/shard_map/pallas_call | solution.py:762
  5.0 0.1 collective-permute-start.5
  5.1 2.1 %collective-permute-start = (bf16[25,8,128]{2,1,0:T(8,128)(2,1)S(1)}, bf16[25,8,128]{2,1,0:T(8,128)(2,1)S(1)}, u32[]{:S(2)}, u32[]{:S(2)}) collective-permute-start(bf16[25,8,128]{2,1,0:T(8,128)(2,1)S(1)} %get-tuple-element.33), channel_id=1, source_target_pairs={{0,1},{2,3},{1,0},{3,2},{4,5},{6,7},{5,4},{7,6},{8,9},{10,11},{9,8... | collective-permute-start | bytes 153608 | tf_op jit(solution)/shard_map/ppermute | solution.py:778
  7.2 2.5 %collective-permute-start.1 = (bf16[25,8,128]{2,1,0:T(8,128)(2,1)S(1)}, bf16[25,8,128]{2,1,0:T(8,128)(2,1)S(1)}, u32[]{:S(2)}, u32[]{:S(2)}) collective-permute-start(bf16[25,8,128]{2,1,0:T(8,128)(2,1)S(1)} %get-tuple-element.34), channel_id=1, source_target_pairs={{0,3},{1,2},{2,1},{3,0},{4,7},{5,6},{6,5},{7,4},{8,11},{9,10},{10,... | collective-permute-start | bytes 153608 | tf_op jit(solution)/shard_map/ppermute | solution.py:779
  9.7 0.0 copy-done
  9.7 0.1 collective-permute-start.2
  9.8 1.8 %shard_map.137 = (f32[16,64,128]{2,1,0:T(8,128)S(1)}, bf16[16,64,128]{2,1,0:T(8,128)(2,1)S(1)}, bf16[192,1152]{1,0:T(8,128)(2,1)S(1)}, bf16[192,1152]{1,0:T(8,128)(2,1)S(1)}) custom-call(bf16[1,16,64,128]{3,2,1,0:T(8,128)(2,1)} %act.3, bf16[1,16,64,128]{3,2,1,0:T(8,128)(2,1)} %par.3, bf16[1,16,64,128]{3,2,1,0:T(8,128)(2,1)} %st.3, ...), custom_call_target="tpu_custom_call" | custom-call | flops 1000 | bytes 1000 | tf_op jit(solution)/shard_map/pallas_call | solution.py:786
  11.6 0.0 collective-permute-done.z0
  11.6 1.5 %collective-permute-done.1.z1 = bf16[25,8,128]{2,1,0:T(8,128)(2,1)S(1)} collective-permute-done((bf16[25,8,128]{2,1,0:T(8,128)(2,1)S(1)}, bf16[25,8,128]{2,1,0:T(8,128)(2,1)S(1)}, u32[]{:S(2)}, u32[]{:S(2)}) %collective-permute-start.1) | collective-permute-done | bytes 51232 | tf_op jit(solution)/shard_map/ppermute | solution.py:779
  13.1 0.0 collective-permute-done.4._stash.st_far
  13.1 1.6 %collective-permute-start.6 = (bf16[11,8,128]{2,1,0:T(8,128)(2,1)S(1)}, bf16[11,8,128]{2,1,0:T(8,128)(2,1)S(1)}, u32[]{:S(2)}, u32[]{:S(2)}) collective-permute-start(bf16[11,8,128]{2,1,0:T(8,128)(2,1)S(1)} %get-tuple-element.43), channel_id=1, source_target_pairs={{0,4},{4,0},{1,5},{5,1},{2,6},{6,2},{3,7},{7,3},{8,12},{12,8},{9,1... | collective-permute-start | bytes 67592 | tf_op jit(solution)/shard_map/ppermute | solution.py:822
  14.7 0.0 collective-permute-done.2.z2
  14.7 2.2 %shard_map.139 = (bf16[27,8,128]{2,1,0:T(8,128)(2,1)S(1)}, bf16[16,80,128]{2,1,0:T(8,128)(2,1)S(1)}, bf16[16,64,128]{2,1,0:T(8,128)(2,1)S(1)}) custom-call(s32[64]{0:T(128)} %bitcast.10, s32[64]{0:T(128)} %cell_in.3, f32[16,64,128]{2,1,0:T(8,128)S(1)} %get-tuple-element.32.base, bf16[25,8,128]{2,1,0:T(8,128)(2,1)S(1)} %collective-permute-done.z0, ...), custom_call_target="tpu_custom_call" | custom-call | flops 2000000000 | bytes 1000 | tf_op jit(solution)/shard_map/pallas_call | solution.py:823
  16.9 1.2 %collective-permute-start.3 = (bf16[27,8,128]{2,1,0:T(8,128)(2,1)S(1)}, bf16[27,8,128]{2,1,0:T(8,128)(2,1)S(1)}, u32[]{:S(2)}, u32[]{:S(2)}) collective-permute-start(bf16[27,8,128]{2,1,0:T(8,128)(2,1)S(1)} %get-tuple-element.38), channel_id=1, source_target_pairs={{0,4},{4,0},{1,5},{5,1},{2,6},{6,2},{3,7},{7,3},{8,12},{12,8},{9,1... | collective-permute-start | bytes 165896 | tf_op jit(solution)/shard_map/ppermute | solution.py:838
  18.1 0.0 collective-permute-done.5.grad_far
  18.1 0.0 collective-permute-done.6.rim_far
  18.1 2.3 %shard_map.142 = (bf16[13,64,128]{2,1,0:T(8,128)(2,1)S(1)}, bf16[16,64,128]{2,1,0:T(8,128)(2,1)S(1)}, f32[432,128]{1,0:T(8,128)S(1)}, bf16[432,128]{1,0:T(8,128)...) custom-call(bf16[16,64,128]{2,1,0:T(8,128)(2,1)S(1)} %get-tuple-element.40.st, ...), custom_call_target="tpu_custom_call" | custom-call | flops 5000000000 | bytes 4000000 | tf_op jit(solution)/shard_map/pallas_call | solution.py:852
  20.4 1.0 %collective-permute-start.9 = (bf16[432,128]{1,0:T(8,128)(2,1)S(1)}, bf16[432,128]{1,0:T(8,128)(2,1)S(1)}, u32[]{:S(2)}, u32[]{:S(2)}) collective-permute-start(bf16[432,128]{1,0:T(8,128)(2,1)S(1)} %get-tuple-element.47), channel_id=1, source_target_pairs={{0,2},{1,3},{2,0},{3,1},{4,6},{5,7},{6,4},{7,5},{8,10},{9,11},{10,... | collective-permute-start | bytes 331784 | tf_op jit(solution)/shard_map/ppermute | solution.py:909
  21.5 0.0 collective-permute-start.8
  21.5 0.0 collective-permute-done.3.refs_0_
  21.5 1.8 %collective-permute-start.11 = (bf16[432,128]{1,0:T(8,128)(2,1)S(1)}, bf16[432,128]{1,0:T(8,128)(2,1)S(1)}, u32[]{:S(2)}, u32[]{:S(2)}) collective-permute-start(bf16[432,128]{1,0:T(8,128)(2,1)S(1)} %get-tuple-element.50), channel_id=1, source_target_pairs={{0,1},{1,0},{2,3},{3,2},{4,5},{5,4},{6,7},{7,6},{8,9},{9,8},{10,11... | collective-permute-start | bytes 331784 | tf_op jit(solution)/shard_map/ppermute | solution.py:909
  23.3 1.6 %collective-permute-start.12 = (bf16[432,128]{1,0:T(8,128)(2,1)S(1)}, bf16[432,128]{1,0:T(8,128)(2,1)S(1)}, u32[]{:S(2)}, u32[]{:S(2)}) collective-permute-start(bf16[432,128]{1,0:T(8,128)(2,1)S(1)} %get-tuple-element.51), channel_id=1, source_target_pairs={{0,3},{1,2},{2,1},{3,0},{4,7},{5,6},{6,5},{7,4},{8,11},{9,10},{10,... | collective-permute-start | bytes 331784 | tf_op jit(solution)/shard_map/ppermute | solution.py:909
  24.9 0.8 %shard_map.143 = (bf16[16,64,128]{2,1,0:T(8,128)(2,1)S(1)}, bf16[3,64,128]{2,1,0:T(8,128)(2,1)S(1)}) custom-call(bf16[16,80,128]{2,1,0:T(8,128)(2,1)S(1)} %get-tuple-element.37.blocks, bf16[27,8,128]{2,1,0:T(8,128)(2,1)S(1)} %shard_map.140.y0, bf16[16,64,128]{2,1,0:T(8,128)(2,1)S(1)} %get-tuple-element.39.value, ...), custom_call_target="tpu_custom_call" | custom-call | flops 600000000 | bytes 4000000 | tf_op jit(solution)/shard_map/pallas_call | solution.py:898
  25.7 1.2 %collective-permute-start.10 = (bf16[3,64,128]{2,1,0:T(8,128)(2,1)S(1)}, bf16[3,64,128]{2,1,0:T(8,128)(2,1)S(1)}, u32[]{:S(2)}, u32[]{:S(2)}) collective-permute-start(bf16[3,64,128]{2,1,0:T(8,128)(2,1)S(1)} %get-tuple-element.48), channel_id=1, source_target_pairs={{0,24},{8,16},{16,8},{24,0},{1,25},{9,17},{17,9},{25,1},{2,26},{10... | collective-permute-start | bytes 147464 | tf_op jit(solution)/shard_map/ppermute | solution.py:907
  27.0 0.7 %collective-permute-done.9.refs_0_ = bf16[432,128]{1,0:T(8,128)(2,1)S(1)} collective-permute-done((bf16[432,128]{1,0:T(8,128)(2,1)S(1)}, bf16[432,128]{1,0:T(8,128)(2,1)S(1)}, u32[]{:S(2)}, u32[]{:S(2)}) %collective-permute-start.9) | collective-permute-done | bytes 110624 | tf_op jit(solution)/shard_map/ppermute | solution.py:909
  27.7 0.0 collective-permute-start.7
  27.7 1.3 %collective-permute-done.8.refs_0_ = bf16[13,64,128]{2,1,0:T(8,128)(2,1)S(1)} collective-permute-done((bf16[13,64,128]{2,1,0:T(8,128)(2,1)S(1)}, bf16[13,64,128]{2,1,0:T(8,128)(2,1)S(1)}, u32[]{:S(2)}, u32[]{:S(2)}) %collective-permute-start.8) | collective-permute-done | bytes 213024 | tf_op jit(solution)/shard_map/ppermute | solution.py:906
  29.0 0.0 collective-permute-done.11.refs_0_
  29.0 2.1 %collective-permute-done.12.refs_1_ = bf16[432,128]{1,0:T(8,128)(2,1)S(1)} collective-permute-done((bf16[432,128]{1,0:T(8,128)(2,1)S(1)}, bf16[432,128]{1,0:T(8,128)(2,1)S(1)}, u32[]{:S(2)}, u32[]{:S(2)}) %collective-permute-start.12) | collective-permute-done | bytes 110624 | tf_op jit(solution)/shard_map/ppermute | solution.py:909
  31.1 0.0 collective-permute-done.10.strip
  31.1 0.0 collective-permute-done.7.near
  31.1 1.2 %shard_map.147 = (bf16[1,16,64,128]{3,2,1,0:T(8,128)(2,1)}, bf16[1,16,64,128]{3,2,1,0:T(8,128)(2,1)}, bf16[1,16,64,128]{3,2,1,0:T(8,128)(2,1)}, f32[216,128]{1,0:T(8,128)}, f32[216,128]{1,0:T(8,128)}) custom-call(bf16[16,64,128]{2,1,0:T(8,128)(2,1)S(1)} %collective-permute-done.7.near, bf16[13,64,128]{2,1,0:T(8,128)(2,1)S(1)} %shard_map.145.refs_2_.far, ...), custom_call_target="tpu_custom_call" | custom-call | flops 1000 | bytes 1000 | tf_op jit(solution)/shard_map/pallas_call | solution.py:914
  (5 shorter events, 0.0 us)
Async XLA Ops:
  0.6 12.5 %collective-permute-start.4 = (bf16[1,16,64,128]{3,2,1,0:T(8,128)(2,1)}, bf16[1,16,64,128]{3,2,1,0:T(8,128)(2,1)S(1)}, u32[]{:S(2)}, u32[]{:S(2)}) collective-permute-start(bf16[1,16,64,128]{3,2,1,0:T(8,128)(2,1)} %st.3), channel_id=1, source_target_pairs={{0,4},{4,0},{1,5},{5,1},{2,6},{6,2},{3,7},{7,3},{8,12},{12,8},{9,1... | collective-permute-start | bytes 786440 | tf_op jit(solution)/shard_map/ppermute | solution.py:759
  3.7 6.0 %copy-start = (bf16[64,128]{1,0:T(8,128)(2,1)S(1)}, bf16[64,128]{1,0:T(8,128)(2,1)}, u32[]{:S(2)}) copy-start(bf16[64,128]{1,0:T(8,128)(2,1)} %coarse.3) | copy-start | bytes 49156
  5.0 13.1 %collective-permute-start.5 = (bf16[16,64,128]{2,1,0:T(8,128)(2,1)S(1)}, bf16[16,64,128]{2,1,0:T(8,128)(2,1)S(1)}, u32[]{:S(2)}, u32[]{:S(2)}) collective-permute-start(bf16[16,64,128]{2,1,0:T(8,128)(2,1)S(1)} %get-tuple-element.41.grad), channel_id=1, source_target_pairs={{0,4},{4,0},{1,5},{5,1},{2,6},{6,2},{3,7},{7,3},{8,12},{12,8},{9,1... | collective-permute-start | bytes 786440 | tf_op jit(solution)/shard_map/ppermute | solution.py:777
  5.1 6.5 %collective-permute-start = (bf16[25,8,128]{2,1,0:T(8,128)(2,1)S(1)}, bf16[25,8,128]{2,1,0:T(8,128)(2,1)S(1)}, u32[]{:S(2)}, u32[]{:S(2)}) collective-permute-start(bf16[25,8,128]{2,1,0:T(8,128)(2,1)S(1)} %get-tuple-element.33), channel_id=1, source_target_pairs={{0,1},{2,3},{1,0},{3,2},{4,5},{6,7},{5,4},{7,6},{8,9},{10,11},{9,8... | collective-permute-start | bytes 153608 | tf_op jit(solution)/shard_map/ppermute | solution.py:778
  7.2 5.9 %collective-permute-start.1 = (bf16[25,8,128]{2,1,0:T(8,128)(2,1)S(1)}, bf16[25,8,128]{2,1,0:T(8,128)(2,1)S(1)}, u32[]{:S(2)}, u32[]{:S(2)}) collective-permute-start(bf16[25,8,128]{2,1,0:T(8,128)(2,1)S(1)} %get-tuple-element.34), channel_id=1, source_target_pairs={{0,3},{1,2},{2,1},{3,0},{4,7},{5,6},{6,5},{7,4},{8,11},{9,10},{10,... | collective-permute-start | bytes 153608 | tf_op jit(solution)/shard_map/ppermute | solution.py:779
  9.7 5.1 %collective-permute-start.2 = (bf16[64,128]{1,0:T(8,128)(2,1)S(1)}, bf16[64,128]{1,0:T(8,128)(2,1)S(1)}, u32[]{:S(2)}, u32[]{:S(2)}) collective-permute-start(bf16[64,128]{1,0:T(8,128)(2,1)S(1)} %copy-done), channel_id=1, source_target_pairs={{0,2},{1,3},{2,0},{3,1},{4,6},{5,7},{6,4},{7,5},{8,10},{9,11},{10,... | collective-permute-start | bytes 49160 | tf_op jit(solution)/shard_map/ppermute | solution.py:781
  13.1 5.0 %collective-permute-start.6 = (bf16[11,8,128]{2,1,0:T(8,128)(2,1)S(1)}, bf16[11,8,128]{2,1,0:T(8,128)(2,1)S(1)}, u32[]{:S(2)}, u32[]{:S(2)}) collective-permute-start(bf16[11,8,128]{2,1,0:T(8,128)(2,1)S(1)} %get-tuple-element.43), channel_id=1, source_target_pairs={{0,4},{4,0},{1,5},{5,1},{2,6},{6,2},{3,7},{7,3},{8,12},{12,8},{9,1... | collective-permute-start | bytes 67592 | tf_op jit(solution)/shard_map/ppermute | solution.py:822
  16.9 4.5 %collective-permute-start.3 = (bf16[27,8,128]{2,1,0:T(8,128)(2,1)S(1)}, bf16[27,8,128]{2,1,0:T(8,128)(2,1)S(1)}, u32[]{:S(2)}, u32[]{:S(2)}) collective-permute-start(bf16[27,8,128]{2,1,0:T(8,128)(2,1)S(1)} %get-tuple-element.38), channel_id=1, source_target_pairs={{0,4},{4,0},{1,5},{5,1},{2,6},{6,2},{3,7},{7,3},{8,12},{12,8},{9,1... | collective-permute-start | bytes 165896 | tf_op jit(solution)/shard_map/ppermute | solution.py:838
  20.4 7.2 %collective-permute-start.9 = (bf16[432,128]{1,0:T(8,128)(2,1)S(1)}, bf16[432,128]{1,0:T(8,128)(2,1)S(1)}, u32[]{:S(2)}, u32[]{:S(2)}) collective-permute-start(bf16[432,128]{1,0:T(8,128)(2,1)S(1)} %get-tuple-element.47), channel_id=1, source_target_pairs={{0,2},{1,3},{2,0},{3,1},{4,6},{5,7},{6,4},{7,5},{8,10},{9,11},{10,... | collective-permute-start | bytes 331784 | tf_op jit(solution)/shard_map/ppermute | solution.py:909
  21.5 7.5 %collective-permute-start.8 = (bf16[13,64,128]{2,1,0:T(8,128)(2,1)S(1)}, bf16[13,64,128]{2,1,0:T(8,128)(2,1)S(1)}, u32[]{:S(2)}, u32[]{:S(2)}) collective-permute-start(bf16[13,64,128]{2,1,0:T(8,128)(2,1)S(1)} %get-tuple-element.46), channel_id=1, source_target_pairs={{0,24},{8,16},{16,8},{24,0},{1,25},{9,17},{17,9},{25,1},{2,26},{10... | collective-permute-start | bytes 638984 | tf_op jit(solution)/shard_map/ppermute | solution.py:906
  21.5 7.5 %collective-permute-start.11 = (bf16[432,128]{1,0:T(8,128)(2,1)S(1)}, bf16[432,128]{1,0:T(8,128)(2,1)S(1)}, u32[]{:S(2)}, u32[]{:S(2)}) collective-permute-start(bf16[432,128]{1,0:T(8,128)(2,1)S(1)} %get-tuple-element.50), channel_id=1, source_target_pairs={{0,1},{1,0},{2,3},{3,2},{4,5},{5,4},{6,7},{7,6},{8,9},{9,8},{10,11... | collective-permute-start | bytes 331784 | tf_op jit(solution)/shard_map/ppermute | solution.py:909
  23.3 7.8 %collective-permute-start.12 = (bf16[432,128]{1,0:T(8,128)(2,1)S(1)}, bf16[432,128]{1,0:T(8,128)(2,1)S(1)}, u32[]{:S(2)}, u32[]{:S(2)}) collective-permute-start(bf16[432,128]{1,0:T(8,128)(2,1)S(1)} %get-tuple-element.51), channel_id=1, source_target_pairs={{0,3},{1,2},{2,1},{3,0},{4,7},{5,6},{6,5},{7,4},{8,11},{9,10},{10,... | collective-permute-start | bytes 331784 | tf_op jit(solution)/shard_map/ppermute | solution.py:909
  25.7 5.4 %collective-permute-start.10 = (bf16[3,64,128]{2,1,0:T(8,128)(2,1)S(1)}, bf16[3,64,128]{2,1,0:T(8,128)(2,1)S(1)}, u32[]{:S(2)}, u32[]{:S(2)}) collective-permute-start(bf16[3,64,128]{2,1,0:T(8,128)(2,1)S(1)} %get-tuple-element.48), channel_id=1, source_target_pairs={{0,24},{8,16},{16,8},{24,0},{1,25},{9,17},{17,9},{25,1},{2,26},{10... | collective-permute-start | bytes 147464 | tf_op jit(solution)/shard_map/ppermute | solution.py:907
  27.7 3.4 %collective-permute-start.7 = (bf16[16,64,128]{2,1,0:T(8,128)(2,1)S(1)}, bf16[16,64,128]{2,1,0:T(8,128)(2,1)S(1)}, u32[]{:S(2)}, u32[]{:S(2)}) collective-permute-start(bf16[16,64,128]{2,1,0:T(8,128)(2,1)S(1)} %get-tuple-element.45), channel_id=1, source_target_pairs={{0,8},{8,0},{16,24},{24,16},{1,9},{9,1},{17,25},{25,17},{2,10},{10... | collective-permute-start | bytes 786440 | tf_op jit(solution)/shard_map/ppermute | solution.py:908

commit v7 on v6

--- a/solution.py
+++ b/solution.py
@@ -474,8 +474,6 @@
     edge = lambda field, row, k: field[first_row + row, pl.ds(LEFT - 1 + k + breadth, 8, stride=2), :]
     flat_edge = lambda ref: ref[...].reshape(edge_count * 8, 9 * 128).astype(BF16)
 
-    for each in (field, grad_field):
-        each[:, wide:] = jnp.zeros((each.shape[0], each.shape[1] - wide, 128), F32)
     fill(field, lambda row: st[row], lambda row: st_far[0, row], 1, 5)
     spread_taps(field, taps.at[:, :, 0:384], taps.at[:, :, 384:768], 2 * count + 1, LEFT - 1)
     for p in range(edge_count):

time: 32.4 us -> 32.4 us (level)
  transfers between devices with their start and end apart: 13 -> 13, of which waited for: 4 -> 4; matrix products, arithmetic and copies ran while one was open for 0% -> 0% of each run, Pallas kernels for 27% -> 26%
where the time goes in v7:
time: 32.4 us; the launch traced here: 32.2 us
  starting transfers between devices  16.2 us (50%)
  Pallas kernels  9.67 us (30%)
  waiting for transfers between devices  5.58 us (17%)
  between operations  0.7 us (2%)
    ppermute x3, starting transfers between devices, local(): lax.ppermute(sends[d - 1], 'ty', crossed('ty', d))  4.45 us
    ppermute x1, starting transfers between devices, local(): st_far = lax.ppermute(stashed, 'tx', crossed('tx', 1))  3.03 us
    ppermute x3, waiting for transfers between devices, local(): lax.ppermute(sends[d - 1], 'ty', crossed('ty', d))  2.78 us
    ppermute x1, starting transfers between devices, local(): z1 = lax.ppermute(z_pay1, 'ty', others)  2.47 us
    pallas_call x1, Pallas kernels, local(): call(paired_kernel, (shape((height - BORDER, breadth, channels), BF16), t...  2.25 us
    pallas_call x1, Pallas kernels, local(): call(condition_inner_kernel, (shape((3 * (breadth // 8 + 1), 8, channels)...  2.2 us
    ppermute x1, starting transfers between devices, local(): z0 = lax.ppermute(z_pay0, 'ty', pairs)  2.06 us
    pallas_call x1, Pallas kernels, local(): call(prepare_kernel, (shape((height, breadth, channels), F32), tile, flat...  1.84 us
  transfers between devices with their start and end apart: 13, of which 4 were waited for; matrix products, arithmetic and copies ran while one was open for 0% of the time, Pallas kernels for 26%

profile of v7, /device:TPU:0, one launch (start us, length us, event | category | flops | bytes accessed | tf_op | source)
XLA Modules:
  0.0 32.2 jit_solution(1702513829671908553)
XLA Ops:
  0.6 3.0 %collective-permute-start.4 = (bf16[1,16,64,128]{3,2,1,0:T(8,128)(2,1)}, bf16[1,16,64,128]{3,2,1,0:T(8,128)(2,1)S(1)}, u32[]{:S(2)}, u32[]{:S(2)}) collective-permute-start(bf16[1,16,64,128]{3,2,1,0:T(8,128)(2,1)} %st.3), channel_id=1, source_target_pairs={{0,4},{4,0},{1,5},{5,1},{2,6},{6,2},{3,7},{7,3},{8,12},{12,8},{9,1... | collective-permute-start | bytes 786440 | tf_op jit(solution)/shard_map/ppermute | solution.py:757
  3.7 0.0 copy-start
  3.7 1.4 %shard_map.138 = (bf16[16,64,128]{2,1,0:T(8,128)(2,1)S(1)}, bf16[25,8,128]{2,1,0:T(8,128)(2,1)S(1)}, bf16[25,8,128]{2,1,0:T(8,128)(2,1)S(1)}) custom-call(s32[64]{0:T(128)} %bitcast.9, s32[64]{0:T(128)} %cell_in.3, s32[4,16]{1,0:T(4,128)} %land_in.1, bf16[1,16,64,128]{3,2,1,0:T(8,128)(2,1)} %act.3, bf16[1,16,64,128]{3,2,1,0:T(8,128)(2,1)} %par.3, ...), custom_call_target="tpu_custom_call" | custom-call | flops 1000 | bytes 1000 | tf_op jit(solution)/shard_map/pallas_call | solution.py:760
  5.0 0.1 collective-permute-start.5
  5.1 2.1 %collective-permute-start = (bf16[25,8,128]{2,1,0:T(8,128)(2,1)S(1)}, bf16[25,8,128]{2,1,0:T(8,128)(2,1)S(1)}, u32[]{:S(2)}, u32[]{:S(2)}) collective-permute-start(bf16[25,8,128]{2,1,0:T(8,128)(2,1)S(1)} %get-tuple-element.33), channel_id=1, source_target_pairs={{0,1},{2,3},{1,0},{3,2},{4,5},{6,7},{5,4},{7,6},{8,9},{10,11},{9,8... | collective-permute-start | bytes 153608 | tf_op jit(solution)/shard_map/ppermute | solution.py:776
  7.2 2.5 %collective-permute-start.1 = (bf16[25,8,128]{2,1,0:T(8,128)(2,1)S(1)}, bf16[25,8,128]{2,1,0:T(8,128)(2,1)S(1)}, u32[]{:S(2)}, u32[]{:S(2)}) collective-permute-start(bf16[25,8,128]{2,1,0:T(8,128)(2,1)S(1)} %get-tuple-element.34), channel_id=1, source_target_pairs={{0,3},{1,2},{2,1},{3,0},{4,7},{5,6},{6,5},{7,4},{8,11},{9,10},{10,... | collective-permute-start | bytes 153608 | tf_op jit(solution)/shard_map/ppermute | solution.py:777
  9.7 0.0 copy-done
  9.7 0.1 collective-permute-start.2
  9.8 1.8 %shard_map.137 = (f32[16,64,128]{2,1,0:T(8,128)S(1)}, bf16[16,64,128]{2,1,0:T(8,128)(2,1)S(1)}, bf16[192,1152]{1,0:T(8,128)(2,1)S(1)}, bf16[192,1152]{1,0:T(8,128)(2,1)S(1)}) custom-call(bf16[1,16,64,128]{3,2,1,0:T(8,128)(2,1)} %act.3, bf16[1,16,64,128]{3,2,1,0:T(8,128)(2,1)} %par.3, bf16[1,16,64,128]{3,2,1,0:T(8,128)(2,1)} %st.3, ...), custom_call_target="tpu_custom_call" | custom-call | flops 1000 | bytes 1000 | tf_op jit(solution)/shard_map/pallas_call | solution.py:784
  11.6 0.0 collective-permute-done.z0
  11.6 1.5 %collective-permute-done.1.z1 = bf16[25,8,128]{2,1,0:T(8,128)(2,1)S(1)} collective-permute-done((bf16[25,8,128]{2,1,0:T(8,128)(2,1)S(1)}, bf16[25,8,128]{2,1,0:T(8,128)(2,1)S(1)}, u32[]{:S(2)}, u32[]{:S(2)}) %collective-permute-start.1) | collective-permute-done | bytes 51232 | tf_op jit(solution)/shard_map/ppermute | solution.py:777
  13.1 0.0 collective-permute-done.4._stash.st_far
  13.1 1.6 %collective-permute-start.6 = (bf16[11,8,128]{2,1,0:T(8,128)(2,1)S(1)}, bf16[11,8,128]{2,1,0:T(8,128)(2,1)S(1)}, u32[]{:S(2)}, u32[]{:S(2)}) collective-permute-start(bf16[11,8,128]{2,1,0:T(8,128)(2,1)S(1)} %get-tuple-element.43), channel_id=1, source_target_pairs={{0,4},{4,0},{1,5},{5,1},{2,6},{6,2},{3,7},{7,3},{8,12},{12,8},{9,1... | collective-permute-start | bytes 67592 | tf_op jit(solution)/shard_map/ppermute | solution.py:820
  14.7 0.0 collective-permute-done.2.z2
  14.7 2.2 %shard_map.139 = (bf16[27,8,128]{2,1,0:T(8,128)(2,1)S(1)}, bf16[16,80,128]{2,1,0:T(8,128)(2,1)S(1)}, bf16[16,64,128]{2,1,0:T(8,128)(2,1)S(1)}) custom-call(s32[64]{0:T(128)} %bitcast.10, s32[64]{0:T(128)} %cell_in.3, f32[16,64,128]{2,1,0:T(8,128)S(1)} %get-tuple-element.32.base, bf16[25,8,128]{2,1,0:T(8,128)(2,1)S(1)} %collective-permute-done.z0, ...), custom_call_target="tpu_custom_call" | custom-call | flops 2000000000 | bytes 1000 | tf_op jit(solution)/shard_map/pallas_call | solution.py:821
  16.9 1.2 %collective-permute-start.3 = (bf16[27,8,128]{2,1,0:T(8,128)(2,1)S(1)}, bf16[27,8,128]{2,1,0:T(8,128)(2,1)S(1)}, u32[]{:S(2)}, u32[]{:S(2)}) collective-permute-start(bf16[27,8,128]{2,1,0:T(8,128)(2,1)S(1)} %get-tuple-element.38), channel_id=1, source_target_pairs={{0,4},{4,0},{1,5},{5,1},{2,6},{6,2},{3,7},{7,3},{8,12},{12,8},{9,1... | collective-permute-start | bytes 165896 | tf_op jit(solution)/shard_map/ppermute | solution.py:836
  18.1 0.0 collective-permute-done.5.grad_far
  18.1 0.0 collective-permute-done.6.rim_far
  18.1 2.3 %shard_map.142 = (bf16[13,64,128]{2,1,0:T(8,128)(2,1)S(1)}, bf16[16,64,128]{2,1,0:T(8,128)(2,1)S(1)}, f32[432,128]{1,0:T(8,128)S(1)}, bf16[432,128]{1,0:T(8,128)...) custom-call(bf16[16,64,128]{2,1,0:T(8,128)(2,1)S(1)} %get-tuple-element.40.st, ...), custom_call_target="tpu_custom_call" | custom-call | flops 5000000000 | bytes 4000000 | tf_op jit(solution)/shard_map/pallas_call | solution.py:850
  20.4 1.0 %collective-permute-start.9 = (bf16[432,128]{1,0:T(8,128)(2,1)S(1)}, bf16[432,128]{1,0:T(8,128)(2,1)S(1)}, u32[]{:S(2)}, u32[]{:S(2)}) collective-permute-start(bf16[432,128]{1,0:T(8,128)(2,1)S(1)} %get-tuple-element.47), channel_id=1, source_target_pairs={{0,2},{1,3},{2,0},{3,1},{4,6},{5,7},{6,4},{7,5},{8,10},{9,11},{10,... | collective-permute-start | bytes 331784 | tf_op jit(solution)/shard_map/ppermute | solution.py:907
  21.4 0.0 collective-permute-start.8
  21.4 0.0 collective-permute-done.3.refs_0_
  21.4 1.8 %collective-permute-start.11 = (bf16[432,128]{1,0:T(8,128)(2,1)S(1)}, bf16[432,128]{1,0:T(8,128)(2,1)S(1)}, u32[]{:S(2)}, u32[]{:S(2)}) collective-permute-start(bf16[432,128]{1,0:T(8,128)(2,1)S(1)} %get-tuple-element.50), channel_id=1, source_target_pairs={{0,1},{1,0},{2,3},{3,2},{4,5},{5,4},{6,7},{7,6},{8,9},{9,8},{10,11... | collective-permute-start | bytes 331784 | tf_op jit(solution)/shard_map/ppermute | solution.py:907
  23.2 1.6 %collective-permute-start.12 = (bf16[432,128]{1,0:T(8,128)(2,1)S(1)}, bf16[432,128]{1,0:T(8,128)(2,1)S(1)}, u32[]{:S(2)}, u32[]{:S(2)}) collective-permute-start(bf16[432,128]{1,0:T(8,128)(2,1)S(1)} %get-tuple-element.51), channel_id=1, source_target_pairs={{0,3},{1,2},{2,1},{3,0},{4,7},{5,6},{6,5},{7,4},{8,11},{9,10},{10,... | collective-permute-start | bytes 331784 | tf_op jit(solution)/shard_map/ppermute | solution.py:907
  24.8 0.8 %shard_map.143 = (bf16[16,64,128]{2,1,0:T(8,128)(2,1)S(1)}, bf16[3,64,128]{2,1,0:T(8,128)(2,1)S(1)}) custom-call(bf16[16,80,128]{2,1,0:T(8,128)(2,1)S(1)} %get-tuple-element.37.blocks, bf16[27,8,128]{2,1,0:T(8,128)(2,1)S(1)} %shard_map.140.y0, bf16[16,64,128]{2,1,0:T(8,128)(2,1)S(1)} %get-tuple-element.39.value, ...), custom_call_target="tpu_custom_call" | custom-call | flops 600000000 | bytes 4000000 | tf_op jit(solution)/shard_map/pallas_call | solution.py:896
  25.6 1.2 %collective-permute-start.10 = (bf16[3,64,128]{2,1,0:T(8,128)(2,1)S(1)}, bf16[3,64,128]{2,1,0:T(8,128)(2,1)S(1)}, u32[]{:S(2)}, u32[]{:S(2)}) collective-permute-start(bf16[3,64,128]{2,1,0:T(8,128)(2,1)S(1)} %get-tuple-element.48), channel_id=1, source_target_pairs={{0,24},{8,16},{16,8},{24,0},{1,25},{9,17},{17,9},{25,1},{2,26},{10... | collective-permute-start | bytes 147464 | tf_op jit(solution)/shard_map/ppermute | solution.py:905
  26.9 0.7 %collective-permute-done.9.refs_0_ = bf16[432,128]{1,0:T(8,128)(2,1)S(1)} collective-permute-done((bf16[432,128]{1,0:T(8,128)(2,1)S(1)}, bf16[432,128]{1,0:T(8,128)(2,1)S(1)}, u32[]{:S(2)}, u32[]{:S(2)}) %collective-permute-start.9) | collective-permute-done | bytes 110624 | tf_op jit(solution)/shard_map/ppermute | solution.py:907
  27.6 0.0 collective-permute-start.7
  27.6 1.3 %collective-permute-done.8.refs_0_ = bf16[13,64,128]{2,1,0:T(8,128)(2,1)S(1)} collective-permute-done((bf16[13,64,128]{2,1,0:T(8,128)(2,1)S(1)}, bf16[13,64,128]{2,1,0:T(8,128)(2,1)S(1)}, u32[]{:S(2)}, u32[]{:S(2)}) %collective-permute-start.8) | collective-permute-done | bytes 213024 | tf_op jit(solution)/shard_map/ppermute | solution.py:904
  28.9 0.0 collective-permute-done.11.refs_0_
  28.9 2.1 %collective-permute-done.12.refs_1_ = bf16[432,128]{1,0:T(8,128)(2,1)S(1)} collective-permute-done((bf16[432,128]{1,0:T(8,128)(2,1)S(1)}, bf16[432,128]{1,0:T(8,128)(2,1)S(1)}, u32[]{:S(2)}, u32[]{:S(2)}) %collective-permute-start.12) | collective-permute-done | bytes 110624 | tf_op jit(solution)/shard_map/ppermute | solution.py:907
  31.0 0.0 collective-permute-done.10.strip
  31.0 0.0 collective-permute-done.7.near
  31.0 1.2 %shard_map.147 = (bf16[1,16,64,128]{3,2,1,0:T(8,128)(2,1)}, bf16[1,16,64,128]{3,2,1,0:T(8,128)(2,1)}, bf16[1,16,64,128]{3,2,1,0:T(8,128)(2,1)}, f32[216,128]{1,0:T(8,128)}, f32[216,128]{1,0:T(8,128)}) custom-call(bf16[16,64,128]{2,1,0:T(8,128)(2,1)S(1)} %collective-permute-done.7.near, bf16[13,64,128]{2,1,0:T(8,128)(2,1)S(1)} %shard_map.145.refs_2_.far, ...), custom_call_target="tpu_custom_call" | custom-call | flops 1000 | bytes 1000 | tf_op jit(solution)/shard_map/pallas_call | solution.py:912
  (5 shorter events, 0.0 us)
Async XLA Ops:
  0.6 12.5 %collective-permute-start.4 = (bf16[1,16,64,128]{3,2,1,0:T(8,128)(2,1)}, bf16[1,16,64,128]{3,2,1,0:T(8,128)(2,1)S(1)}, u32[]{:S(2)}, u32[]{:S(2)}) collective-permute-start(bf16[1,16,64,128]{3,2,1,0:T(8,128)(2,1)} %st.3), channel_id=1, source_target_pairs={{0,4},{4,0},{1,5},{5,1},{2,6},{6,2},{3,7},{7,3},{8,12},{12,8},{9,1... | collective-permute-start | bytes 786440 | tf_op jit(solution)/shard_map/ppermute | solution.py:757
  3.7 6.0 %copy-start = (bf16[64,128]{1,0:T(8,128)(2,1)S(1)}, bf16[64,128]{1,0:T(8,128)(2,1)}, u32[]{:S(2)}) copy-start(bf16[64,128]{1,0:T(8,128)(2,1)} %coarse.3) | copy-start | bytes 49156
  5.0 13.1 %collective-permute-start.5 = (bf16[16,64,128]{2,1,0:T(8,128)(2,1)S(1)}, bf16[16,64,128]{2,1,0:T(8,128)(2,1)S(1)}, u32[]{:S(2)}, u32[]{:S(2)}) collective-permute-start(bf16[16,64,128]{2,1,0:T(8,128)(2,1)S(1)} %get-tuple-element.41.grad), channel_id=1, source_target_pairs={{0,4},{4,0},{1,5},{5,1},{2,6},{6,2},{3,7},{7,3},{8,12},{12,8},{9,1... | collective-permute-start | bytes 786440 | tf_op jit(solution)/shard_map/ppermute | solution.py:775
  5.1 6.5 %collective-permute-start = (bf16[25,8,128]{2,1,0:T(8,128)(2,1)S(1)}, bf16[25,8,128]{2,1,0:T(8,128)(2,1)S(1)}, u32[]{:S(2)}, u32[]{:S(2)}) collective-permute-start(bf16[25,8,128]{2,1,0:T(8,128)(2,1)S(1)} %get-tuple-element.33), channel_id=1, source_target_pairs={{0,1},{2,3},{1,0},{3,2},{4,5},{6,7},{5,4},{7,6},{8,9},{10,11},{9,8... | collective-permute-start | bytes 153608 | tf_op jit(solution)/shard_map/ppermute | solution.py:776
  7.2 5.9 %collective-permute-start.1 = (bf16[25,8,128]{2,1,0:T(8,128)(2,1)S(1)}, bf16[25,8,128]{2,1,0:T(8,128)(2,1)S(1)}, u32[]{:S(2)}, u32[]{:S(2)}) collective-permute-start(bf16[25,8,128]{2,1,0:T(8,128)(2,1)S(1)} %get-tuple-element.34), channel_id=1, source_target_pairs={{0,3},{1,2},{2,1},{3,0},{4,7},{5,6},{6,5},{7,4},{8,11},{9,10},{10,... | collective-permute-start | bytes 153608 | tf_op jit(solution)/shard_map/ppermute | solution.py:777
  9.7 5.1 %collective-permute-start.2 = (bf16[64,128]{1,0:T(8,128)(2,1)S(1)}, bf16[64,128]{1,0:T(8,128)(2,1)S(1)}, u32[]{:S(2)}, u32[]{:S(2)}) collective-permute-start(bf16[64,128]{1,0:T(8,128)(2,1)S(1)} %copy-done), channel_id=1, source_target_pairs={{0,2},{1,3},{2,0},{3,1},{4,6},{5,7},{6,4},{7,5},{8,10},{9,11},{10,... | collective-permute-start | bytes 49160 | tf_op jit(solution)/shard_map/ppermute | solution.py:779
  13.1 5.0 %collective-permute-start.6 = (bf16[11,8,128]{2,1,0:T(8,128)(2,1)S(1)}, bf16[11,8,128]{2,1,0:T(8,128)(2,1)S(1)}, u32[]{:S(2)}, u32[]{:S(2)}) collective-permute-start(bf16[11,8,128]{2,1,0:T(8,128)(2,1)S(1)} %get-tuple-element.43), channel_id=1, source_target_pairs={{0,4},{4,0},{1,5},{5,1},{2,6},{6,2},{3,7},{7,3},{8,12},{12,8},{9,1... | collective-permute-start | bytes 67592 | tf_op jit(solution)/shard_map/ppermute | solution.py:820
  16.9 4.5 %collective-permute-start.3 = (bf16[27,8,128]{2,1,0:T(8,128)(2,1)S(1)}, bf16[27,8,128]{2,1,0:T(8,128)(2,1)S(1)}, u32[]{:S(2)}, u32[]{:S(2)}) collective-permute-start(bf16[27,8,128]{2,1,0:T(8,128)(2,1)S(1)} %get-tuple-element.38), channel_id=1, source_target_pairs={{0,4},{4,0},{1,5},{5,1},{2,6},{6,2},{3,7},{7,3},{8,12},{12,8},{9,1... | collective-permute-start | bytes 165896 | tf_op jit(solution)/shard_map/ppermute | solution.py:836
  20.4 7.2 %collective-permute-start.9 = (bf16[432,128]{1,0:T(8,128)(2,1)S(1)}, bf16[432,128]{1,0:T(8,128)(2,1)S(1)}, u32[]{:S(2)}, u32[]{:S(2)}) collective-permute-start(bf16[432,128]{1,0:T(8,128)(2,1)S(1)} %get-tuple-element.47), channel_id=1, source_target_pairs={{0,2},{1,3},{2,0},{3,1},{4,6},{5,7},{6,4},{7,5},{8,10},{9,11},{10,... | collective-permute-start | bytes 331784 | tf_op jit(solution)/shard_map/ppermute | solution.py:907
  21.4 7.5 %collective-permute-start.8 = (bf16[13,64,128]{2,1,0:T(8,128)(2,1)S(1)}, bf16[13,64,128]{2,1,0:T(8,128)(2,1)S(1)}, u32[]{:S(2)}, u32[]{:S(2)}) collective-permute-start(bf16[13,64,128]{2,1,0:T(8,128)(2,1)S(1)} %get-tuple-element.46), channel_id=1, source_target_pairs={{0,24},{8,16},{16,8},{24,0},{1,25},{9,17},{17,9},{25,1},{2,26},{10... | collective-permute-start | bytes 638984 | tf_op jit(solution)/shard_map/ppermute | solution.py:904
  21.4 7.5 %collective-permute-start.11 = (bf16[432,128]{1,0:T(8,128)(2,1)S(1)}, bf16[432,128]{1,0:T(8,128)(2,1)S(1)}, u32[]{:S(2)}, u32[]{:S(2)}) collective-permute-start(bf16[432,128]{1,0:T(8,128)(2,1)S(1)} %get-tuple-element.50), channel_id=1, source_target_pairs={{0,1},{1,0},{2,3},{3,2},{4,5},{5,4},{6,7},{7,6},{8,9},{9,8},{10,11... | collective-permute-start | bytes 331784 | tf_op jit(solution)/shard_map/ppermute | solution.py:907
  23.2 7.8 %collective-permute-start.12 = (bf16[432,128]{1,0:T(8,128)(2,1)S(1)}, bf16[432,128]{1,0:T(8,128)(2,1)S(1)}, u32[]{:S(2)}, u32[]{:S(2)}) collective-permute-start(bf16[432,128]{1,0:T(8,128)(2,1)S(1)} %get-tuple-element.51), channel_id=1, source_target_pairs={{0,3},{1,2},{2,1},{3,0},{4,7},{5,6},{6,5},{7,4},{8,11},{9,10},{10,... | collective-permute-start | bytes 331784 | tf_op jit(solution)/shard_map/ppermute | solution.py:907
  25.6 5.4 %collective-permute-start.10 = (bf16[3,64,128]{2,1,0:T(8,128)(2,1)S(1)}, bf16[3,64,128]{2,1,0:T(8,128)(2,1)S(1)}, u32[]{:S(2)}, u32[]{:S(2)}) collective-permute-start(bf16[3,64,128]{2,1,0:T(8,128)(2,1)S(1)} %get-tuple-element.48), channel_id=1, source_target_pairs={{0,24},{8,16},{16,8},{24,0},{1,25},{9,17},{17,9},{25,1},{2,26},{10... | collective-permute-start | bytes 147464 | tf_op jit(solution)/shard_map/ppermute | solution.py:905
  27.6 3.4 %collective-permute-start.7 = (bf16[16,64,128]{2,1,0:T(8,128)(2,1)S(1)}, bf16[16,64,128]{2,1,0:T(8,128)(2,1)S(1)}, u32[]{:S(2)}, u32[]{:S(2)}) collective-permute-start(bf16[16,64,128]{2,1,0:T(8,128)(2,1)S(1)} %get-tuple-element.45), channel_id=1, source_target_pairs={{0,8},{8,0},{16,24},{24,16},{1,9},{9,1},{17,25},{25,17},{2,10},{10... | collective-permute-start | bytes 786440 | tf_op jit(solution)/shard_map/ppermute | solution.py:906
